TPU v7x, 32 devices: a whole 2x2x4 slice. The times are simulated.
32 devices in a mesh: dp: 8 (over z, x), tensor: 4 (over y, core).
Axes of the slice: x: 2, y: 2, z: 4, core: 2. Of those that a mesh axis runs over, the one named last changes fastest.
Arguments:
- tokens: bfloat16 [448, 257, 384], P(('dp', 'tensor')), may hold values from -6 to 6
- image_mask: int32 [448], P(('dp', 'tensor')), may hold values 0 or 1
- patch_mask: int32 [448, 256], P(('dp', 'tensor')), may hold values 0 or 1
- first_gain: bfloat16 [384], replicated, may hold values from 0.5 to 1.5
- first_shift: bfloat16 [384], replicated, may hold values from -1.75 to 1.75
- attend_weight: bfloat16 [384, 1152], replicated, may hold values from -0.4375 to 0.4375
- attend_bias: bfloat16 [2, 384], replicated, may hold values from -1.75 to 1.75
- merge_weight: bfloat16 [384, 384], replicated, may hold values from -0.875 to 0.875
- merge_bias: bfloat16 [384], replicated, may hold values from -1.75 to 1.75
- second_gain: bfloat16 [384], replicated, may hold values from 0.5 to 1.5
- second_shift: bfloat16 [384], replicated, may hold values from -1.75 to 1.75
- up_weight: bfloat16 [384, 1536], P(None, 'tensor'), may hold values from -0.3125 to 0.3125
- up_bias: bfloat16 [1536], P('tensor'), may hold values from -1.75 to 1.75
- down_weight: bfloat16 [1536, 384], P('tensor'), may hold values from -0.15625 to 0.15625
- down_bias: bfloat16 [384], replicated, may hold values from -1.75 to 1.75
- cotangent: bfloat16 [448, 257, 384], P(('dp', 'tensor')), may hold values from -6 to 6
Outputs:
- output: bfloat16 [448, 257, 384], P(('dp', 'tensor'))
- input_grad: bfloat16 [448, 257, 384], P(('dp', 'tensor'))
- first_gain_grad: float32 [384], replicated
- first_shift_grad: float32 [384], replicated
- attend_weight_grad: float32 [384, 1152], replicated
- attend_bias_grad: float32 [2, 384], replicated
- merge_weight_grad: float32 [384, 384], replicated
- merge_bias_grad: float32 [384], replicated
- second_gain_grad: float32 [384], replicated
- second_shift_grad: float32 [384], replicated
- up_weight_grad: float32 [384, 1536], P(None, 'tensor')
- up_bias_grad: float32 [1536], P('tensor')
- down_weight_grad: float32 [1536, 384], P('tensor')
- down_bias_grad: float32 [384], replicated
All inputs are finite; a program needn't handle non-finite values. No bound on the sum of `image_mask` or of `patch_mask` on one device may be relied on, other than what follows from the above.
Results may differ from a plain program's by a relative error of at most 0.012.
The roundings to bfloat16 on the way count: a program that leaves them out, or rounds other values in their place, can miss the bound.
Values may be sent and summed in bfloat16 or wider, within the bound.
A program may use at most 256 MiB of HBM per device.

v0:
```python
from functools import partial

import jax
import jax.numpy as jnp
from jax import lax
from jax.sharding import PartitionSpec as P

HEADS = 6
HEAD = 64


epsilon = 1e-06
neg_large = -1e30


def layer_norm(values, norm_gain, norm_shift):
    center = values - jnp.mean(values, axis=-1, keepdims=True)
    spread = jnp.mean(center * center, axis=-1, keepdims=True)
    return center * lax.rsqrt(spread + epsilon) * norm_gain + norm_shift


def contract(form, left, right):
    return jnp.einsum(form, left, right, preferred_element_type=jnp.float32)


def pair_scores(queries, key_rows, live_keys):
    scores = contract("bqhe,bkhe->bhqk", queries, key_rows) * HEAD ** (-0.5)
    return jnp.where(live_keys[:, None, None, :], scores, neg_large)


def attend_block(block_args):
    queries, key_rows, value_rows, live_keys = block_args
    scores = pair_scores(queries, key_rows, live_keys)
    row_peak = jnp.max(scores, axis=-1, keepdims=True)
    raised = jnp.exp(scores - row_peak)
    row_total = jnp.sum(raised, axis=-1, keepdims=True)
    attn_weights = (raised / row_total).astype(jnp.bfloat16)
    mixed_heads = contract("bhqk,bkhe->bqhe", attn_weights, value_rows)
    return (mixed_heads, row_peak[..., 0] + jnp.log(row_total[..., 0]))


def attend_back(block_args):
    queries, key_rows, value_rows, live_keys, grad_mixed, log_total = block_args
    scores = pair_scores(queries, key_rows, live_keys)
    attn_weights = jnp.exp(scores - log_total[..., None])
    value_grad = contract("bhqk,bqhe->bkhe", attn_weights.astype(jnp.bfloat16), grad_mixed)
    prob_grad = contract("bqhe,bkhe->bhqk", grad_mixed, value_rows)
    row_dot = jnp.sum(attn_weights * prob_grad, axis=-1, keepdims=True)
    score_grad = (attn_weights * (prob_grad - row_dot)).astype(jnp.bfloat16)
    query_grad = contract("bhqk,bkhe->bqhe", score_grad, key_rows) * HEAD ** (-0.5)
    key_grad = contract("bhqk,bqhe->bkhe", score_grad, queries) * HEAD ** (-0.5)
    return (
        query_grad.astype(jnp.bfloat16),
        key_grad.astype(jnp.bfloat16),
        value_grad.astype(jnp.bfloat16),
    )


def shards(
    tokens,
    image_mask,
    patch_mask,
    first_gain,
    first_shift,
    attend_weight,
    attend_bias,
    merge_weight,
    merge_bias,
    second_gain,
    second_shift,
    up_weight,
    up_bias,
    down_weight,
    down_bias,
    cotangent,
):
    images, seq_len, features = tokens.shape
    pairs = images // 2
    live_rows = image_mask.astype(jnp.float32)[:, None, None]
    live_keys = jnp.concatenate([jnp.ones((images, 1), jnp.bool_), patch_mask == 1], axis=1)
    live_pairs = live_keys.reshape(pairs, 2, seq_len)
    inputs = tokens.astype(jnp.float32)
    gain_one = first_gain.astype(jnp.float32)
    shift_one = first_shift.astype(jnp.float32)
    gain_two = second_gain.astype(jnp.float32)
    shift_two = second_shift.astype(jnp.float32)
    normed_one, first_back = jax.vjp(layer_norm, inputs, gain_one, shift_one)
    first_in = normed_one.astype(jnp.bfloat16)
    bias_full = jnp.concatenate(
        [
            attend_bias[0].astype(jnp.float32),
            jnp.zeros((features,), jnp.float32),
            attend_bias[1].astype(jnp.float32),
        ]
    )
    packed = (contract("isd,de->ise", first_in, attend_weight) + bias_full).astype(jnp.bfloat16)
    head_shape = (pairs, 2, seq_len, HEADS, HEAD)
    queries = packed[..., :features].reshape(head_shape)
    key_rows = packed[..., features : 2 * features].reshape(head_shape)
    value_rows = packed[..., 2 * features :].reshape(head_shape)
    mixed_heads, log_total = lax.map(attend_block, (queries, key_rows, value_rows, live_pairs))
    attended = mixed_heads.reshape(images, seq_len, features).astype(jnp.bfloat16)
    branch = contract("isd,de->ise", attended, merge_weight) + merge_bias.astype(jnp.float32)
    hidden = inputs + live_rows * branch
    normed_two, second_back = jax.vjp(layer_norm, hidden, gain_two, shift_two)
    second_in = normed_two.astype(jnp.bfloat16)
    gelu_exact = partial(jax.nn.gelu, approximate=False)
    up_all, down_all, up_bias_all = (
        lax.all_gather(up_weight, "tensor", axis=1, tiled=True),
        lax.all_gather(down_weight, "tensor", axis=0, tiled=True),
        lax.all_gather(up_bias, "tensor", axis=0, tiled=True),
    )
    pre_act = contract("isd,df->isf", second_in, up_all) + up_bias_all.astype(jnp.float32)
    act_full, gelu_back = jax.vjp(gelu_exact, pre_act)
    activated = act_full.astype(jnp.bfloat16)
    reduced = contract("isf,fd->isd", activated, down_all)
    output = (hidden + live_rows * (reduced + down_bias.astype(jnp.float32))).astype(jnp.bfloat16)
    grad_out = cotangent.astype(jnp.float32)
    grad_branch = (live_rows * grad_out).astype(jnp.bfloat16)
    down_bias_grad = jnp.sum(grad_branch.astype(jnp.float32), axis=(0, 1))
    down_grad_all = contract("isf,isd->fd", activated, grad_branch)
    grad_act = contract("isd,fd->isf", grad_branch, down_all)
    grad_pre = gelu_back(grad_act)[0].astype(jnp.bfloat16)
    up_grad_all = contract("isd,isf->df", second_in, grad_pre)
    up_bias_all_grad = jnp.sum(grad_pre.astype(jnp.float32), axis=(0, 1))
    grad_second = contract("isf,df->isd", grad_pre, up_all)
    grad_hidden_norm, gain_two_grad, shift_two_grad = second_back(grad_second)
    grad_hidden = grad_out + grad_hidden_norm
    grad_attn = (live_rows * grad_hidden).astype(jnp.bfloat16)
    merge_grad = contract("isd,ise->de", attended, grad_attn)
    merge_bias_grad = jnp.sum(grad_attn.astype(jnp.float32), axis=(0, 1))
    grad_mixed = (
        contract("ise,de->isd", grad_attn, merge_weight).astype(jnp.bfloat16).reshape(head_shape)
    )
    query_grad, key_grad, value_grad = lax.map(
        attend_back, (queries, key_rows, value_rows, live_pairs, grad_mixed, log_total)
    )
    query_grad = query_grad.reshape(images, seq_len, features)
    key_grad = key_grad.reshape(images, seq_len, features)
    value_grad = value_grad.reshape(images, seq_len, features)
    grad_packed = jnp.concatenate([query_grad, key_grad, value_grad], axis=-1)
    attend_grad = contract("isd,ise->de", first_in, grad_packed)
    attend_bias_grad = jnp.stack(
        [
            jnp.sum(query_grad.astype(jnp.float32), axis=(0, 1)),
            jnp.sum(value_grad.astype(jnp.float32), axis=(0, 1)),
        ]
    )
    grad_first = contract("ise,de->isd", grad_packed, attend_weight)
    grad_input_norm, gain_one_grad, shift_one_grad = first_back(grad_first)
    input_grad = (grad_hidden + grad_input_norm).astype(jnp.bfloat16)
    summed = lax.psum(
        (
            gain_one_grad,
            shift_one_grad,
            attend_grad,
            attend_bias_grad,
            merge_grad,
            merge_bias_grad,
            gain_two_grad,
            shift_two_grad,
            down_bias_grad,
            up_grad_all,
            up_bias_all_grad,
            down_grad_all,
        ),
        ("dp", "tensor"),
    )
    shared = summed[:9]
    share = up_weight.shape[1]
    offset = lax.axis_index("tensor") * share
    up_grad = lax.dynamic_slice_in_dim(summed[9], offset, share, 1)
    up_bias_grad = lax.dynamic_slice_in_dim(summed[10], offset, share, 0)
    down_grad = lax.dynamic_slice_in_dim(summed[11], offset, share, 0)
    return (
        output,
        input_grad,
        shared[0],
        shared[1],
        shared[2],
        shared[3],
        shared[4],
        shared[5],
        shared[6],
        shared[7],
        up_grad,
        up_bias_grad,
        down_grad,
        shared[8],
    )


def solution(mesh):
    in_specs = (
        P(("dp", "tensor"), None, None),
        P(("dp", "tensor")),
        P(("dp", "tensor"), None),
        P(),
        P(),
        P(),
        P(),
        P(),
        P(),
        P(),
        P(),
        P(None, "tensor"),
        P("tensor"),
        P("tensor", None),
        P(),
        P(("dp", "tensor"), None, None),
    )
    out_specs = (
        P(("dp", "tensor"), None, None),
        P(("dp", "tensor"), None, None),
        P(),
        P(),
        P(),
        P(),
        P(),
        P(),
        P(),
        P(),
        P(None, "tensor"),
        P("tensor"),
        P("tensor", None),
        P(),
    )
    return jax.shard_map(shards, mesh=mesh, in_specs=in_specs, out_specs=out_specs, check_vma=False)
```

profile of v0, /device:TPU:0, one launch (start us, length us, event | category | flops | bytes accessed | tf_op | source)
XLA Modules:
  0.0 596.3 jit_solution(17227819906402795988)
XLA Ops:
  8.8 2.7 convert_reduce_fusion.1
  11.6 2.9 fusion.80
  15.1 5.6 fusion.67
  20.7 3.6 fusion.107
  24.3 5.7 copy.63
  30.0 5.7 copy.64
  35.7 5.7 copy.65
  41.6 51.6 %while.26 = (s32[]{:T(128)}, bf16[7,2,257,6,64]{2,4,3,1,0:T(8,128)(2,1)}, f32[7,2,6,257]{3,2,1,0:T(8,128)S(1)}, bf16[7,2,257,6,64]{2,4,3,1,0:T(8,128)(2,1)}, pre...) while((s32[]{:T(128)}, ...), condition=%wide.region_5.6_spmd, body=%wide.region_2.5_spmd.sunk | while | flops 212410512 | bytes 12600295 | solution.py:101
  41.6 2.7 fusion.136
  45.6 3.5 fusion.138
  53.0 3.4 fusion.138
  60.3 3.4 fusion.138
  63.7 2.7 fusion.136
  67.6 3.5 fusion.138
  75.0 3.4 fusion.138
  78.5 2.7 fusion.136
  82.4 3.5 fusion.138
  89.8 3.4 fusion.138
  93.2 5.7 fusion.108
  103.2 6.1 %all-gather = bf16[4,1,384]{2,1,0:T(2,128)(2,1)S(1)} all-gather(bf16[1,1,384]{2,1,0:T(2,128)(2,1)S(1)} %reshape.166), channel_id=1, replica_groups=mesh['dp'=8,'tensor'=4] {'tensor'}, dimensions={0}, use_global_device_ids=true | all-gather | bytes 3840 | tf_op jit(solution)/shard_map/all_gather | solution.py:111
  110.0 14.2 %fusion.69 = (u16[257,1536]{1,0:T(8,128)(2,1)S(1)}, u16[257,1536]{1,0:T(8,128)(2,1)S(1)}, f32[14,257,1536]{2,1,0:T(8,128)S(1)}) fusion(f32[1536]{0:T(1024)S(1)} %reshape.168, bf16[384,1536]{1,0:T(8,128)(2,1)} %all-gather.4.cloned.1.call-done, f32[14,257,384]{2,1,0:T(8,128)} %copy-done.5, f32[384]{0:T(512)S(1)} %convert_element_type.136, ...), kind=kOutput, calls=%fused_computation.91 | convolution fusion | flops 4327863296 | bytes 30429296 | tf_op jit(solution)/shard_map/isd,df->isf/dot_general | solution.py:23
  124.2 7.5 %copy-done.4 = f32[14,257,1536]{2,1,0:T(8,128)} copy-done((f32[14,257,1536]{2,1,0:T(8,128)}, f32[14,257,1536]{2,1,0:T(8,128)S(1)}, u32[]{:S(2)}) %copy-start.4) | copy-done | bytes 22106136
  131.7 53.0 %multiply_convert_fusion.1 = (bf16[14,257,1536]{2,1,0:T(8,128)(2,1)}, f32[14,257,1536]{2,1,0:T(8,128)}) fusion(f32[14,257,1536]{2,1,0:T(8,128)S(1)} %get-tuple-element.201, f32[1536]{0:T(1024)S(1)} %reshape.168, u16[257,1536]{1,0:T(8,128)(2,1)S(1)} %get-tuple-element.129, u16[257,1536]{1,0:T(8,128)(2,1)S(1)} %get-tuple-element.128), kind=kLoop, calls=%fused_computation.75 | loop fusion | flops 392383488 | bytes 56850432 | tf_op jit(solution)/shard_map/convert_element_type | solution.py:115
  184.7 25.4 %convert_reduce_fusion = (f32[1536]{0:T(1024)S(1)}, bf16[14,257,1536]{2,1,0:T(8,128)(2,1)}) fusion(f32[14,257,1536]{2,1,0:T(8,128)} %get-tuple-element.190, bf16[1536,384]{1,0:T(8,128)(2,1)} %all-gather.6.cloned.1.call-done, bf16[14,257,384]{2,1,0:T(8,128)(2,1)} %param.35, f32[14]{0:T(128)S(1)} %convert_element_type.123, f32[14,257,1536]{2,1,0:T(8,128)} %copy-done.4, ...), kind=kOutput, calls=%fused_computation.73 | convolution fusion | flops 4342468096 | bytes 59220536 | tf_op jit(solution)/shard_map/isd,fd->isf/dot_general | solution.py:23
  210.2 12.4 %convolution_bitcast_fusion.1 = f32[384,1536]{1,0:T(8,128)} fusion(bf16[14,257,1536]{2,1,0:T(8,128)(2,1)} %get-tuple-element.205, f32[14,257,384]{2,1,0:T(8,128)} %copy-done.5, f32[384]{0:T(512)S(1)} %convert_element_type.136, f32[384]{0:T(512)S(1)} %convert_element_type.135, f32[14,257]{1,0:T(8,128)S(1)} %fusion.99, f32[14,257]{1,0:T(8,128)S(1)} %broadcast_multiply_fusion), kind=kOutput, calls=%fused_computation.127 | convolution fusion | flops 4251281664 | bytes 18970736 | tf_op jit(solution)/shard_map/isd,isf->df/dot_general | solution.py:23
  222.6 11.7 %multiply_reduce_fusion.1 = (f32[384]{0:T(512)S(1)}, f32[14,257]{1,0:T(8,128)S(1)}, f32[384]{0:T(512)S(1)}, f32[14,257,384]{2,1,0:T(8,128)S(1)}) fusion(f32[14,257,384]{2,1,0:T(8,128)} %copy-done.5, f32[14,257]{1,0:T(8,128)S(1)} %fusion.99, f32[14,257]{1,0:T(8,128)S(1)} %broadcast_multiply_fusion, f32[384]{0:T(512)S(1)} %convert_element_type.135, ...), kind=kOutput, calls=%fused_computation.115 | convolution fusion | flops 4255421952 | bytes 23333544 | tf_op jit(solution)/shard_map/isf,df->isd/dot_general | solution.py:23
  239.5 4.8 convolution_bitcast_fusion.2
  244.3 3.8 convolution_convert_fusion
  248.0 5.7 copy.67
  253.7 111.7 %while.27 = (s32[]{:T(128)}, bf16[7,2,257,6,64]{2,4,3,1,0:T(8,128)(2,1)}, bf16[7,2,257,6,64]{2,4,3,1,0:T(8,128)(2,1)}, bf16[7,2,257,6,64]{2,4,3,1,0:T(8,128)(2,1...) while((s32[]{:T(128)}, ...), condition=%wide.region_12.13_spmd, body=%wide.region_10.12_spmd.sunk | while | flops 520128960 | bytes 29770040 | solution.py:135
  256.0 3.3 multiply_reduce_fusion.5
  261.0 2.9 fusion.149
  266.5 3.2 fusion.150
  272.0 3.3 multiply_reduce_fusion.5
  276.9 2.9 fusion.149
  282.4 3.2 fusion.150
  288.0 3.3 multiply_reduce_fusion.5
  292.9 2.9 fusion.149
  298.4 3.2 fusion.150
  303.9 3.3 multiply_reduce_fusion.5
  308.8 3.0 fusion.149
  314.4 3.2 fusion.150
  319.9 3.3 multiply_reduce_fusion.5
  324.8 3.0 fusion.149
  330.4 3.3 fusion.150
  336.0 3.3 multiply_reduce_fusion.5
  340.9 2.9 fusion.149
  346.4 3.2 fusion.150
  351.9 3.3 multiply_reduce_fusion.5
  356.8 2.9 fusion.149
  362.3 3.2 fusion.150
  365.4 5.7 copy.68
  371.1 5.9 copy.69
  377.1 4.8 convert_reduce_fusion.2
  381.9 5.7 copy.70
  387.6 10.0 %fusion.84 = f32[384,1152]{1,0:T(8,128)} fusion(bf16[14,257,384]{2,1,0:T(8,128)(2,1)} %copy.70, bf16[14,257,384]{2,1,0:T(8,128)(2,1)} %copy.69, bf16[14,257,384]{2,1,0:T(8,128)(2,1)} %copy.68, bf16[14,257,384]{2,1,0:T(8,128)(2,1)} %param.20, f32[384]{0:T(512)S(1)} %copy-done.22, f32[384]{0:T(512)S(1)} %copy-done.18, f32[14,257]{1,0:T(8,128)S(1)} %copy-done.16, ...), kind=kOutput, calls=%fused_computation.125 | convolution fusion | flops 3216439296 | bytes 12854384 | tf_op jit(solution)/shard_map/isd,ise->de/dot_general | solution.py:23
  397.7 9.7 %fusion.104 = (f32[384]{0:T(512)S(1)}, f32[14,257]{1,0:T(8,128)S(1)}, f32[14,257,384]{2,1,0:T(8,128)}) fusion(f32[384]{0:T(512)S(1)} %copy-done.18, f32[14,257]{1,0:T(8,128)S(1)} %copy-done.11, bf16[14,257,384]{2,1,0:T(8,128)(2,1)S(1)} %copy-done.3, bf16[384,1152]{1,0:T(8,128)(2,1)S(1)} %copy-done, bf16[14,257,384]{2,1,0:T(8,128)(2,1)} %copy.70, ...), kind=kOutput, calls=%fused_computation.161 | convolution fusion | flops 3216435456 | bytes 17496176 | tf_op jit(solution)/shard_map/ise,de->isd/dot_general | solution.py:23
  407.4 7.8 %convolution_bitcast_fusion = f32[1536,384]{1,0:T(8,128)} fusion(bf16[14,257,1536]{2,1,0:T(8,128)(2,1)S(1)} %bitcast.173, bf16[14,257,384]{2,1,0:T(8,128)(2,1)S(1)} %copy-done.7, f32[14]{0:T(128)S(1)} %convert_element_type.123), kind=kOutput, calls=%fused_computation.126 | convolution fusion | flops 4248518400 | bytes 16175672 | tf_op jit(solution)/shard_map/isf,isd->fd/dot_general | solution.py:23
  416.1 5.4 fusion.78
  421.5 43.7 %all-reduce.1 = (f32[384]{0:T(512)}, f32[384]{0:T(512)}, f32[2,384]{1,0:T(2,128)}, f32[384]{0:T(512)}, f32[384]{0:T(512)}, /*index=5*/f32[384]{0:T(512)}, f32[1536]{0:T(1024)S(1)}, f32[384]{0:T(512)}) all-reduce(f32[384]{0:T(512)S(1)} %get-tuple-element.132, ...), channel_id=1, replica_groups=mesh['dp'=8,'tensor'=4] {'dp','tensor'}, use_global_device_ids=true, to_apply=%region_16.17 | all-reduce | flops 4608 | bytes 36864 | tf_op jit(solution)/shard_map/psum | solution.py:152
  465.8 9.8 %add_convert_fusion.1 = bf16[14,257,384]{2,1,0:T(8,128)(2,1)} fusion(f32[14,257,384]{2,1,0:T(8,128)} %copy-done.1, bf16[14,257,384]{2,1,0:T(8,128)(2,1)} %param.35, f32[14,257]{1,0:T(8,128)S(1)} %negate_multiply_fusion.1, f32[14,257]{1,0:T(8,128)S(1)} %negate_multiply_fusion.2, f32[14,257]{1,0:T(8,128)S(1)} %multiply_multiply_fusion.5, ...), kind=kLoop, calls=%fused_computation.117 | loop fusion | flops 17961216 | bytes 19416344 | tf_op jit(solution)/shard_map/convert_element_type | solution.py:151
  475.6 10.2 %add_convert_fusion.2 = bf16[14,257,384]{2,1,0:T(8,128)(2,1)} fusion(f32[14,257,384]{2,1,0:T(8,128)S(1)} %bitcast.168, f32[384]{0:T(512)S(1)} %copy-done.23, f32[14]{0:T(128)S(1)} %convert_element_type.123, bf16[14,257,1536]{2,1,0:T(8,128)(2,1)} %get-tuple-element.189, bf16[1536,384]{1,0:T(8,128)(2,1)S(1)} %copy-done.31), kind=kOutput, calls=%fused_computation.120 | convolution fusion | flops 4249900032 | bytes 20524088 | tf_op jit(solution)/shard_map/isf,fd->isd/dot_general | solution.py:23
  485.9 97.4 %all-reduce.5.cloned.1.call-done = (f32[384,1152]{1,0:T(8,128)}, f32[384,384]{1,0:T(8,128)}, f32[384,1536]{1,0:T(8,128)}, f32[1536,384]{1,0:T(8,128)}) async-done(((f32[384,1152]{1,0:T(8,128)}, f32[384,384]{1,0:T(8,128)}, f32[384,1536]{1,0:T(8,128)}, f32[1536,384]{1,0:T(8,128)}), (f32[384,1152]{1,0:T(8,128)}, f32[384,384]{1,0:T(8,128)}, f32[384,1536]{1,0:T(8,128)}, ...) | async-done | bytes 7077904 | tf_op jit(solution)/shard_map/psum | solution.py:152
  585.6 2.8 copy.109
  (190 shorter events, 81.3 us)
Async XLA Ops:
  7.2 7.9 %copy-start = (bf16[384,1152]{1,0:T(8,128)(2,1)S(1)}, bf16[384,1152]{1,0:T(8,128)(2,1)}, u32[]{:S(2)}) copy-start(bf16[384,1152]{1,0:T(8,128)(2,1)} %param.25) | copy-start | bytes 2654212
  7.2 7.3 %copy-start.24 = (bf16[384]{0:T(512)(128)(2,1)S(1)}, bf16[384]{0:T(512)(128)(2,1)}, u32[]{:S(2)}) copy-start(bf16[384]{0:T(512)(128)(2,1)} %param.23) | copy-start | bytes 2308
  7.2 7.3 %copy-start.20 = (bf16[2,384]{1,0:T(2,128)(2,1)S(1)}, bf16[2,384]{1,0:T(2,128)(2,1)}, u32[]{:S(2)}) copy-start(bf16[2,384]{1,0:T(2,128)(2,1)} %param.26) | copy-start | bytes 4612
  7.2 7.4 %copy-start.25 = (bf16[384]{0:T(512)(128)(2,1)S(1)}, bf16[384]{0:T(512)(128)(2,1)}, u32[]{:S(2)}) copy-start(bf16[384]{0:T(512)(128)(2,1)} %param.24) | copy-start | bytes 2308
  7.2 102.7 %all-gather.4.cloned.1.call-start = ((), (), s32[]{:S(2)}) async-start(), calls=%async_computation | async-start | bytes 1474560 | tf_op jit(solution)/shard_map/all_gather | solution.py:109
  8.0 176.8 %all-gather.6.cloned.1.call-start = ((), (), s32[]{:S(2)}) async-start(), calls=%async_computation.1 | async-start | bytes 1474560 | tf_op jit(solution)/shard_map/all_gather | solution.py:110
  8.7 574.5 %all-reduce.5.cloned.1.call-start = ((), (), s32[]{:S(2)}) async-start(), calls=%async_computation.2 | async-start | bytes 14155776 | tf_op jit(solution)/shard_map/psum | solution.py:152
  8.8 6.3 %copy-start.2 = (bf16[14,257,384]{2,1,0:T(8,128)(2,1)S(1)}, bf16[14,257,384]{2,1,0:T(8,128)(2,1)}, u32[]{:S(2)}) copy-start(bf16[14,257,384]{2,1,0:T(8,128)(2,1)} %param.20) | copy-start | bytes 8289796
  11.6 9.1 %copy-start.10 = (f32[14,257]{1,0:T(8,128)}, f32[14,257]{1,0:T(8,128)S(1)}, u32[]{:S(2)}) copy-start(f32[14,257]{1,0:T(8,128)S(1)} %broadcast_multiply_fusion.1) | copy-start | bytes 43180
  14.5 0.6 copy-start.13
  14.5 6.2 %copy-start.15 = (f32[14,257]{1,0:T(8,128)}, f32[14,257]{1,0:T(8,128)S(1)}, u32[]{:S(2)}) copy-start(f32[14,257]{1,0:T(8,128)S(1)} %fusion.98) | copy-start | bytes 43180
  14.5 6.1 %copy-start.17 = (f32[384]{0:T(512)}, f32[384]{0:T(512)S(1)}, u32[]{:S(2)}) copy-start(f32[384]{0:T(512)S(1)} %convert_element_type.124) | copy-start | bytes 4612
  14.6 6.1 %copy-start.21 = (f32[384]{0:T(512)}, f32[384]{0:T(512)S(1)}, u32[]{:S(2)}) copy-start(f32[384]{0:T(512)S(1)} %convert_element_type.125) | copy-start | bytes 4612
  30.0 11.4 %copy-start.19 = (s32[14,256]{1,0:T(8,128)S(1)}, s32[14,256]{1,0:T(8,128)}, u32[]{:S(2)}) copy-start(s32[14,256]{1,0:T(8,128)} %param.22) | copy-start | bytes 43012
  41.5 51.7 %copy-start.33 = (s32[14]{0:T(128)S(1)}, s32[14]{0:T(128)}, u32[]{:S(2)}) copy-start(s32[14]{0:T(128)} %param.21) | copy-start | bytes 172
  41.6 51.6 %copy-start.26 = (bf16[384]{0:T(512)(128)(2,1)S(1)}, bf16[384]{0:T(512)(128)(2,1)}, u32[]{:S(2)}) copy-start(bf16[384]{0:T(512)(128)(2,1)} %param.28) | copy-start | bytes 2308
  41.6 51.6 %copy-start.12 = (bf16[384,384]{1,0:T(8,128)(2,1)S(1)}, bf16[384,384]{1,0:T(8,128)(2,1)}, u32[]{:S(2)}) copy-start(bf16[384,384]{1,0:T(8,128)(2,1)} %param.27) | copy-start | bytes 884740
  98.9 2.5 copy-start.5
  98.9 4.2 copy-start.27
  98.9 4.2 copy-start.30
  98.9 10.4 %copy-start.28 = (bf16[384]{0:T(512)(128)(2,1)S(1)}, bf16[384]{0:T(512)(128)(2,1)}, u32[]{:S(2)}) copy-start(bf16[384]{0:T(512)(128)(2,1)} %param.30) | copy-start | bytes 2308
  99.0 10.4 %copy-start.29 = (bf16[384]{0:T(512)(128)(2,1)S(1)}, bf16[384]{0:T(512)(128)(2,1)}, u32[]{:S(2)}) copy-start(bf16[384]{0:T(512)(128)(2,1)} %param.34) | copy-start | bytes 2308
  124.2 7.5 %copy-start.4 = (f32[14,257,1536]{2,1,0:T(8,128)}, f32[14,257,1536]{2,1,0:T(8,128)S(1)}, u32[]{:S(2)}) copy-start(f32[14,257,1536]{2,1,0:T(8,128)S(1)} %get-tuple-element.201) | copy-start | bytes 66318340
  210.2 12.4 %copy-start.32 = (bf16[384,1536]{1,0:T(8,128)(2,1)S(1)}, bf16[384,1536]{1,0:T(8,128)(2,1)}, u32[]{:S(2)}) copy-start(bf16[384,1536]{1,0:T(8,128)(2,1)} %all-gather.4.cloned.1.call-done) | copy-start | bytes 3538948
  210.2 24.2 %slice-start = ((s8[5677056]{0:T(1024)(128)(4,1)}), s8[4194304]{0:T(1024)(128)(4,1)S(1)}, s32[]{:S(2)}) async-start(s8[5677056]{0:T(1024)(128)(4,1)} %bitcast.165), calls=%async_computation.3 | async-start | bytes 8388608
  222.6 11.8 %slice-start.1 = ((s8[5677056]{0:T(1024)(128)(4,1)}), s8[1482752]{0:T(1024)(128)(4,1)S(1)}, s32[]{:S(2)}) async-start(s8[5677056]{0:T(1024)(128)(4,1)} %bitcast.165), calls=%async_computation.4 | async-start | bytes 2965504
  234.4 2.7 copy-start.6
  237.1 2.4 copy-start.1
  377.0 10.5 %copy-start.11 = (f32[14,257]{1,0:T(8,128)S(1)}, f32[14,257]{1,0:T(8,128)}, u32[]{:S(2)}) copy-start(f32[14,257]{1,0:T(8,128)} %copy-done.10) | copy-start | bytes 43180
  377.0 10.5 %copy-start.16 = (f32[14,257]{1,0:T(8,128)S(1)}, f32[14,257]{1,0:T(8,128)}, u32[]{:S(2)}) copy-start(f32[14,257]{1,0:T(8,128)} %copy-done.15) | copy-start | bytes 43180
  377.1 10.5 %copy-start.18 = (f32[384]{0:T(512)S(1)}, f32[384]{0:T(512)}, u32[]{:S(2)}) copy-start(f32[384]{0:T(512)} %copy-done.17) | copy-start | bytes 4612
  377.1 10.5 %copy-start.22 = (f32[384]{0:T(512)S(1)}, f32[384]{0:T(512)}, u32[]{:S(2)}) copy-start(f32[384]{0:T(512)} %copy-done.21) | copy-start | bytes 4612
  387.6 10.1 %copy-start.3 = (bf16[14,257,384]{2,1,0:T(8,128)(2,1)S(1)}, bf16[14,257,384]{2,1,0:T(8,128)(2,1)}, u32[]{:S(2)}) copy-start(bf16[14,257,384]{2,1,0:T(8,128)(2,1)} %param.20) | copy-start | bytes 8289796
  387.6 10.1 %copy-start.8 = (bf16[14,257,384]{2,1,0:T(8,128)(2,1)S(1)}, bf16[14,257,384]{2,1,0:T(8,128)(2,1)}, u32[]{:S(2)}) copy-start(bf16[14,257,384]{2,1,0:T(8,128)(2,1)} %copy.68) | copy-start | bytes 8289796
  387.6 19.8 %slice-start.4 = ((s8[11354112]{0:T(1024)(128)(4,1)}), s8[4194304]{0:T(1024)(128)(4,1)S(1)}, s32[]{:S(2)}) async-start(s8[11354112]{0:T(1024)(128)(4,1)} %bitcast.172), calls=%async_computation.7 | async-start | bytes 8388608
  387.6 19.8 %slice-start.5 = ((s8[11354112]{0:T(1024)(128)(4,1)}), s8[4194304]{0:T(1024)(128)(4,1)S(1)}, s32[]{:S(2)}) async-start(s8[11354112]{0:T(1024)(128)(4,1)} %bitcast.172), calls=%async_computation.8 | async-start | bytes 8388608
  397.7 9.7 %slice-start.6 = ((s8[11354112]{0:T(1024)(128)(4,1)}), s8[2965504]{0:T(1024)(128)(4,1)S(1)}, s32[]{:S(2)}) async-start(s8[11354112]{0:T(1024)(128)(4,1)} %bitcast.172), calls=%async_computation.9 | async-start | bytes 5931008
  397.7 9.7 %copy-start.7 = (bf16[14,257,384]{2,1,0:T(8,128)(2,1)S(1)}, bf16[14,257,384]{2,1,0:T(8,128)(2,1)}, u32[]{:S(2)}) copy-start(bf16[14,257,384]{2,1,0:T(8,128)(2,1)} %param.35) | copy-start | bytes 8289796
  415.2 0.7 copy-start.14
  416.1 59.5 %slice-start.2 = ((s8[5677056]{0:T(1024)(128)(4,1)}), s8[1482752]{0:T(1024)(128)(4,1)S(1)}, s32[]{:S(2)}) async-start(s8[5677056]{0:T(1024)(128)(4,1)} %bitcast.167), calls=%async_computation.5 | async-start | bytes 2965504
  465.8 9.8 %slice-start.3 = ((s8[5677056]{0:T(1024)(128)(4,1)}), s8[4194304]{0:T(1024)(128)(4,1)S(1)}, s32[]{:S(2)}) async-start(s8[5677056]{0:T(1024)(128)(4,1)} %bitcast.167), calls=%async_computation.6 | async-start | bytes 8388608
  465.8 9.8 %copy-start.23 = (f32[384]{0:T(512)S(1)}, f32[384]{0:T(512)}, u32[]{:S(2)}) copy-start(f32[384]{0:T(512)} %convert_element_type.140) | copy-start | bytes 4612
  465.8 9.8 %copy-start.31 = (bf16[1536,384]{1,0:T(8,128)(2,1)S(1)}, bf16[1536,384]{1,0:T(8,128)(2,1)}, u32[]{:S(2)}) copy-start(bf16[1536,384]{1,0:T(8,128)(2,1)} %all-gather.6.cloned.1.call-done) | copy-start | bytes 3538948
  583.3 5.2 copy-start.9
Sparse Core Ops, SparseCore 0:
  9.6 20.1 all-gather.3
  31.4 17.4 all-gather.5
  415.3 167.8 all-reduce.4
where the time goes:
time: 608 us; the launch traced here: 596 us
  matrix products  264 us (43%)
  other arithmetic  105 us (17%)
  waiting for transfers between devices  98.8 us (16%)
  local copies, waits for them, and re-layouts  62.6 us (10%)
  blocking collectives  49.8 us (8%)
  between operations  15 us (2%)
    dot_general x61, matrix products, contract(): return jnp.einsum(form, left, right, preferred_element_type=jnp.float32)  264 us
    psum x1, waiting for transfers between devices, shards(): lax.psum((gain_one_grad, shift_one_grad, attend_grad, attend_bias_grad, m...  97.4 us
    convert_element_type x1, other arithmetic, shards(): activated = act_full.astype(jnp.bfloat16)  53 us
    psum x1, blocking collectives, shards(): lax.psum((gain_one_grad, shift_one_grad, attend_grad, attend_bias_grad, m...  43.7 us
    unnamed x85, local copies, waits for them, and re-layouts  15.4 us
  transfers between devices with their start and end apart: 3, of which 1 were waited for; matrix products, arithmetic and copies ran while one was open for 31% of the time, Pallas kernels for 0%

commit v1 on v0

v1 whole, which is shorter than its diff:
```python
import functools

import jax
import jax.numpy as jnp
from jax import lax
from jax.experimental import pallas as pl
from jax.experimental.pallas import tpu as pltpu
from jax.sharding import PartitionSpec as P

HEADS = 6
HEAD = 64
MAIN = 256
EPS = 1e-06
MASKED = -1e30
f32, bf16 = jnp.float32, jnp.bfloat16

NN = ((1,), (0,))
NT = ((1,), (1,))
TN = ((0,), (0,))


def dot(left, right, dims=NN):
    return lax.dot_general(left, right, (dims, ((), ())), preferred_element_type=f32)


def rows_where(index, value, rows, dtype):
    columns = value.shape[-1]
    at = lax.broadcasted_iota(jnp.int32, (rows, columns), 0)
    return jnp.where(at == index, value, 0.0).astype(dtype)


def wide(column, width):
    return jnp.concatenate([column] * (width // 128), axis=1)


def as_column(row):
    return jnp.broadcast_to(row, (128, row.shape[1])).T


def norm_columns(values):
    center = values - jnp.mean(values, axis=0, keepdims=True)
    scale = lax.rsqrt(jnp.mean(center * center, axis=0, keepdims=True) + EPS)
    return center * scale, scale


def norm_rows(values):
    center = values - jnp.mean(values, axis=1, keepdims=True)
    scale = lax.rsqrt(jnp.mean(center * center, axis=1, keepdims=True) + EPS)
    return center * scale, scale


def norm_back(grad, normed, scale, axis):
    mean_grad = jnp.mean(grad, axis=axis, keepdims=True)
    mean_both = jnp.mean(grad * normed, axis=axis, keepdims=True)
    return scale * (grad - mean_grad - normed * mean_both)


def gelu_both(pre):
    curve = 0.5 + 0.5 * lax.erf(pre * 0.7071067811865476)
    bell = 0.3989422804014327 * jnp.exp(-0.5 * pre * pre)
    return pre * curve, curve + pre * bell


def head_rows(rows, features):
    at = lax.broadcasted_iota(jnp.int32, (rows, features), 0)
    head = lax.broadcasted_iota(jnp.int32, (rows, features), 1) // HEAD
    return jnp.where(at == head, 1.0, 0.0)


def lane_live(live_ref, first, count):
    flags = [
        jnp.full((1, MAIN), live_ref[first + g].astype(f32)) for g in range(count)
    ]
    return jnp.concatenate(flags, axis=1)


def row_live(live_ref, count, rows):
    at = lax.broadcasted_iota(jnp.int32, (rows, 1), 0)
    flags = jnp.zeros((rows, 1), f32)
    for image in range(count):
        flags = jnp.where(at == image, live_ref[image].astype(f32), flags)
    return flags


def take_left(left_ref, to_ref, count):
    to_ref[...] = jnp.zeros_like(to_ref)
    for image in range(count):
        to_ref[image : image + 1, :] = left_ref[image].astype(f32)[0:1, :]


def attend_kernel(
    count, group,
    tok, left, pmask, live, vec, aw, mw,
    fi_out, qkv_out, probs_out, edge_out, inv_out, lp_out, lself_out, att_out, hid_out,
    fil_out, qkvl_out, attl_out, hidl_out,
    awt, mwt, fia, atta, cols, peaks, xl, qkvl, attl,
):
    step = pl.program_id(0)
    features = aw.shape[0]
    packed = aw.shape[1]
    rows = xl.shape[0]
    heads = head_rows(rows, features)

    @pl.when(step == 0)
    def _():
        for part in range(3):
            span = slice(part * features, (part + 1) * features)
            block = aw[:, span].astype(f32).T
            awt[span, :features] = (block * (HEAD**-0.5 if part == 0 else 1.0)).astype(bf16)
            if part == 1:
                bias = jnp.zeros((1, features), f32)
            else:
                bias = vec[2:3, :] * (HEAD**-0.5) if part == 0 else vec[3:4, :]
            awt[span, features:] = rows_where(0, bias, 128, f32).T.astype(bf16)
        mwt[:, :features] = mw[...].astype(f32).T.astype(bf16)
        mwt[:, features:] = rows_where(0, vec[4:5, :], 128, f32).T.astype(bf16)
        ones = rows_where(0, jnp.ones((1, fia.shape[1]), f32), 128, bf16)
        fia[features:, :] = ones
        atta[features:, :] = ones
        cols[0] = as_column(vec[0:1, :])
        cols[1] = as_column(vec[1:2, :])
        peaks[...] = jnp.zeros_like(peaks)
        take_left(left, xl, count)
        normed, _ = norm_rows(xl[...])
        fil = (normed * vec[0:1, :] + vec[1:2, :]).astype(bf16)
        fil_out[...] = fil.astype(f32)
        bias = jnp.concatenate([vec[2:3, :], jnp.zeros((1, features), f32), vec[3:4, :]], axis=1)
        rounded = (dot(fil, aw[...]) + bias).astype(bf16).astype(f32)
        at = lax.broadcasted_iota(jnp.int32, (1, packed), 1)
        qkvl[...] = rounded * jnp.where(at < features, HEAD**-0.5, 1.0)
        qkvl_out[...] = qkvl[...]
        attl[...] = jnp.zeros_like(attl)

    tokens = jnp.concatenate([tok[g].astype(f32).T for g in range(group)], axis=1)
    width = group * MAIN
    normed, _ = norm_columns(tokens)
    fi = (normed * wide(cols[0], width) + wide(cols[1], width)).astype(bf16)
    fia[:features, :] = fi
    qkv = dot(awt[...], fia[...]).astype(bf16)
    one_row = rows_where(0, jnp.ones((1, MAIN), f32), 16, bf16)
    for g in range(group):
        image = step * group + g
        lanes = slice(g * MAIN, (g + 1) * MAIN)
        fi_out[g] = fi[:, lanes]
        qt = qkv[:features, lanes]
        kt = qkv[features : 2 * features, lanes]
        vt = qkv[2 * features :, lanes]
        qkv_out[g] = qkv[:, lanes]
        qkv_row = qkvl[pl.ds(image, 1), :]
        ql, kl, vl = (qkv_row[:, p * features : (p + 1) * features] for p in range(3))
        qlb, klb, vlb = ((heads * v).astype(bf16) for v in (ql, kl, vl))

        key_bias = jnp.where(pmask[pl.ds(image, 1), :] == 1, 0.0, MASKED)
        moved = pltpu.roll(key_bias, 1, axis=1)
        left_bias = moved[:, 0:1]
        at = lax.broadcasted_iota(jnp.int32, moved.shape, 1)
        main_bias = jnp.where(at == 0, 0.0, moved)
        bias_rows = rows_where(0, main_bias, 16, bf16)

        slk = dot(klb, qt) + left_bias
        outs = []
        for h in range(HEADS):
            span = slice(h * HEAD, (h + 1) * HEAD)
            scores = dot(
                jnp.concatenate([kt[span], bias_rows], axis=0),
                jnp.concatenate([qt[span], one_row], axis=0),
                TN,
            )
            peak = jnp.maximum(jnp.max(scores, axis=0, keepdims=True), slk[h : h + 1, :])
            raised = jnp.exp(scores - peak).astype(bf16)
            probs_out[g, h] = raised
            peaks[g, h : h + 1, :] = peak
            outs.append(dot(jnp.concatenate([vt[span], one_row], axis=0), raised))
        edge = jnp.exp(slk - peaks[g])
        edge_out[g] = edge
        added = dot(vlb, edge.astype(bf16), TN)
        for h in range(HEADS):
            span = slice(h * HEAD, (h + 1) * HEAD)
            inv = 1.0 / (outs[h][HEAD : HEAD + 1, :] + edge[h : h + 1, :])
            inv_out[g, h : h + 1, :] = inv
            mixed = ((outs[h][:HEAD, :] + added[span]) * inv).astype(bf16)
            atta[span, lanes] = mixed
            att_out[g, span, :] = mixed

        sl = dot(qlb, kt) + main_bias
        self_score = jnp.sum(heads * (ql * kl), axis=1, keepdims=True) + left_bias
        peak = jnp.maximum(jnp.max(sl, axis=1, keepdims=True), self_score)
        raised = jnp.exp(sl - peak)
        raised_self = jnp.exp(self_score - peak)
        inv = 1.0 / (jnp.sum(raised, axis=1, keepdims=True) + raised_self)
        lp = raised * inv
        lself = raised_self * inv
        lp_out[g] = lp
        lself_out[g] = jnp.broadcast_to(lself, (rows, 128))
        mixed = dot(lp.astype(bf16), vt, NT) + lself * vl
        attl[pl.ds(image, 1), :] = jnp.sum(mixed * heads, axis=0, keepdims=True).astype(bf16).astype(f32)

    branch = dot(mwt[...], atta[...])
    hidden = tokens + lane_live(live, step * group, group) * branch
    for g in range(group):
        hid_out[g] = hidden[:, g * MAIN : (g + 1) * MAIN]

    @pl.when(step == pl.num_programs(0) - 1)
    def _():
        attl_out[...] = attl[...]
        branch = dot(attl[...].astype(bf16), mw[...]) + vec[4:5, :]
        hidl_out[...] = xl[...] + row_live(live, count, rows) * branch


def feed_kernel(
    count, group,
    hid, att, cot, cleft, live, vec, hidl, attl, upw, upb, dnw,
    out, gh_out, ga_out, ghl_out, gal_out, up_acc, down_acc, merge_acc, sums_out,
    upt, dnt, sia, atta, act, gpre, gb, cols, gsum, xl, outl,
):
    step = pl.program_id(0)
    features, hidden_units = upw.shape
    rows = xl.shape[0]
    width = group * MAIN
    part = 384

    @pl.when(step == 0)
    def _():
        for at in range(0, hidden_units, part):
            span = slice(at, at + part)
            upt[span, :features] = upw[:, span].astype(f32).T.astype(bf16)
            upt[span, features:] = rows_where(0, upb[0:1, span].astype(f32), 128, f32).T.astype(bf16)
            dnt[:, span] = dnw[span, :].astype(f32).T.astype(bf16)
        ones = rows_where(0, jnp.ones((1, width), f32), 128, bf16)
        sia[features:, :] = ones
        atta[features:, :] = ones
        cols[0] = as_column(vec[5:6, :])
        cols[1] = as_column(vec[6:7, :])
        cols[2] = as_column(vec[7:8, :])
        gsum[...] = jnp.zeros_like(gsum)
        take_left(cleft, xl, count)
        alive = row_live(live, count, rows)
        normed, scale = norm_rows(hidl[...])
        si = (normed * vec[5:6, :] + vec[6:7, :]).astype(bf16)
        pre = dot(si, upw[...]) + upb[0:1, :].astype(f32)
        value, slope = gelu_both(pre)
        value = value.astype(bf16)
        outl[...] = hidl[...] + alive * (dot(value, dnw[...]) + vec[7:8, :])
        grad_branch = (alive * xl[...]).astype(bf16)
        grad_pre = (dot(grad_branch, dnw[...], NT) * slope).astype(bf16)
        grad_second = dot(grad_pre, upw[...], NT)
        grad_hidden = xl[...] + norm_back(grad_second * vec[5:6, :], normed, scale, 1)
        ghl_out[...] = grad_hidden
        grad_attn = (alive * grad_hidden).astype(bf16)
        gal_out[...] = grad_attn.astype(f32)
        one = jnp.ones((rows, 16), bf16)
        up_acc[...] = dot(jnp.concatenate([si.astype(f32), one.astype(f32)], axis=1).astype(bf16), grad_pre, TN)
        down_acc[...] = dot(grad_branch, value, TN)
        merge_acc[...] = dot(
            jnp.concatenate([attl[...], one.astype(f32)], axis=1).astype(bf16), grad_attn, TN
        )
        sums_out[...] = jnp.zeros_like(sums_out)
        sums_out[0:1, :] = jnp.sum(grad_second * normed, axis=0, keepdims=True)
        sums_out[1:2, :] = jnp.sum(grad_second, axis=0, keepdims=True)
        sums_out[2:3, :] = jnp.sum(grad_branch.astype(f32), axis=0, keepdims=True)

    alive = lane_live(live, step * group, group)
    hidden = jnp.concatenate([hid[g] for g in range(group)], axis=1)
    normed, scale = norm_columns(hidden)
    sia[:features, :] = (normed * wide(cols[0], width) + wide(cols[1], width)).astype(bf16)
    cotangent = jnp.concatenate([cot[g].astype(f32).T for g in range(group)], axis=1)
    gb[...] = (cotangent * alive).astype(bf16)
    for at in range(0, hidden_units, part):
        span = slice(at, at + part)
        pre = dot(upt[span, :], sia[...])
        grad_act = dot(dnw[span, :], gb[...])
        value, slope = gelu_both(pre)
        act[span, :] = value.astype(bf16)
        gpre[span, :] = (grad_act * slope).astype(bf16)
    reduced = dot(dnt[...], act[...])
    grad_second = dot(upw[...], gpre[...])
    result = hidden + alive * (reduced + wide(cols[2], width))
    up_acc[...] += dot(sia[: up_acc.shape[0], :], gpre[...], NT)
    down_acc[...] += dot(gb[...], act[...], NT)
    grad_hidden = cotangent + norm_back(grad_second * wide(cols[0], width), normed, scale, 0)
    grad_attn = (alive * grad_hidden).astype(bf16)
    both = grad_second * normed
    for at in range(0, width, 128):
        gsum[0] += both[:, at : at + 128]
        gsum[1] += grad_second[:, at : at + 128]
    sums_out[2:3, :] += dot(jnp.ones((16, width), bf16), gb[...], NT)[0:1, :]
    for g in range(group):
        lanes = slice(g * MAIN, (g + 1) * MAIN)
        image = step * group + g
        gh_out[g] = grad_hidden[:, lanes]
        ga_out[g] = grad_attn[:, lanes]
        atta[:features, lanes] = att[g]
        out[g, :MAIN, :] = result[:, lanes].T.astype(bf16)
        out[g, MAIN : MAIN + 1, :] = outl[pl.ds(image, 1), :].astype(bf16)
    merge_acc[...] += dot(atta[: merge_acc.shape[0], :], grad_attn, NT)

    @pl.when(step == pl.num_programs(0) - 1)
    def _():
        sums_out[0:1, :] += jnp.sum(gsum[0].T, axis=0, keepdims=True)
        sums_out[1:2, :] += jnp.sum(gsum[1].T, axis=0, keepdims=True)


def attend_back_kernel(
    count, group,
    qkv, probs, edge, inv, lp, lself, att, ga, fi, fil, qkvl, attl, gal, mw,
    gp_out, gpl_out, acc,
    fia, gpa, gml, dots, gmleft, gpl,
):
    step = pl.program_id(0)
    features = mw.shape[0]
    rows = gal.shape[0]
    heads = head_rows(rows, features)

    @pl.when(step == 0)
    def _():
        fia[features:, :] = rows_where(0, jnp.ones((1, fia.shape[1]), f32), 16, bf16)
        acc[...] = jnp.zeros_like(acc)
        dots[...] = jnp.zeros_like(dots)
        gmleft[...] = dot(gal[...].astype(bf16), mw[...], NT).astype(bf16).astype(f32)
        gpl[...] = jnp.zeros_like(gpl)

    at16 = lax.broadcasted_iota(jnp.int32, (16, MAIN), 0)
    minus = jnp.where(at16 < 2, -1.0, 0.0).astype(bf16)
    for g in range(group):
        image = step * group + g
        lanes = slice(g * MAIN, (g + 1) * MAIN)
        qt = qkv[g, :features, :]
        kt = qkv[g, features : 2 * features, :]
        vt = qkv[g, 2 * features :, :]
        fia[:features, lanes] = fi[g]
        grad_mixed = dot(mw[...], ga[g]).astype(bf16).astype(f32)
        both = grad_mixed * att[g].astype(f32)
        edge_f = edge[g]
        tails = []
        for h in range(HEADS):
            span = slice(h * HEAD, (h + 1) * HEAD)
            row_inv = inv[g, h : h + 1, :]
            gml[span, lanes] = (grad_mixed[span] * row_inv).astype(bf16)
            row_dot = jnp.sum(both[span], axis=0, keepdims=True) * row_inv
            dots[g, h : h + 1, :] = row_dot
            high = row_dot.astype(bf16).astype(f32)
            tails.append(
                jnp.where(at16 == 0, high, jnp.where(at16 == 1, row_dot - high, 0.0)).astype(bf16)
            )

        qkv_row = qkvl[pl.ds(image, 1), :]
        ql, kl, vl = (qkv_row[:, p * features : (p + 1) * features] for p in range(3))
        qlb, klb, vlb = ((heads * v).astype(bf16) for v in (ql, kl, vl))
        scaled = gml[:, lanes]
        edge_grad = (edge_f * (dot(vlb, scaled) - dots[g])).astype(bf16)
        grad_kl = jnp.sum(dot(edge_grad, qt, NT) * heads, axis=0, keepdims=True)
        grad_vl = jnp.sum(dot(edge_f.astype(bf16), scaled, NT) * heads, axis=0, keepdims=True)
        gm_row = gmleft[pl.ds(image, 1), :]
        gmb = (heads * gm_row).astype(bf16)
        row_dot = jnp.sum(heads * (gm_row * attl[pl.ds(image, 1), :]), axis=1, keepdims=True)
        left_grad = (lp[g] * (dot(gmb, vt) - row_dot)).astype(bf16)
        self_prob = lself[g][:, 0:1]
        self_grad = self_prob * (jnp.sum(heads * (gm_row * vl), axis=1, keepdims=True) - row_dot)
        self_grad = self_grad.astype(bf16).astype(f32)
        self_row = jnp.sum(heads * self_grad, axis=0, keepdims=True)
        prob_row = jnp.sum(heads * self_prob.astype(bf16).astype(f32), axis=0, keepdims=True)
        grad_ql = jnp.sum(dot(left_grad, kt, NT) * heads, axis=0, keepdims=True) + self_row * kl
        grad_kl = grad_kl + self_row * ql
        grad_vl = grad_vl + prob_row * gm_row
        gpl[pl.ds(image, 1), :] = (
            jnp.concatenate([grad_ql * HEAD**-0.5, grad_kl, grad_vl], axis=1).astype(bf16).astype(f32)
        )
        add_q = dot(klb, edge_grad, TN)
        add_k = dot(qlb, left_grad, TN)
        add_v = dot(gmb, lp[g].astype(bf16), TN)
        for h in range(HEADS):
            span = slice(h * HEAD, (h + 1) * HEAD)
            raised = probs[g, h]
            change = dot(
                jnp.concatenate([vt[span], minus], axis=0),
                jnp.concatenate([scaled[span], tails[h]], axis=0),
                TN,
            )
            score_grad = raised * change.astype(bf16)
            grad_q = (dot(kt[span], score_grad) + add_q[span]) * HEAD**-0.5
            grad_k = dot(qt[span], score_grad, NT) + add_k[span]
            grad_v = dot(scaled[span], raised, NT) + add_v[span]
            for p, grad in enumerate((grad_q, grad_k, grad_v)):
                to = slice(p * features + h * HEAD, p * features + (h + 1) * HEAD)
                rounded = grad.astype(bf16)
                gpa[to, lanes] = rounded
                gp_out[g, to, :] = rounded
    acc[...] += dot(fia[...], gpa[...], NT)

    @pl.when(step == pl.num_programs(0) - 1)
    def _():
        gpl_out[...] = gpl[...]
        one = jnp.ones((rows, 16), f32)
        acc[...] += dot(
            jnp.concatenate([fil[...], one], axis=1).astype(bf16), gpl[...].astype(bf16), TN
        )


def first_back_kernel(
    count, group,
    tok, left, gp, gh, gpl, ghl, vec, aw,
    out, sums_out,
    cols, gsum, xl, outl,
):
    step = pl.program_id(0)
    width = group * MAIN

    @pl.when(step == 0)
    def _():
        cols[...] = as_column(vec[0:1, :])
        gsum[...] = jnp.zeros_like(gsum)
        take_left(left, xl, count)
        normed, scale = norm_rows(xl[...])
        grad_first = dot(gpl[...].astype(bf16), aw[...], NT)
        outl[...] = ghl[...] + norm_back(grad_first * vec[0:1, :], normed, scale, 1)
        sums_out[...] = jnp.zeros_like(sums_out)
        sums_out[0:1, :] = jnp.sum(grad_first * normed, axis=0, keepdims=True)
        sums_out[1:2, :] = jnp.sum(grad_first, axis=0, keepdims=True)

    tokens = jnp.concatenate([tok[g].astype(f32).T for g in range(group)], axis=1)
    normed, scale = norm_columns(tokens)
    packed = jnp.concatenate([gp[g] for g in range(group)], axis=1)
    grad_first = dot(aw[...], packed)
    grad = norm_back(grad_first * wide(cols[...], width), normed, scale, 0)
    both = grad_first * normed
    for at in range(0, width, 128):
        gsum[0] += both[:, at : at + 128]
        gsum[1] += grad_first[:, at : at + 128]
    for g in range(group):
        image = step * group + g
        result = gh[g] + grad[:, g * MAIN : (g + 1) * MAIN]
        out[g, :MAIN, :] = result.T.astype(bf16)
        out[g, MAIN : MAIN + 1, :] = outl[pl.ds(image, 1), :].astype(bf16)

    @pl.when(step == pl.num_programs(0) - 1)
    def _():
        sums_out[0:1, :] += jnp.sum(gsum[0].T, axis=0, keepdims=True)
        sums_out[1:2, :] += jnp.sum(gsum[1].T, axis=0, keepdims=True)


def per_step(group, *dims):
    return pl.BlockSpec((group, *dims), lambda i: (i,) + (0,) * len(dims))


def whole(*dims):
    return pl.BlockSpec(dims, lambda i: (0,) * len(dims))


LIVE = pl.BlockSpec(memory_space=pltpu.SMEM)


def params():
    return pltpu.CompilerParams(vmem_limit_bytes=58 * 2**20, dimension_semantics=("arbitrary",))


def shape(dtype, *dims):
    return jax.ShapeDtypeStruct(dims, dtype)


def shards(
    tokens, image_mask, patch_mask, first_gain, first_shift, attend_weight, attend_bias,
    merge_weight, merge_bias, second_gain, second_shift, up_weight, up_bias, down_weight,
    down_bias, cotangent,
):
    n, seq, d = tokens.shape
    packed = attend_weight.shape[1]
    rows = -(-n // 16) * 16
    group = 2 if n % 2 == 0 else 1
    steps = n // group
    width = group * MAIN
    left = pl.BlockSpec((n, 16, d), lambda i: (0, MAIN // 16, 0))
    vec = jnp.stack(
        [
            v.astype(f32)
            for v in (
                first_gain, first_shift, attend_bias[0], attend_bias[1], merge_bias,
                second_gain, second_shift, down_bias,
            )
        ]
    )
    up_all = lax.all_gather(up_weight, "tensor", axis=1, tiled=True)
    down_all = lax.all_gather(down_weight, "tensor", axis=0, tiled=True)
    up_bias_all = lax.all_gather(up_bias, "tensor", axis=0, tiled=True)[None, :]
    units = up_all.shape[1]

    main = per_step(group, d, MAIN)
    token_in = per_step(group, MAIN, d)
    token_out = per_step(group, seq, d)
    edge = per_step(group, rows, MAIN)
    fi, qkv, probs, edges, invs, lp, lself, att, hid, fil, qkvl, attl, hidl = pl.pallas_call(
        functools.partial(attend_kernel, n, group),
        grid=(steps,),
        in_specs=[token_in, left, whole(n, MAIN), LIVE, whole(8, d), whole(d, packed), whole(d, d)],
        out_specs=[
            main, per_step(group, packed, MAIN), per_step(group, HEADS, MAIN, MAIN), edge, edge, edge,
            per_step(group, rows, 128), main, main,
            whole(rows, d), whole(rows, packed), whole(rows, d), whole(rows, d),
        ],
        out_shape=[
            shape(bf16, n, d, MAIN), shape(bf16, n, packed, MAIN), shape(bf16, n, HEADS, MAIN, MAIN),
            shape(f32, n, rows, MAIN), shape(f32, n, rows, MAIN), shape(f32, n, rows, MAIN),
            shape(f32, n, rows, 128), shape(bf16, n, d, MAIN), shape(f32, n, d, MAIN),
            shape(f32, rows, d), shape(f32, rows, packed), shape(f32, rows, d), shape(f32, rows, d),
        ],
        scratch_shapes=[
            pltpu.VMEM((packed, d + 128), bf16), pltpu.VMEM((d, d + 128), bf16),
            pltpu.VMEM((d + 128, width), bf16), pltpu.VMEM((d + 128, width), bf16),
            pltpu.VMEM((2, d, 128), f32), pltpu.VMEM((group, rows, MAIN), f32),
            pltpu.VMEM((rows, d), f32), pltpu.VMEM((rows, packed), f32), pltpu.VMEM((rows, d), f32),
        ],
        compiler_params=params(),
        name="attend",
    )(tokens, tokens, patch_mask, image_mask, vec, attend_weight, merge_weight)

    output, gh, ga, ghl, gal, up_acc, down_acc, merge_acc, second_sums = pl.pallas_call(
        functools.partial(feed_kernel, n, group),
        grid=(steps,),
        in_specs=[
            main, main, token_in, left, LIVE, whole(8, d), whole(rows, d), whole(rows, d),
            whole(d, units), whole(1, units), whole(units, d),
        ],
        out_specs=[
            token_out, main, main, whole(rows, d), whole(rows, d),
            whole(d + 16, units), whole(d, units), whole(d + 16, d), whole(8, d),
        ],
        out_shape=[
            shape(bf16, n, seq, d), shape(f32, n, d, MAIN), shape(bf16, n, d, MAIN),
            shape(f32, rows, d), shape(f32, rows, d),
            shape(f32, d + 16, units), shape(f32, d, units), shape(f32, d + 16, d), shape(f32, 8, d),
        ],
        scratch_shapes=[
            pltpu.VMEM((units, d + 128), bf16), pltpu.VMEM((d, units), bf16),
            pltpu.VMEM((d + 128, width), bf16), pltpu.VMEM((d + 128, width), bf16),
            pltpu.VMEM((units, width), bf16), pltpu.VMEM((units, width), bf16),
            pltpu.VMEM((d, width), bf16), pltpu.VMEM((3, d, 128), f32), pltpu.VMEM((2, d, 128), f32),
            pltpu.VMEM((rows, d), f32), pltpu.VMEM((rows, d), f32),
        ],
        compiler_params=params(),
        name="feed",
    )(hid, att, cotangent, cotangent, image_mask, vec, hidl, attl, up_all, up_bias_all, down_all)

    feed_sums = lax.psum((up_acc, down_acc, merge_acc, second_sums), ("dp", "tensor"))

    gp, gpl, attend_acc = pl.pallas_call(
        functools.partial(attend_back_kernel, n, group),
        grid=(steps,),
        in_specs=[
            per_step(group, packed, MAIN), per_step(group, HEADS, MAIN, MAIN), edge, edge, edge,
            per_step(group, rows, 128), main, main, main,
            whole(rows, d), whole(rows, packed), whole(rows, d), whole(rows, d), whole(d, d),
        ],
        out_specs=[per_step(group, packed, MAIN), whole(rows, packed), whole(d + 16, packed)],
        out_shape=[shape(bf16, n, packed, MAIN), shape(f32, rows, packed), shape(f32, d + 16, packed)],
        scratch_shapes=[
            pltpu.VMEM((d + 16, width), bf16), pltpu.VMEM((packed, width), bf16),
            pltpu.VMEM((d, width), bf16), pltpu.VMEM((group, rows, MAIN), f32),
            pltpu.VMEM((rows, d), f32), pltpu.VMEM((rows, packed), f32),
        ],
        compiler_params=params(),
        name="attend_back",
    )(qkv, probs, edges, invs, lp, lself, att, ga, fi, fil, qkvl, attl, gal, merge_weight)

    input_grad, first_sums = pl.pallas_call(
        functools.partial(first_back_kernel, n, group),
        grid=(steps,),
        in_specs=[
            token_in, left, per_step(group, packed, MAIN), main, whole(rows, packed), whole(rows, d),
            whole(8, d), whole(d, packed),
        ],
        out_specs=[token_out, whole(8, d)],
        out_shape=[shape(bf16, n, seq, d), shape(f32, 8, d)],
        scratch_shapes=[
            pltpu.VMEM((d, 128), f32), pltpu.VMEM((2, d, 128), f32),
            pltpu.VMEM((rows, d), f32), pltpu.VMEM((rows, d), f32),
        ],
        compiler_params=params(),
        name="first_back",
    )(tokens, tokens, gp, gh, gpl, ghl, vec, attend_weight)

    attend_acc, first_sums = lax.psum((attend_acc, first_sums), ("dp", "tensor"))
    up_acc, down_acc, merge_acc, second_sums = feed_sums
    share = up_weight.shape[1]
    offset = lax.axis_index("tensor") * share
    up_grad = lax.dynamic_slice_in_dim(up_acc, offset, share, 1)
    down_grad = lax.dynamic_slice_in_dim(down_acc, offset, share, 1).T
    return (
        output,
        input_grad,
        first_sums[0],
        first_sums[1],
        attend_acc[:d],
        jnp.stack([attend_acc[d, :d], attend_acc[d, 2 * d :]]),
        merge_acc[:d],
        merge_acc[d],
        second_sums[0],
        second_sums[1],
        up_grad[:d],
        up_grad[d],
        down_grad,
        second_sums[2],
    )


def solution(mesh):
    split = ("dp", "tensor")
    in_specs = (
        P(split, None, None), P(split), P(split, None), P(), P(), P(), P(), P(), P(), P(), P(),
        P(None, "tensor"), P("tensor"), P("tensor", None), P(), P(split, None, None),
    )
    out_specs = (
        P(split, None, None), P(split, None, None), P(), P(), P(), P(), P(), P(), P(), P(),
        P(None, "tensor"), P("tensor"), P("tensor", None), P(),
    )
    return jax.shard_map(shards, mesh=mesh, in_specs=in_specs, out_specs=out_specs, check_vma=False)
```

time: 608 us -> 334 us (0.55); the launches traced: 596 us -> 334 us
  matrix products: 264 us -> 0 us
  Pallas kernels: 0 us -> 139 us
  other arithmetic: 105 us -> 1.18 us
  local copies, waits for them, and re-layouts: 62.6 us -> 15 us
  waiting for transfers between devices: 98.8 us -> 115 us
    dot_general x61 -> x0, matrix products: 264 us -> none  [contract(): return jnp.einsum(form, left, right, preferred_element_type=jnp.float32)]
    pallas_call x0 -> x4, Pallas kernels: none -> 139 us  [the longest x1 45.1 us: shards(): pl.pallas_call(functools.partial(feed_kernel, n, group), grid=(steps,), i...]
    convert_element_type x18 -> x0, other arithmetic: 74.5 us -> none  [the longest x1 53 us: shards(): activated = act_full.astype(jnp.bfloat16)]
    reduce_sum x14 -> x0, other arithmetic: 30.4 us -> none  [the longest x7 8.38 us: attend_block(): row_total = jnp.sum(raised, axis=-1, keepdims=True)]
    reshape x4 -> x0, local copies, waits for them, and re-layouts: 17.3 us -> none  [the longest x1 5.88 us: shards(): key_grad = key_grad.reshape(images, seq_len, features)]
    psum x1, waiting for transfers between devices: 97.4 us -> 113 us  [shards(): lax.psum((attend_acc, first_sums), ('dp', 'tensor'))]
    slice x4 -> x5, local copies, waits for them, and re-layouts: 20.7 us -> 6.29 us  [the longest x1 2.8 us: shards(): attend_acc[:d]]
    unnamed x85 -> x6, local copies, waits for them, and re-layouts: 15.4 us -> 1.74 us
  transfers between devices with their start and end apart: 3 -> 3, of which waited for: 1 -> 1; matrix products, arithmetic and copies ran while one was open for 31% -> 2% of each run, Pallas kernels for 0% -> 16%
where the time goes in v1:
time: 334 us
  Pallas kernels  139 us (42%)
  waiting for transfers between devices  115 us (34%)
  blocking collectives  49.3 us (15%)
  local copies, waits for them, and re-layouts  15 us (4%)
  between operations  13.8 us (4%)
    psum x1, waiting for transfers between devices, shards(): lax.psum((attend_acc, first_sums), ('dp', 'tensor'))  113 us
    pallas_call x1, Pallas kernels, shards(): pl.pallas_call(functools.partial(feed_kernel, n, group), grid=(steps,), i...  45.1 us
    psum x1, blocking collectives, shards(): lax.psum((attend_acc, first_sums), ('dp', 'tensor'))  42.5 us
    pallas_call x1, Pallas kernels, shards(): pl.pallas_call(functools.partial(attend_back_kernel, n, group), grid=(ste...  41.4 us
    pallas_call x1, Pallas kernels, shards(): pl.pallas_call(functools.partial(attend_kernel, n, group), grid=(steps,),...  38.8 us
    pallas_call x1, Pallas kernels, shards(): pl.pallas_call(functools.partial(first_back_kernel, n, group), grid=(step...  14.1 us
    all_gather x1, blocking collectives, shards(): up_bias_all = lax.all_gather(up_bias, 'tensor', axis=0, tiled=True)[None, :]  6.75 us
  transfers between devices with their start and end apart: 3, of which 1 were waited for; matrix products, arithmetic and copies ran while one was open for 2% of the time, Pallas kernels for 16%

profile of v1, /device:TPU:0, one launch (start us, length us, event | category | flops | bytes accessed | tf_op | source)
XLA Modules:
  0.0 333.7 jit_solution(16941747906538912842)
XLA Ops:
  7.2 0.0 all-gather.4.cloned.1.call-start
  7.2 0.7 all-gather.4.cloned.1.call-update
  7.9 0.0 all-gather.6.cloned.1.call-start
  8.0 0.7 all-gather.6.cloned.1.call-update
  8.7 0.0 all-reduce.4.cloned.1.call-start
  8.7 0.7 stack.34
  9.4 0.7 stack.35
  10.1 0.7 stack.36
  10.8 0.7 stack.37
  11.4 0.7 stack.38
  12.1 0.7 stack.39
  12.8 0.7 stack.40
  13.5 0.6 stack.41.vec
  14.1 0.7 reshape.28
  14.8 38.8 %attend.1 = (bf16[14,384,256]{2,1,0:T(8,128)(2,1)}, bf16[14,1152,256]{2,1,0:T(8,128)(2,1)}, bf16[14,6,256,256]{3,2,1,0:T(8,128)(2,1)}, f32[14,16,256]{2,1,0:T(8,...) custom-call(bf16[14,257,384]{2,1,0:T(8,128)(2,1)} %left.3, ...), custom_call_target="tpu_custom_call" | custom-call | tf_op jit(solution)/shard_map/attend/pallas_call | solution.py:490
  53.6 6.8 %all-gather = bf16[4,1,384]{2,1,0:T(2,128)(2,1)} all-gather(bf16[1,1,384]{2,1,0:T(2,128)(2,1)S(1)} %reshape.28), channel_id=1, replica_groups=mesh['dp'=8,'tensor'=4] {'tensor'}, dimensions={0}, use_global_device_ids=true | all-gather | bytes 3840 | tf_op jit(solution)/shard_map/all_gather | solution.py:483
  60.3 0.0 all-gather.4.cloned.1.call-done.upw
  60.3 0.0 all-gather.6.cloned.1.call-done.dnw
  60.3 45.1 %feed.1 = (bf16[14,257,384]{2,1,0:T(8,128)(2,1)}, f32[14,384,256]{2,1,0:T(8,128)}, bf16[14,384,256]{2,1,0:T(8,128)(2,1)}, f32[16,384]{1,0:T(8,128)}, f32[16,384]...) custom-call(f32[14,384,256]{2,1,0:T(8,128)} %get-tuple-element.41.hid, ...), custom_call_target="tpu_custom_call" | custom-call | tf_op jit(solution)/shard_map/feed/pallas_call | solution.py:515
  105.5 41.4 %attend_back.1 = (bf16[14,1152,256]{2,1,0:T(8,128)(2,1)}, f32[16,1152]{1,0:T(8,128)}, f32[400,1152]{1,0:T(8,128)}) custom-call(bf16[14,1152,256]{2,1,0:T(8,128)(2,1)} %get-tuple-element.46.qkv, bf16[14,6,256,256]{3,2,1,0:T(8,128)(2,1)} %get-tuple-element.47.probs, f32[14,16,256]{2,1,0:T(8,128)} %get-tuple-element.48.edge, ...), custom_call_target="tpu_custom_call" | custom-call | tf_op jit(solution)/shard_map/attend_back/pallas_call | solution.py:544
  146.9 0.0 all-reduce.4.cloned.1.call-update
  147.0 0.0 copy-start.1
  147.0 14.1 %first_back.1 = (bf16[14,257,384]{2,1,0:T(8,128)(2,1)}, f32[8,384]{1,0:T(8,128)}) custom-call(bf16[14,257,384]{2,1,0:T(8,128)(2,1)} %left.3, bf16[14,257,384]{2,1,0:T(8,128)(2,1)} %left.3, bf16[14,1152,256]{2,1,0:T(8,128)(2,1)} %get-tuple-element.57.gp, f32[14,384,256]{2,1,0:T(8,128)} %get-tuple-element.58.gh, f32[16,1152]{1,0:T(8,128)} %get-tuple-element.59.gpl, ...), custom_call_target="tpu_custom_call" | custom-call | tf_op jit(solution)/shard_map/first_back/pallas_call | solution.py:563
  161.0 0.0 copy-done.1
  161.0 42.5 %all-reduce = (f32[8,384]{1,0:T(8,128)S(1)}, f32[8,384]{1,0:T(8,128)S(1)}) all-reduce(f32[8,384]{1,0:T(8,128)} %get-tuple-element.62, f32[8,384]{1,0:T(8,128)S(1)} %copy-done.1), channel_id=1, replica_groups=mesh['dp'=8,'tensor'=4] {'dp','tensor'}, use_global_device_ids=true, to_apply=%region_0.0 | all-reduce | flops 6144 | bytes 49152 | tf_op jit(solution)/shard_map/psum | solution.py:580
  203.6 0.6 slice_reduce_fusion
  204.2 113.4 %all-reduce.4.cloned.1.call-done = (f32[400,1152]{1,0:T(8,128)}, f32[400,384]{1,0:T(8,128)}, f32[400,1536]{1,0:T(8,128)}, f32[384,1536]{1,0:T(8,128)}) async-done(((f32[400,1152]{1,0:T(8,128)}, f32[400,384]{1,0:T(8,128)}, f32[400,1536]{1,0:T(8,128)}, f32[384,1536]{1,0:T(8,128)}), (f32[400,1152]{1,0:T(8,128)}, f32[400,384]{1,0:T(8,128)}, f32[400,1536]{1,0:T(8,128)}, ...) | async-done | bytes 7274512 | tf_op jit(solution)/shard_map/psum | solution.py:580
  317.6 0.7 fusion
  318.3 2.8 slice.53
  321.1 0.0 copy-start
  321.1 2.2 dynamic-slice_bitcast_fusion
  323.3 1.0 copy.31
  324.4 0.0 copy-done
  324.4 0.9 slice.56
  325.2 1.3 dynamic-slice_reduce_fusion
  326.5 0.6 pad_maximum_fusion
Async XLA Ops:
  7.2 53.2 %all-gather.4.cloned.1.call-start = ((), (), s32[]{:S(2)}) async-start(), calls=%async_computation | async-start | bytes 1474560 | tf_op jit(solution)/shard_map/all_gather | solution.py:481
  7.9 52.4 %all-gather.6.cloned.1.call-start = ((), (), s32[]{:S(2)}) async-start(), calls=%async_computation.1 | async-start | bytes 1474560 | tf_op jit(solution)/shard_map/all_gather | solution.py:482
  8.7 308.9 %all-reduce.4.cloned.1.call-start = ((), (), s32[]{:S(2)}) async-start(), calls=%async_computation.2 | async-start | bytes 14548992 | tf_op jit(solution)/shard_map/psum | solution.py:580
  147.0 14.1 %copy-start.1 = (f32[8,384]{1,0:T(8,128)S(1)}, f32[8,384]{1,0:T(8,128)}, u32[]{:S(2)}) copy-start(f32[8,384]{1,0:T(8,128)} %get-tuple-element.65) | copy-start | bytes 36868
  321.1 3.3 copy-start
Sparse Core Ops, SparseCore 0:
  9.6 20.1 all-gather.3
  31.3 17.5 all-gather.5
  147.1 170.4 all-reduce.3

commit v2 on v1

--- a/solution.py
+++ b/solution.py
@@ -86,6 +86,163 @@
     to_ref[...] = jnp.zeros_like(to_ref)
     for image in range(count):
         to_ref[image : image + 1, :] = left_ref[image].astype(f32)[0:1, :]
+
+
+class Sums:
+    def __init__(self, mesh_sizes, streams, rows, shared):
+        self.dp, self.tensor = mesh_sizes
+        self.far = self.dp // 2
+        self.streams, self.rows, self.shared = streams, rows, shared
+        self.copies = 2 + 3 + 2 + 2 * (self.far - 1) + 1 + 3
+
+    def scratch(self):
+        s, r, far = self.streams, self.rows, self.far
+        vm = lambda *dims: pltpu.VMEM((s, *dims, 128), bf16)
+        return [
+            vm(2, r), vm(2, r), vm(r // 2), vm(2, r // 4), vm(2, r // 4),
+            vm(r // 2), vm(max(far - 1, 1), r // 2 // far), vm(2, r // 2),
+            vm(4, self.shared[1]),
+            pltpu.SemaphoreType.DMA((s, self.copies)), pltpu.SemaphoreType.DMA((s, self.copies)),
+        ]
+
+    def bind(self, send, refs):
+        self.send = send
+        (self.work, self.r1, self.r2y, self.r2x, self.r3, self.cur, self.r4, self.fin, self.out,
+         self.ss, self.rs) = refs
+        self.me_dp, self.me_t = lax.axis_index("dp"), lax.axis_index("tensor")
+        self.x = lax.rem(self.me_dp, 2)
+        self.z = self.me_dp // 2
+
+    def peer(self, kind, j=1):
+        if kind == "t":
+            t = self.me_t
+            flip0 = t + 1 - 2 * lax.rem(t, 2) if j & 1 else t
+            high = flip0 // 2
+            flipped = flip0 + 2 - 4 * lax.rem(high, 2) if j & 2 else flip0
+            return (self.me_dp, flipped)
+        if kind == "x":
+            return (self.me_dp + 1 - 2 * self.x, self.me_t)
+        return (lax.rem(self.z + j, self.far) * 2 + self.x, self.me_t)
+
+    def peers(self):
+        found = [self.peer("t", j) for j in (1, 2, 3)] + [self.peer("x")]
+        return found + [self.peer("z", j) for j in range(1, self.far)]
+
+    def greet(self):
+        barrier = pltpu.get_barrier_semaphore()
+        for peer in self.peers():
+            pl.semaphore_signal(barrier, inc=1, device_id=peer, device_id_type=pl.DeviceIdType.MESH)
+
+    def meet(self):
+        pl.semaphore_wait(pltpu.get_barrier_semaphore(), len(self.peers()))
+
+    def copy(self, s, index, src, dst, peer):
+        return pltpu.make_async_remote_copy(
+            src_ref=src, dst_ref=dst, send_sem=self.ss.at[s, index], recv_sem=self.rs.at[s, index],
+            device_id=peer, device_id_type=pl.DeviceIdType.MESH,
+        )
+
+    def copies_of(self, phase, s):
+        half, part = self.rows // 2, self.rows // 4
+        chunk = half // self.far
+        t, x, z = self.me_t, self.x, self.z
+        cp = functools.partial(self.copy, s)
+        if phase == 1:
+            core = self.peer("t", 1)
+            return [
+                cp(0, self.send.at[s, core[1]], self.r1.at[s, 0], core),
+                cp(1, self.send.at[s, self.peer("t", 3)[1]], self.r1.at[s, 1], core),
+            ]
+        if phase == 2:
+            other = pl.ds(pl.multiple_of(half + (1 - x) * part, 16), part)
+            return [
+                cp(2, self.work.at[s, 1, pl.ds(0, half)], self.r2y.at[s], self.peer("t", 2)),
+                cp(3, self.work.at[s, 0, other], self.r2x.at[s, 0], self.peer("x")),
+                cp(4, self.work.at[s, 1, other], self.r2x.at[s, 1], self.peer("x")),
+            ]
+        if phase == 3:
+            other = pl.ds(pl.multiple_of((1 - x) * part, 16), part)
+            mine = pl.ds(pl.multiple_of(half + x * part, 16), part)
+            return [
+                cp(5, self.work.at[s, 0, other], self.r3.at[s, 0], self.peer("x")),
+                cp(6, self.work.at[s, 1, mine], self.r3.at[s, 1], self.peer("t", 2)),
+            ]
+        found = []
+        if phase == 4:
+            for j in range(1, self.far):
+                place = lax.rem(z + j, self.far)
+                src = self.cur.at[s, pl.ds(pl.multiple_of(place * chunk, 16), chunk)]
+                found.append(cp(6 + j, src, self.r4.at[s, j - 1], self.peer("z", j)))
+        if phase == 5:
+            mine = pl.ds(pl.multiple_of(z * chunk, 16), chunk)
+            for j in range(1, self.far):
+                ref = self.fin.at[s, x, mine]
+                found.append(cp(5 + self.far + j, ref, ref, self.peer("z", j)))
+        if phase == 6:
+            ref = self.fin.at[s, x]
+            found.append(cp(5 + 2 * self.far, ref, ref, self.peer("x")))
+        if phase == 7:
+            for j in (1, 2, 3):
+                src = self.out.at[s, t]
+                found.append(cp(5 + 2 * self.far + j, src, src, self.peer("t", j)))
+        return found
+
+    def start(self, phase, s):
+        for copy in self.copies_of(phase, s):
+            copy.start()
+
+    def finish(self, phase, s):
+        for copy in self.copies_of(phase, s):
+            copy.wait()
+        half, part = self.rows // 2, self.rows // 4
+        chunk = half // self.far
+        t, x, z = self.me_t, self.x, self.z
+
+        def plus(*parts):
+            total = parts[0].astype(f32)
+            for one in parts[1:]:
+                total = total + one.astype(f32)
+            return total.astype(bf16)
+
+        if phase == 1:
+            self.work[s, 0] = plus(self.send[s, t], self.r1[s, 0])
+            self.work[s, 1] = plus(self.send[s, self.peer("t", 2)[1]], self.r1[s, 1])
+        if phase == 2:
+            self.work[s, 0, :half] = plus(self.work[s, 0, :half], self.r2y[s])
+            mine = pl.ds(pl.multiple_of(half + x * part, 16), part)
+            for q in range(2):
+                self.work[s, q, mine] = plus(self.work[s, q, mine], self.r2x[s, q])
+        if phase == 3:
+            mine = pl.ds(pl.multiple_of(x * part, 16), part)
+            self.cur[s, :part] = plus(self.work[s, 0, mine], self.r3[s, 0])
+            mine = pl.ds(pl.multiple_of(half + x * part, 16), part)
+            self.cur[s, part:] = plus(self.work[s, 0, mine], self.r3[s, 1])
+        if phase == 4:
+            mine = pl.ds(pl.multiple_of(z * chunk, 16), chunk)
+            self.fin[s, x, mine] = plus(
+                self.cur[s, mine], *(self.r4[s, j - 1] for j in range(1, self.far))
+            )
+        if phase == 6:
+            first, count = self.shared
+            first = first - self.rows // 2
+            side, first = first // part, first % part
+            self.out[s, t] = self.fin[s, side, part + first : part + first + count]
+
+    def advance(self, phase, s):
+        self.finish(phase, s)
+        if phase < 7:
+            self.start(phase + 1, s)
+
+    def quarter_rows(self, s, first, count):
+        half, part = self.rows // 2, self.rows // 4
+        pieces, at = [], first
+        while at < first + count:
+            block = at // part
+            end = min(first + count, (block + 1) * part)
+            low = (block // 2) * part + at - block * part
+            pieces.append(self.fin[s, block % 2, low : low + end - at].astype(f32))
+            at = end
+        return pieces[0] if len(pieces) == 1 else jnp.concatenate(pieces, axis=0)
 
 
 def attend_kernel(
@@ -210,8 +367,8 @@
 def feed_kernel(
     count, group,
     hid, att, cot, cleft, live, vec, hidl, attl, upw, upb, dnw,
-    out, gh_out, ga_out, ghl_out, gal_out, up_acc, down_acc, merge_acc, sums_out,
-    upt, dnt, sia, atta, act, gpre, gb, cols, gsum, xl, outl,
+    out, gh_out, ga_out, ghl_out, gal_out, send,
+    upt, dnt, sia, atta, act, gpre, gb, cols, gsum, xl, outl, up_acc, down_acc, merge_acc, sums_out,
 ):
     step = pl.program_id(0)
     features, hidden_units = upw.shape
@@ -298,15 +455,40 @@
     def _():
         sums_out[0:1, :] += jnp.sum(gsum[0].T, axis=0, keepdims=True)
         sums_out[1:2, :] += jnp.sum(gsum[1].T, axis=0, keepdims=True)
+        up_rows, merge_rows = up_acc.shape[0], merge_acc.shape[0]
+        quarter = (merge_rows + 48) // 4
+        used = up_rows + features + quarter
+        shared = jnp.concatenate(
+            [merge_acc[...], sums_out[...], jnp.zeros((40, features), f32)], axis=0
+        ).astype(bf16)
+        for s in range(send.shape[0]):
+            for q in range(4):
+                lanes = slice(q * features + s * 128, q * features + (s + 1) * 128)
+                send[s, q, :up_rows] = up_acc[:, lanes].astype(bf16)
+                send[s, q, up_rows : up_rows + features] = down_acc[:, lanes].astype(bf16)
+                send[s, q, up_rows + features : used] = shared[
+                    q * quarter : (q + 1) * quarter, s * 128 : (s + 1) * 128
+                ]
+                if used < send.shape[2]:
+                    send[s, q, used:] = jnp.zeros((send.shape[2] - used, 128), bf16)
 
 
 def attend_back_kernel(
-    count, group,
-    qkv, probs, edge, inv, lp, lself, att, ga, fi, fil, qkvl, attl, gal, mw,
-    gp_out, gpl_out, acc,
-    fia, gpa, gml, dots, gmleft, gpl,
+    count, group, sums, plan,
+    qkv, probs, edge, inv, lp, lself, att, ga, fi, fil, qkvl, attl, gal, mw, send,
+    gp_out, gpl_out, acc, up_out, down_out, merge_out, rows_out,
+    fia, gpa, gml, dots, gmleft, gpl, *comm,
 ):
     step = pl.program_id(0)
+    sums.bind(send, comm)
+
+    @pl.when(step == 0)
+    def _():
+        sums.greet()
+        sums.meet()
+        for s in range(sums.streams):
+            sums.start(1, s)
+
     features = mw.shape[0]
     rows = gal.shape[0]
     heads = head_rows(rows, features)
@@ -322,6 +504,9 @@
     at16 = lax.broadcasted_iota(jnp.int32, (16, MAIN), 0)
     minus = jnp.where(at16 < 2, -1.0, 0.0).astype(bf16)
     for g in range(group):
+        for slot, phase, s in plan:
+            if slot < count and slot % group == g:
+                pl.when(step == slot // group)(functools.partial(sums.advance, phase, s))
         image = step * group + g
         lanes = slice(g * MAIN, (g + 1) * MAIN)
         qt = qkv[g, :features, :]
@@ -394,6 +579,18 @@
         acc[...] += dot(
             jnp.concatenate([fil[...], one], axis=1).astype(bf16), gpl[...].astype(bf16), TN
         )
+        for slot, phase, s in plan:
+            if slot >= count:
+                sums.advance(phase, s)
+        for s in range(sums.streams):
+            lanes = slice(s * 128, (s + 1) * 128)
+            up_out[:, lanes] = sums.quarter_rows(s, 0, features)
+            rows_out[8:16, lanes] = sums.quarter_rows(s, features, 16)[:8]
+            down_out[lanes, :] = sums.quarter_rows(s, features + 16, features).T
+            shared = jnp.concatenate([sums.out[s, q].astype(f32) for q in range(4)], axis=0)
+            merge_out[:, lanes] = shared[:features]
+            rows_out[16:24, lanes] = shared[features : features + 8]
+            rows_out[:8, lanes] = shared[features + 16 : features + 24]
 
 
 def first_back_kernel(
@@ -458,7 +655,7 @@
 
 
 def shards(
-    tokens, image_mask, patch_mask, first_gain, first_shift, attend_weight, attend_bias,
+    mesh_sizes, tokens, image_mask, patch_mask, first_gain, first_shift, attend_weight, attend_bias,
     merge_weight, merge_bias, second_gain, second_shift, up_weight, up_bias, down_weight,
     down_bias, cotangent,
 ):
@@ -512,7 +709,12 @@
         name="attend",
     )(tokens, tokens, patch_mask, image_mask, vec, attend_weight, merge_weight)
 
-    output, gh, ga, ghl, gal, up_acc, down_acc, merge_acc, second_sums = pl.pallas_call(
+    rows_quarter = d + 16 + d + (d + 64) // 4
+    unit = 16 * mesh_sizes[0]
+    rows_quarter = -(-rows_quarter // unit) * unit
+    sums = Sums(mesh_sizes, d // 128, rows_quarter, (2 * d + 16, (d + 64) // 4))
+    plan = [(1 + s + 2 * (phase - 1), phase, s) for phase in range(1, 8) for s in range(sums.streams)]
+    output, gh, ga, ghl, gal, send = pl.pallas_call(
         functools.partial(feed_kernel, n, group),
         grid=(steps,),
         in_specs=[
@@ -521,12 +723,11 @@
         ],
         out_specs=[
             token_out, main, main, whole(rows, d), whole(rows, d),
-            whole(d + 16, units), whole(d, units), whole(d + 16, d), whole(8, d),
+            whole(sums.streams, 4, rows_quarter, 128),
         ],
         out_shape=[
             shape(bf16, n, seq, d), shape(f32, n, d, MAIN), shape(bf16, n, d, MAIN),
-            shape(f32, rows, d), shape(f32, rows, d),
-            shape(f32, d + 16, units), shape(f32, d, units), shape(f32, d + 16, d), shape(f32, 8, d),
+            shape(f32, rows, d), shape(f32, rows, d), shape(bf16, sums.streams, 4, rows_quarter, 128),
         ],
         scratch_shapes=[
             pltpu.VMEM((units, d + 128), bf16), pltpu.VMEM((d, units), bf16),
@@ -534,31 +735,41 @@
             pltpu.VMEM((units, width), bf16), pltpu.VMEM((units, width), bf16),
             pltpu.VMEM((d, width), bf16), pltpu.VMEM((3, d, 128), f32), pltpu.VMEM((2, d, 128), f32),
             pltpu.VMEM((rows, d), f32), pltpu.VMEM((rows, d), f32),
+            pltpu.VMEM((d + 16, units), f32), pltpu.VMEM((d, units), f32), pltpu.VMEM((d + 16, d), f32),
+            pltpu.VMEM((8, d), f32),
         ],
         compiler_params=params(),
         name="feed",
     )(hid, att, cotangent, cotangent, image_mask, vec, hidl, attl, up_all, up_bias_all, down_all)
 
-    feed_sums = lax.psum((up_acc, down_acc, merge_acc, second_sums), ("dp", "tensor"))
-
-    gp, gpl, attend_acc = pl.pallas_call(
-        functools.partial(attend_back_kernel, n, group),
+    gp, gpl, attend_acc, up_grad, down_grad, merge_grad, row_grads = pl.pallas_call(
+        functools.partial(attend_back_kernel, n, group, sums, plan),
         grid=(steps,),
         in_specs=[
             per_step(group, packed, MAIN), per_step(group, HEADS, MAIN, MAIN), edge, edge, edge,
             per_step(group, rows, 128), main, main, main,
             whole(rows, d), whole(rows, packed), whole(rows, d), whole(rows, d), whole(d, d),
-        ],
-        out_specs=[per_step(group, packed, MAIN), whole(rows, packed), whole(d + 16, packed)],
-        out_shape=[shape(bf16, n, packed, MAIN), shape(f32, rows, packed), shape(f32, d + 16, packed)],
+            whole(sums.streams, 4, rows_quarter, 128),
+        ],
+        out_specs=[
+            per_step(group, packed, MAIN), whole(rows, packed), whole(d + 16, packed),
+            whole(d, d), whole(d, d), whole(d, d), whole(24, d),
+        ],
+        out_shape=[
+            shape(bf16, n, packed, MAIN), shape(f32, rows, packed), shape(f32, d + 16, packed),
+            shape(f32, d, d), shape(f32, d, d), shape(f32, d, d), shape(f32, 24, d),
+        ],
         scratch_shapes=[
             pltpu.VMEM((d + 16, width), bf16), pltpu.VMEM((packed, width), bf16),
             pltpu.VMEM((d, width), bf16), pltpu.VMEM((group, rows, MAIN), f32),
-            pltpu.VMEM((rows, d), f32), pltpu.VMEM((rows, packed), f32),
-        ],
-        compiler_params=params(),
+            pltpu.VMEM((rows, d), f32), pltpu.VMEM((rows, packed), f32), *sums.scratch(),
+        ],
+        compiler_params=pltpu.CompilerParams(
+            vmem_limit_bytes=58 * 2**20, dimension_semantics=("arbitrary",), collective_id=0,
+            has_side_effects=True,
+        ),
         name="attend_back",
-    )(qkv, probs, edges, invs, lp, lself, att, ga, fi, fil, qkvl, attl, gal, merge_weight)
+    )(qkv, probs, edges, invs, lp, lself, att, ga, fi, fil, qkvl, attl, gal, merge_weight, send)
 
     input_grad, first_sums = pl.pallas_call(
         functools.partial(first_back_kernel, n, group),
@@ -578,11 +789,6 @@
     )(tokens, tokens, gp, gh, gpl, ghl, vec, attend_weight)
 
     attend_acc, first_sums = lax.psum((attend_acc, first_sums), ("dp", "tensor"))
-    up_acc, down_acc, merge_acc, second_sums = feed_sums
-    share = up_weight.shape[1]
-    offset = lax.axis_index("tensor") * share
-    up_grad = lax.dynamic_slice_in_dim(up_acc, offset, share, 1)
-    down_grad = lax.dynamic_slice_in_dim(down_acc, offset, share, 1).T
     return (
         output,
         input_grad,
@@ -590,14 +796,14 @@
         first_sums[1],
         attend_acc[:d],
         jnp.stack([attend_acc[d, :d], attend_acc[d, 2 * d :]]),
-        merge_acc[:d],
-        merge_acc[d],
-        second_sums[0],
-        second_sums[1],
-        up_grad[:d],
-        up_grad[d],
+        merge_grad,
+        row_grads[16],
+        row_grads[0],
+        row_grads[1],
+        up_grad,
+        row_grads[8],
         down_grad,
-        second_sums[2],
+        row_grads[2],
     )
 
 
@@ -611,4 +817,5 @@
         P(split, None, None), P(split, None, None), P(), P(), P(), P(), P(), P(), P(), P(),
         P(None, "tensor"), P("tensor"), P("tensor", None), P(),
     )
-    return jax.shard_map(shards, mesh=mesh, in_specs=in_specs, out_specs=out_specs, check_vma=False)
+    sizes = (mesh.shape["dp"], mesh.shape["tensor"])
+    return jax.shard_map(functools.partial(shards, sizes), mesh=mesh, in_specs=in_specs, out_specs=out_specs, check_vma=False)

time: 334 us -> 306 us (0.916)
  waiting for transfers between devices: 115 us -> 79 us
  Pallas kernels: 139 us -> 151 us
    psum x1, waiting for transfers between devices: 113 us -> 77.6 us  [shards(): lax.psum((attend_acc, first_sums), ('dp', 'tensor'))]
    pallas_call x1, Pallas kernels: 41.4 us -> 54.3 us  [shards(): pl.pallas_call(functools.partial(attend_back_kernel, n, group, sums, plan...]
  transfers between devices with their start and end apart: 3 -> 3, of which waited for: 1 -> 1; matrix products, arithmetic and copies ran while one was open for 2% -> 3% of each run, Pallas kernels for 16% -> 17%
where the time goes in v2:
time: 306 us
  Pallas kernels  151 us (49%)
  waiting for transfers between devices  79 us (26%)
  blocking collectives  46.7 us (15%)
  between operations  13.8 us (5%)
  local copies, waits for them, and re-layouts  13.6 us (4%)
    psum x1, waiting for transfers between devices, shards(): lax.psum((attend_acc, first_sums), ('dp', 'tensor'))  77.6 us
    pallas_call x1, Pallas kernels, shards(): pl.pallas_call(functools.partial(attend_back_kernel, n, group, sums, plan...  54.3 us
    pallas_call x1, Pallas kernels, shards(): pl.pallas_call(functools.partial(feed_kernel, n, group), grid=(steps,), i...  44.9 us
    psum x1, blocking collectives, shards(): lax.psum((attend_acc, first_sums), ('dp', 'tensor'))  40 us
    pallas_call x1, Pallas kernels, shards(): pl.pallas_call(functools.partial(attend_kernel, n, group), grid=(steps,),...  38.8 us
    pallas_call x1, Pallas kernels, shards(): pl.pallas_call(functools.partial(first_back_kernel, n, group), grid=(step...  13.3 us
    all_gather x1, blocking collectives, shards(): up_bias_all = lax.all_gather(up_bias, 'tensor', axis=0, tiled=True)[None, :]  6.73 us
  transfers between devices with their start and end apart: 3, of which 1 were waited for; matrix products, arithmetic and copies ran while one was open for 3% of the time, Pallas kernels for 17%

profile of v2, /device:TPU:0, one launch (start us, length us, event | category | flops | bytes accessed | tf_op | source)
XLA Modules:
  0.0 305.6 jit_solution(4154116637450069811)
XLA Ops:
  7.2 0.0 all-gather.4.cloned.1.call-start
  7.2 0.7 all-gather.4.cloned.1.call-update
  7.9 0.0 all-gather.6.cloned.1.call-start
  8.0 0.7 all-gather.6.cloned.1.call-update
  8.7 0.0 all-reduce.2.cloned.1.call-start
  8.7 0.7 stack.34
  9.4 0.7 stack.35
  10.1 0.7 stack.36
  10.8 0.7 stack.37
  11.4 0.7 stack.38
  12.1 0.7 reshape.28
  12.8 0.7 stack.39
  13.5 0.7 stack.40
  14.2 0.6 stack.41.vec
  14.8 38.8 %attend.1 = (bf16[14,384,256]{2,1,0:T(8,128)(2,1)}, bf16[14,1152,256]{2,1,0:T(8,128)(2,1)}, bf16[14,6,256,256]{3,2,1,0:T(8,128)(2,1)}, f32[14,16,256]{2,1,0:T(8,...) custom-call(bf16[14,257,384]{2,1,0:T(8,128)(2,1)} %left.3, ...), custom_call_target="tpu_custom_call" | custom-call | tf_op jit(solution)/shard_map/attend/pallas_call | solution.py:687
  53.6 6.7 %all-gather = bf16[4,1,384]{2,1,0:T(2,128)(2,1)} all-gather(bf16[1,1,384]{2,1,0:T(2,128)(2,1)S(1)} %reshape.28), channel_id=1, replica_groups=mesh['dp'=8,'tensor'=4] {'tensor'}, dimensions={0}, use_global_device_ids=true | all-gather | bytes 3840 | tf_op jit(solution)/shard_map/all_gather | solution.py:680
  60.3 0.0 all-gather.4.cloned.1.call-done.upw
  60.3 0.0 all-gather.6.cloned.1.call-done.dnw
  60.3 44.9 %feed.1 = (bf16[14,257,384]{2,1,0:T(8,128)(2,1)}, f32[14,384,256]{2,1,0:T(8,128)}, bf16[14,384,256]{2,1,0:T(8,128)(2,1)}, f32[16,384]{1,0:T(8,128)}, f32[16,384]...) custom-call(f32[14,384,256]{2,1,0:T(8,128)} %get-tuple-element.42.hid, bf16[14,384,256]{2,1,0:T(8,128)(2,1)} %get-tuple-element.43.att, ...), custom_call_target="tpu_custom_call" | custom-call | tf_op jit(solution)/shard_map/feed/pallas_call | solution.py:717
  105.2 54.3 %attend_back.1 = (bf16[14,1152,256]{2,1,0:T(8,128)(2,1)}, f32[16,1152]{1,0:T(8,128)}, f32[400,1152]{1,0:T(8,128)}, f32[384,384]{1,0:T(8,128)}, f32[384,384]{1,0:...) custom-call(bf16[14,1152,256]{2,1,0:T(8,128)(2,1)} %get-tuple-element.47.qkv, ...), custom_call_target="tpu_custom_call" | custom-call | tf_op jit(solution)/shard_map/attend_back/pallas_call | solution.py:745
  159.5 0.0 all-reduce.2.cloned.1.call-update
  159.6 13.3 %first_back.1 = (bf16[14,257,384]{2,1,0:T(8,128)(2,1)}, f32[8,384]{1,0:T(8,128)}) custom-call(bf16[14,257,384]{2,1,0:T(8,128)(2,1)} %left.3, bf16[14,257,384]{2,1,0:T(8,128)(2,1)} %left.3, bf16[14,1152,256]{2,1,0:T(8,128)(2,1)} %get-tuple-element.59.gp, f32[14,384,256]{2,1,0:T(8,128)} %get-tuple-element.60.gh, f32[16,1152]{1,0:T(8,128)} %get-tuple-element.61.gpl, ...), custom_call_target="tpu_custom_call" | custom-call | tf_op jit(solution)/shard_map/first_back/pallas_call | solution.py:774
  172.8 0.0 copy-start.2
  172.8 0.0 copy-start.1
  172.8 40.0 %psum.14 = f32[8,384]{1,0:T(8,128)S(1)} all-reduce(f32[8,384]{1,0:T(8,128)} %get-tuple-element.64), channel_id=1, replica_groups=mesh['dp'=8,'tensor'=4] {'dp','tensor'}, use_global_device_ids=true, to_apply=%region_0.0 | all-reduce | flops 3072 | bytes 24576 | tf_op jit(solution)/shard_map/psum | solution.py:791
  212.8 0.6 slice_reduce_fusion
  213.4 1.4 slice_reduce_fusion.2
  214.9 77.6 %all-reduce.2.cloned.1.call-done = f32[400,1152]{1,0:T(8,128)} async-done(((f32[400,1152]{1,0:T(8,128)}), f32[400,1152]{1,0:T(8,128)}) %all-reduce.2.cloned.1.call-update) | async-done | bytes 1843216 | tf_op jit(solution)/shard_map/psum | solution.py:791
  292.4 0.7 fusion
  293.2 0.6 pad_maximum_fusion
  293.7 0.0 copy-start
  293.7 2.9 slice.45
  296.6 0.0 copy-done.2
  296.6 0.8 copy.34
  297.4 0.0 copy-done.1
  297.4 0.8 copy.35
  298.2 0.0 copy-done
  298.2 0.8 copy.36
Async XLA Ops:
  7.2 53.1 %all-gather.4.cloned.1.call-start = ((), (), s32[]{:S(2)}) async-start(), calls=%async_computation | async-start | bytes 1474560 | tf_op jit(solution)/shard_map/all_gather | solution.py:678
  7.9 52.4 %all-gather.6.cloned.1.call-start = ((), (), s32[]{:S(2)}) async-start(), calls=%async_computation.1 | async-start | bytes 1474560 | tf_op jit(solution)/shard_map/all_gather | solution.py:679
  8.7 283.8 %all-reduce.2.cloned.1.call-start = ((), (), s32[]{:S(2)}) async-start(), calls=%async_computation.2 | async-start | bytes 3686400 | tf_op jit(solution)/shard_map/psum | solution.py:791
  172.8 123.8 %copy-start.2 = (f32[384,384]{1,0:T(8,128)S(1)}, f32[384,384]{1,0:T(8,128)}, u32[]{:S(2)}) copy-start(f32[384,384]{1,0:T(8,128)} %get-tuple-element.99) | copy-start | bytes 1769476
  172.8 124.6 %copy-start.1 = (f32[384,384]{1,0:T(8,128)S(1)}, f32[384,384]{1,0:T(8,128)}, u32[]{:S(2)}) copy-start(f32[384,384]{1,0:T(8,128)} %get-tuple-element.103) | copy-start | bytes 1769476
  293.7 4.5 %copy-start = (f32[384,384]{1,0:T(8,128)S(1)}, f32[384,384]{1,0:T(8,128)}, u32[]{:S(2)}) copy-start(f32[384,384]{1,0:T(8,128)} %get-tuple-element.105) | copy-start | bytes 1769476
Sparse Core Ops, SparseCore 0:
  9.6 20.1 all-gather.3
  31.3 17.4 all-gather.5
  159.7 132.7 all-reduce.1

commit v3 on v2

v3 whole, which is shorter than its diff:
```python
import functools

import jax
import jax.numpy as jnp
from jax import lax
from jax.experimental import pallas as pl
from jax.experimental.pallas import tpu as pltpu
from jax.sharding import PartitionSpec as P

HEADS = 6
HEAD = 64
MAIN = 256
EPS = 1e-06
MASKED = -1e30
f32, bf16 = jnp.float32, jnp.bfloat16

NN = ((1,), (0,))
NT = ((1,), (1,))
TN = ((0,), (0,))


def dot(left, right, dims=NN):
    return lax.dot_general(left, right, (dims, ((), ())), preferred_element_type=f32)


def rows_where(index, value, rows, dtype):
    columns = value.shape[-1]
    at = lax.broadcasted_iota(jnp.int32, (rows, columns), 0)
    return jnp.where(at == index, value, 0.0).astype(dtype)


def wide(column, width):
    return jnp.concatenate([column] * (width // 128), axis=1)


def as_column(row):
    return jnp.broadcast_to(row, (128, row.shape[1])).T


def norm_columns(values):
    center = values - jnp.mean(values, axis=0, keepdims=True)
    scale = lax.rsqrt(jnp.mean(center * center, axis=0, keepdims=True) + EPS)
    return center * scale, scale


def norm_rows(values):
    center = values - jnp.mean(values, axis=1, keepdims=True)
    scale = lax.rsqrt(jnp.mean(center * center, axis=1, keepdims=True) + EPS)
    return center * scale, scale


def norm_back(grad, normed, scale, axis):
    mean_grad = jnp.mean(grad, axis=axis, keepdims=True)
    mean_both = jnp.mean(grad * normed, axis=axis, keepdims=True)
    return scale * (grad - mean_grad - normed * mean_both)


def gelu_both(pre):
    curve = 0.5 + 0.5 * lax.erf(pre * 0.7071067811865476)
    bell = 0.3989422804014327 * jnp.exp(-0.5 * pre * pre)
    return pre * curve, curve + pre * bell


def head_rows(rows, features):
    at = lax.broadcasted_iota(jnp.int32, (rows, features), 0)
    head = lax.broadcasted_iota(jnp.int32, (rows, features), 1) // HEAD
    return jnp.where(at == head, 1.0, 0.0)


def lane_live(live_ref, first, count):
    flags = [
        jnp.full((1, MAIN), live_ref[first + g].astype(f32)) for g in range(count)
    ]
    return jnp.concatenate(flags, axis=1)


def row_live(live_ref, count, rows):
    at = lax.broadcasted_iota(jnp.int32, (rows, 1), 0)
    flags = jnp.zeros((rows, 1), f32)
    for image in range(count):
        flags = jnp.where(at == image, live_ref[image].astype(f32), flags)
    return flags


def take_left(left_ref, to_ref, count):
    to_ref[...] = jnp.zeros_like(to_ref)
    for image in range(count):
        to_ref[image : image + 1, :] = left_ref[image].astype(f32)[0:1, :]


class Sums:
    def __init__(self, mesh_sizes, streams, rows, shared):
        self.dp, self.tensor = mesh_sizes
        self.far = self.dp // 2
        self.streams, self.rows, self.shared = streams, rows, shared
        self.copies = 2 + 3 + 2 + 2 * (self.far - 1) + 1 + 3

    def scratch(self):
        s, r, far = self.streams, self.rows, self.far
        vm = lambda *dims: pltpu.VMEM((s, *dims, 128), bf16)
        return [
            vm(2, r), vm(2, r), vm(r // 2), vm(2, r // 4), vm(2, r // 4),
            vm(r // 2), vm(max(far - 1, 1), r // 2 // far), vm(2, r // 2),
            vm(4, self.shared[1]),
            pltpu.SemaphoreType.DMA((s, self.copies)), pltpu.SemaphoreType.DMA((s, self.copies)),
        ]

    def bind(self, send, refs):
        self.send = send
        (self.work, self.r1, self.r2y, self.r2x, self.r3, self.cur, self.r4, self.fin, self.out,
         self.ss, self.rs) = refs
        self.me_dp, self.me_t = lax.axis_index("dp"), lax.axis_index("tensor")
        self.x = lax.rem(self.me_dp, 2)
        self.z = self.me_dp // 2

    def peer(self, kind, j=1):
        if kind == "t":
            t = self.me_t
            flip0 = t + 1 - 2 * lax.rem(t, 2) if j & 1 else t
            high = flip0 // 2
            flipped = flip0 + 2 - 4 * lax.rem(high, 2) if j & 2 else flip0
            return (self.me_dp, flipped)
        if kind == "x":
            return (self.me_dp + 1 - 2 * self.x, self.me_t)
        return (lax.rem(self.z + j, self.far) * 2 + self.x, self.me_t)

    def peers(self):
        found = [self.peer("t", j) for j in (1, 2, 3)] + [self.peer("x")]
        return found + [self.peer("z", j) for j in range(1, self.far)]

    def greet(self):
        barrier = pltpu.get_barrier_semaphore()
        for peer in self.peers():
            pl.semaphore_signal(barrier, inc=1, device_id=peer, device_id_type=pl.DeviceIdType.MESH)

    def meet(self):
        pl.semaphore_wait(pltpu.get_barrier_semaphore(), len(self.peers()))

    def copy(self, s, index, src, dst, peer):
        return pltpu.make_async_remote_copy(
            src_ref=src, dst_ref=dst, send_sem=self.ss.at[s, index], recv_sem=self.rs.at[s, index],
            device_id=peer, device_id_type=pl.DeviceIdType.MESH,
        )

    def copies_of(self, phase, s):
        half, part = self.rows // 2, self.rows // 4
        chunk = half // self.far
        t, x, z = self.me_t, self.x, self.z
        cp = functools.partial(self.copy, s)
        if phase == 1:
            core = self.peer("t", 1)
            return [
                cp(0, self.send.at[s, core[1]], self.r1.at[s, 0], core),
                cp(1, self.send.at[s, self.peer("t", 3)[1]], self.r1.at[s, 1], core),
            ]
        if phase == 2:
            other = pl.ds(pl.multiple_of(half + (1 - x) * part, 16), part)
            return [
                cp(2, self.work.at[s, 1, pl.ds(0, half)], self.r2y.at[s], self.peer("t", 2)),
                cp(3, self.work.at[s, 0, other], self.r2x.at[s, 0], self.peer("x")),
                cp(4, self.work.at[s, 1, other], self.r2x.at[s, 1], self.peer("x")),
            ]
        if phase == 3:
            other = pl.ds(pl.multiple_of((1 - x) * part, 16), part)
            mine = pl.ds(pl.multiple_of(half + x * part, 16), part)
            return [
                cp(5, self.work.at[s, 0, other], self.r3.at[s, 0], self.peer("x")),
                cp(6, self.work.at[s, 1, mine], self.r3.at[s, 1], self.peer("t", 2)),
            ]
        found = []
        if phase == 4:
            for j in range(1, self.far):
                place = lax.rem(z + j, self.far)
                src = self.cur.at[s, pl.ds(pl.multiple_of(place * chunk, 16), chunk)]
                found.append(cp(6 + j, src, self.r4.at[s, j - 1], self.peer("z", j)))
        if phase == 5:
            mine = pl.ds(pl.multiple_of(z * chunk, 16), chunk)
            for j in range(1, self.far):
                ref = self.fin.at[s, x, mine]
                found.append(cp(5 + self.far + j, ref, ref, self.peer("z", j)))
        if phase == 6:
            ref = self.fin.at[s, x]
            found.append(cp(5 + 2 * self.far, ref, ref, self.peer("x")))
        if phase == 7:
            for j in (1, 2, 3):
                src = self.out.at[s, t]
                found.append(cp(5 + 2 * self.far + j, src, src, self.peer("t", j)))
        return found

    def start(self, phase, s):
        for copy in self.copies_of(phase, s):
            copy.start()

    def finish(self, phase, s):
        for copy in self.copies_of(phase, s):
            copy.wait()
        half, part = self.rows // 2, self.rows // 4
        chunk = half // self.far
        t, x, z = self.me_t, self.x, self.z

        def plus(*parts):
            total = parts[0].astype(f32)
            for one in parts[1:]:
                total = total + one.astype(f32)
            return total.astype(bf16)

        if phase == 1:
            self.work[s, 0] = plus(self.send[s, t], self.r1[s, 0])
            self.work[s, 1] = plus(self.send[s, self.peer("t", 2)[1]], self.r1[s, 1])
        if phase == 2:
            self.work[s, 0, :half] = plus(self.work[s, 0, :half], self.r2y[s])
            mine = pl.ds(pl.multiple_of(half + x * part, 16), part)
            for q in range(2):
                self.work[s, q, mine] = plus(self.work[s, q, mine], self.r2x[s, q])
        if phase == 3:
            mine = pl.ds(pl.multiple_of(x * part, 16), part)
            self.cur[s, :part] = plus(self.work[s, 0, mine], self.r3[s, 0])
            mine = pl.ds(pl.multiple_of(half + x * part, 16), part)
            self.cur[s, part:] = plus(self.work[s, 0, mine], self.r3[s, 1])
        if phase == 4:
            mine = pl.ds(pl.multiple_of(z * chunk, 16), chunk)
            self.fin[s, x, mine] = plus(
                self.cur[s, mine], *(self.r4[s, j - 1] for j in range(1, self.far))
            )
        if phase == 6:
            first, count = self.shared
            first = first - self.rows // 2
            side, first = first // part, first % part
            self.out[s, t] = self.fin[s, side, part + first : part + first + count]

    def advance(self, phase, s):
        self.finish(phase, s)
        if phase < 7:
            self.start(phase + 1, s)

    def quarter_rows(self, s, first, count):
        half, part = self.rows // 2, self.rows // 4
        pieces, at = [], first
        while at < first + count:
            block = at // part
            end = min(first + count, (block + 1) * part)
            low = (block // 2) * part + at - block * part
            pieces.append(self.fin[s, block % 2, low : low + end - at].astype(f32))
            at = end
        return pieces[0] if len(pieces) == 1 else jnp.concatenate(pieces, axis=0)


class Spread:
    def __init__(self, mesh_sizes, streams, chunk):
        self.dp, self.tensor = mesh_sizes
        self.far = self.dp // 2
        self.streams, self.chunk = streams, chunk
        self.copies = 1 + 3 + (self.far - 1) + 3 + 1

    def scratch(self):
        s, c = self.streams, self.chunk
        vm = lambda *dims: pltpu.VMEM((s, *dims, 128), bf16)
        return [
            vm(8 * c), vm(4 * c), vm(4 * c), vm(3, c), vm(self.far, c), vm(8 * c),
            pltpu.SemaphoreType.DMA((s, self.copies)), pltpu.SemaphoreType.DMA((s, self.copies)),
        ]

    def bind(self, refs):
        self.send, self.r1, self.work, self.r2, self.r3, self.out, self.ss, self.rs = refs
        self.me_dp, self.me_t = lax.axis_index("dp"), lax.axis_index("tensor")
        self.x, self.z = lax.rem(self.me_dp, 2), self.me_dp // 2
        self.c, self.y = lax.rem(self.me_t, 2), self.me_t // 2
        self.place = 2 * self.y + self.x

    def plane(self, j):
        x = 1 - self.x if j & 1 else self.x
        y = 1 - self.y if j & 2 else self.y
        return (self.z * 2 + x, 2 * y + self.c), 2 * y + x

    def core(self):
        return (self.me_dp, 2 * self.y + 1 - self.c)

    def line(self, j):
        return (lax.rem(self.z + j, self.far) * 2 + self.x, self.me_t)

    def rows(self, first, count):
        return pl.ds(pl.multiple_of(first * self.chunk, 16), count * self.chunk)

    def copies_of(self, phase, s):
        def cp(index, src, dst, peer):
            return pltpu.make_async_remote_copy(
                src_ref=src, dst_ref=dst, send_sem=self.ss.at[s, index], recv_sem=self.rs.at[s, index],
                device_id=peer, device_id_type=pl.DeviceIdType.MESH,
            )

        if phase == 1:
            return [cp(0, self.send.at[s, self.rows(4 * (1 - self.c), 4)], self.r1.at[s], self.core())]
        found = []
        if phase == 2:
            for j in (1, 2, 3):
                peer, place = self.plane(j)
                found.append(cp(j, self.work.at[s, self.rows(place, 1)], self.r2.at[s, j - 1], peer))
        if phase == 3:
            for j in range(1, self.far):
                ref = self.r3.at[s, self.z]
                found.append(cp(3 + j, ref, ref, self.line(j)))
        mine = self.out.at[s, self.rows(4 * self.c + self.place, 1)]
        if phase == 4:
            for j in (1, 2, 3):
                found.append(cp(2 + self.far + j, mine, mine, self.plane(j)[0]))
        if phase == 5:
            ref = self.out.at[s, self.rows(4 * self.c, 4)]
            found.append(cp(6 + self.far, ref, ref, self.core()))
        return found

    def start(self, phase, s):
        for copy in self.copies_of(phase, s):
            copy.start()

    def advance(self, phase, s):
        for copy in self.copies_of(phase, s):
            copy.wait()
        if phase == 1:
            half = self.send[s, self.rows(4 * self.c, 4)].astype(f32)
            self.work[s] = (half + self.r1[s].astype(f32)).astype(bf16)
        if phase == 2:
            total = self.work[s, self.rows(self.place, 1)].astype(f32)
            for j in range(3):
                total = total + self.r2[s, j].astype(f32)
            self.r3[s, self.z] = total.astype(bf16)
        if phase == 3:
            total = self.r3[s, 0].astype(f32)
            for j in range(1, self.far):
                total = total + self.r3[s, j].astype(f32)
            self.out[s, self.rows(4 * self.c + self.place, 1)] = total.astype(bf16)
        if phase < 5:
            self.start(phase + 1, s)


def row_of(ref):
    return ref[...].astype(f32).reshape(1, ref.shape[0])


def parts_of(at, pair):
    return slice(pair * 384 + at * 128, pair * 384 + (at + 1) * 128)


def attend_kernel(
    count, group, steps,
    tok0, tok, left, pmask, live, gain, shift, abias, mbias, aw, mw,
    fi_out, qkv_out, probs_out, edge_out, inv_out, lp_out, lself_out, att_out, hid_out,
    fil_out, qkvl_out, attl_out, hidl_out,
    awt, mwt, fia, atta, cols, peaks, edges, qkv2, toks, xl, qkvl, attl,
):
    step = pl.program_id(0)
    features = aw.shape[0]
    packed = aw.shape[1]
    rows = xl.shape[0]
    width = group * MAIN
    pairs = HEADS // 2
    heads = head_rows(rows, features)

    def first_norm(block):
        tokens = jnp.concatenate([block[g].T for g in range(group)], axis=1)
        normed, _ = norm_columns(tokens.astype(f32))
        return tokens, (normed * wide(cols[0], width) + wide(cols[1], width)).astype(bf16)

    def project(slot, part):
        span = slice(part * features, (part + 1) * features)
        qkv2[slot, span, :] = dot(awt[span, :], fia[...]).astype(bf16)

    @pl.when(step == 0)
    def _():
        ab = abias[...].astype(f32)
        for pair in range(pairs):
            for at in range(3):
                cut = slice(at * features + pair * 128, at * features + (pair + 1) * 128)
                to = parts_of(at, pair)
                scale = HEAD**-0.5 if at == 0 else 1.0
                awt[to, :features] = (aw[:, cut].astype(f32).T * scale).astype(bf16)
                if at == 1:
                    bias = jnp.zeros((1, 128), f32)
                else:
                    bias = ab[at // 2 : at // 2 + 1, pair * 128 : (pair + 1) * 128] * scale
                awt[to, features:] = rows_where(0, bias, 128, f32).T.astype(bf16)
        mwt[:, :features] = mw[...].astype(f32).T.astype(bf16)
        mwt[:, features:] = rows_where(0, row_of(mbias), 128, f32).T.astype(bf16)
        ones = rows_where(0, jnp.ones((1, fia.shape[1]), f32), 128, bf16)
        fia[features:, :] = ones
        atta[features:, :] = ones
        cols[0] = as_column(row_of(gain))
        cols[1] = as_column(row_of(shift))
        peaks[...] = jnp.zeros_like(peaks)
        edges[...] = jnp.zeros_like(edges)
        take_left(left, xl, count)
        normed, _ = norm_rows(xl[...])
        fil = (normed * row_of(gain) + row_of(shift)).astype(bf16)
        fil_out[...] = fil.astype(f32)
        plain = dot(fil, aw[...])
        for pair in range(pairs):
            for at in range(3):
                cut = slice(at * features + pair * 128, at * features + (pair + 1) * 128)
                value = plain[:, cut]
                if at != 1:
                    value = value + ab[at // 2 : at // 2 + 1, pair * 128 : (pair + 1) * 128]
                value = value.astype(bf16).astype(f32)
                qkvl[:, parts_of(at, pair)] = value * (HEAD**-0.5) if at == 0 else value
        qkvl_out[...] = qkvl[...]
        attl[...] = jnp.zeros_like(attl)
        tokens, fi = first_norm(tok0)
        toks[0] = tokens
        fia[:features, :] = fi
        for part in range(3):
            project(0, part)

    def merge_branch():
        return dot(mwt[...], atta[...])

    def hidden_of(branch, index):
        tokens = toks[lax.rem(index, 3)].astype(f32)
        return tokens + lane_live(live, index * group, group) * branch

    @pl.when(step < steps)
    def _():
        edge_out[...] = jnp.zeros_like(edge_out)
        lp_out[...] = jnp.zeros_like(lp_out)
        lself_out[...] = jnp.zeros_like(lself_out)
        now, later = lax.rem(step, 2), lax.rem(step + 1, 2)
        one_row = rows_where(0, jnp.ones((1, MAIN), f32), 16, bf16)
        held = {}
        units = [(g, h) for g in range(group) for h in range(HEADS)]

        def lanes_of(g):
            return slice(g * MAIN, (g + 1) * MAIN)

        def part(at, g, h):
            low = (h // 2) * 384 + at * 128 + (h % 2) * HEAD
            return qkv2[now, low : low + HEAD, lanes_of(g)]

        def all_heads(at, g):
            return jnp.concatenate(
                [qkv2[now, parts_of(at, pair), lanes_of(g)] for pair in range(pairs)], axis=0
            )

        def begin(g):
            image = step * group + g
            row = qkvl[pl.ds(image, 1), :]
            ql, kl, vl = (
                jnp.concatenate([row[:, parts_of(at, pair)] for pair in range(pairs)], axis=1)
                for at in range(3)
            )
            key_bias = jnp.where(pmask[pl.ds(image, 1), :] == 1, 0.0, MASKED)
            moved = pltpu.roll(key_bias, 1, axis=1)
            at = lax.broadcasted_iota(jnp.int32, moved.shape, 1)
            main_bias = jnp.where(at == 0, 0.0, moved)
            left_bias = moved[:, 0:1]
            held["bias", g] = rows_where(0, main_bias, 16, bf16)
            held["vl", g] = vl
            held["slk", g] = dot((heads * kl).astype(bf16), all_heads(0, g)) + left_bias
            held["sl", g] = dot((heads * ql).astype(bf16), all_heads(1, g)) + main_bias
            held["self", g] = jnp.sum(heads * (ql * kl), axis=1, keepdims=True) + left_bias

        def left_query(g):
            sl, self_score = held.pop(("sl", g)), held.pop(("self", g))
            peak = jnp.maximum(jnp.max(sl, axis=1, keepdims=True), self_score)
            raised = jnp.exp(sl - peak)
            raised_self = jnp.exp(self_score - peak)
            inv = 1.0 / (jnp.sum(raised, axis=1, keepdims=True) + raised_self)
            lp = raised * inv
            lself = raised_self * inv
            for pair in range(pairs):
                lp_out[g, pair, 0:2, :] = lp[2 * pair : 2 * pair + 2, :]
                lself_out[g, pair, 0:2, :] = jnp.broadcast_to(lself[2 * pair : 2 * pair + 2, :], (2, 128))
            mixed = dot(lp.astype(bf16), all_heads(2, g), NT) + lself * held["vl", g]
            image = step * group + g
            attl[pl.ds(image, 1), :] = (
                jnp.sum(mixed * heads, axis=0, keepdims=True).astype(bf16).astype(f32)
            )

        def scores(g, h):
            held["s", g, h] = dot(
                jnp.concatenate([part(1, g, h), held["bias", g]], axis=0),
                jnp.concatenate([part(0, g, h), one_row], axis=0),
                TN,
            )

        def soften(g, h):
            value = held.pop(("s", g, h))
            slk = held["slk", g][h : h + 1, :]
            peak = jnp.maximum(jnp.max(value, axis=0, keepdims=True), slk)
            raised = jnp.exp(value - peak).astype(bf16)
            probs_out[g, h] = raised
            held["e", g, h] = raised
            edge = jnp.exp(slk - peak)
            held["edge", g, h] = edge
            edges[g, h : h + 1, :] = edge
            edge_out[g, h // 2, h % 2 : h % 2 + 1, :] = edge

        def mix(g, h):
            held["o", g, h] = dot(
                jnp.concatenate([part(2, g, h), one_row], axis=0), held.pop(("e", g, h))
            )

        def add_left(g):
            held["add", g] = dot((heads * held["vl", g]).astype(bf16), edges[g].astype(bf16), TN)

        def finish(g, h):
            out = held.pop(("o", g, h))
            span = slice(h * HEAD, (h + 1) * HEAD)
            inv = 1.0 / (out[HEAD : HEAD + 1, :] + held["edge", g, h])
            inv_out[g, h : h + 1, :] = inv
            mixed = ((out[:HEAD, :] + held["add", g][span]) * inv).astype(bf16)
            atta[span, lanes_of(g)] = mixed
            att_out[span, lanes_of(g)] = mixed

        count_units = len(units)
        for t in range(-2, count_units + 4):
            if t + 2 == 0:
                for g in range(group):
                    begin(g)
                held["branch"] = merge_branch()
            if 0 <= t + 2 < count_units:
                scores(*units[t + 2])
            if t == -1:
                hid_out[...] = hidden_of(held.pop("branch"), step - 1 + 3 * (1 - jnp.minimum(step, 1)))
                qkv_out[...] = qkv2[now]
                fi_out[:features, :] = fia[:features, :]
                fi_out[features:, :] = fia[features : features + 16, :]
                held["next"] = first_norm(tok)
            if t == 1:
                tokens, fi = held.pop("next")
                toks[lax.rem(step + 1, 3)] = tokens
                fia[:features, :] = fi
            if t in (2, 4, 6):
                project(later, (t - 2) // 2)
            if 0 <= t < count_units:
                soften(*units[t])
            if 0 <= t - 2 < count_units:
                mix(*units[t - 2])
            for g in range(group):
                if t == HEADS * g + 3:
                    left_query(g)
                if t == HEADS * (g + 1):
                    add_left(g)
                if t == HEADS * (g + 1) + 3:
                    for h in range(HEADS):
                        finish(g, h)

    @pl.when(step == steps)
    def _():
        hid_out[...] = hidden_of(merge_branch(), step - 1)
        attl_out[...] = attl[...]
        branch = dot(attl[...].astype(bf16), mw[...]) + row_of(mbias)
        hidl_out[...] = xl[...] + row_live(live, count, rows) * branch


def feed_kernel(
    count, group,
    hid, att, inv, cot, cleft, live, gain, shift, dbias, hidl, attl, upw, upb, dnw, mw,
    out, gh_out, gml_out, dots_out, ghl_out, gmleft_out, send,
    upt, dnt, sia, atta, act, gpre, gb, cols, gsum, xl, outl, up_acc, down_acc, merge_acc, sums_out,
):
    step = pl.program_id(0)
    features, hidden_units = upw.shape
    rows = xl.shape[0]
    width = group * MAIN
    part = 384

    @pl.when(step == 0)
    def _():
        gain_row, shift_row, dbias_row = row_of(gain), row_of(shift), row_of(dbias)
        for at in range(0, hidden_units, part):
            span = slice(at, at + part)
            upt[span, :features] = upw[:, span].astype(f32).T.astype(bf16)
            upt[span, features:] = rows_where(0, upb[0:1, span].astype(f32), 128, f32).T.astype(bf16)
            dnt[:, span] = dnw[span, :].astype(f32).T.astype(bf16)
        ones = rows_where(0, jnp.ones((1, width), f32), 128, bf16)
        sia[features:, :] = ones
        atta[features:, :] = ones
        cols[0] = as_column(gain_row)
        cols[1] = as_column(shift_row)
        cols[2] = as_column(dbias_row)
        gsum[...] = jnp.zeros_like(gsum)
        take_left(cleft, xl, count)
        alive = row_live(live, count, rows)
        normed, scale = norm_rows(hidl[...])
        si = (normed * gain_row + shift_row).astype(bf16)
        pre = dot(si, upw[...]) + upb[0:1, :].astype(f32)
        value, slope = gelu_both(pre)
        value = value.astype(bf16)
        outl[...] = hidl[...] + alive * (dot(value, dnw[...]) + dbias_row)
        grad_branch = (alive * xl[...]).astype(bf16)
        grad_pre = (dot(grad_branch, dnw[...], NT) * slope).astype(bf16)
        grad_second = dot(grad_pre, upw[...], NT)
        grad_hidden = xl[...] + norm_back(grad_second * gain_row, normed, scale, 1)
        ghl_out[...] = grad_hidden
        grad_attn = (alive * grad_hidden).astype(bf16)
        gmleft_out[...] = dot(grad_attn, mw[...], NT).astype(bf16).astype(f32)
        one = jnp.ones((rows, 16), f32)
        up_acc[...] = dot(jnp.concatenate([si.astype(f32), one], axis=1).astype(bf16), grad_pre, TN)
        down_acc[...] = dot(grad_branch, value, TN)
        merge_acc[...] = dot(jnp.concatenate([attl[...], one], axis=1).astype(bf16), grad_attn, TN)
        sums_out[...] = jnp.zeros_like(sums_out)
        sums_out[0:1, :] = jnp.sum(grad_second * normed, axis=0, keepdims=True)
        sums_out[1:2, :] = jnp.sum(grad_second, axis=0, keepdims=True)
        sums_out[2:3, :] = jnp.sum(grad_branch.astype(f32), axis=0, keepdims=True)

    alive = lane_live(live, step * group, group)
    hidden = hid[...]
    normed, scale = norm_columns(hidden)
    sia[:features, :] = (normed * wide(cols[0], width) + wide(cols[1], width)).astype(bf16)
    cotangent = jnp.concatenate([cot[g].T for g in range(group)], axis=1).astype(f32)
    gb[...] = (cotangent * alive).astype(bf16)
    pres, grads = {}, {}
    ready = hidden_units // part

    def into(c):
        span = slice(c * part, (c + 1) * part)
        pres[c] = dot(upt[span, :], sia[...])
        grads[c] = dot(dnw[span, :], gb[...])

    def through(c):
        span = slice(c * part, (c + 1) * part)
        value, slope = gelu_both(pres.pop(c))
        act[span, :] = value.astype(bf16)
        gpre[span, :] = (grads.pop(c) * slope).astype(bf16)

    into(0)
    for c in range(ready):
        if c + 1 < ready:
            into(c + 1)
        through(c)
    grad_second = dot(upw[...], gpre[...])
    reduced = dot(dnt[...], act[...])
    up_acc[...] += dot(sia[: up_acc.shape[0], :], gpre[...], NT)
    grad_hidden = cotangent + norm_back(grad_second * wide(cols[0], width), normed, scale, 0)
    gh_out[...] = grad_hidden
    grad_attn = (alive * grad_hidden).astype(bf16)
    grad_mixed = dot(mw[...], grad_attn)
    down_acc[...] += dot(gb[...], act[...], NT)
    result = hidden + alive * (reduced + wide(cols[2], width))
    for g in range(group):
        image = step * group + g
        out[g, :MAIN, :] = result[:, g * MAIN : (g + 1) * MAIN].astype(bf16).T
        out[g, MAIN : MAIN + 1, :] = outl[pl.ds(image, 1), :].astype(bf16)
    both = grad_second * normed
    for at in range(0, width, 128):
        gsum[0] += both[:, at : at + 128]
        gsum[1] += grad_second[:, at : at + 128]
    sums_out[2:3, :] += dot(jnp.ones((16, width), bf16), gb[...], NT)[0:1, :]
    atta[:features, :] = att[...]
    merge_acc[...] += dot(atta[: merge_acc.shape[0], :], grad_attn, NT)
    grad_mixed = grad_mixed.astype(bf16).astype(f32)
    both = grad_mixed * att[...].astype(f32)
    dots_out[...] = jnp.zeros_like(dots_out)
    for g in range(group):
        lanes = slice(g * MAIN, (g + 1) * MAIN)
        for h in range(HEADS):
            span = slice(h * HEAD, (h + 1) * HEAD)
            row_inv = inv[g, h : h + 1, :]
            gml_out[span, lanes] = (grad_mixed[span, lanes] * row_inv).astype(bf16)
            row_dot = jnp.sum(both[span, lanes], axis=0, keepdims=True) * row_inv
            dots_out[g, h // 2, h % 2 : h % 2 + 1, :] = row_dot

    @pl.when(step == pl.num_programs(0) - 1)
    def _():
        sums_out[0:1, :] += jnp.sum(gsum[0].T, axis=0, keepdims=True)
        sums_out[1:2, :] += jnp.sum(gsum[1].T, axis=0, keepdims=True)
        up_rows, merge_rows = up_acc.shape[0], merge_acc.shape[0]
        quarter = (merge_rows + 48) // 4
        used = up_rows + features + quarter
        shared = jnp.concatenate(
            [merge_acc[...], sums_out[...], jnp.zeros((40, features), f32)], axis=0
        ).astype(bf16)
        for s in range(send.shape[0]):
            for q in range(4):
                lanes = slice(q * features + s * 128, q * features + (s + 1) * 128)
                send[s, q, :up_rows] = up_acc[:, lanes].astype(bf16)
                send[s, q, up_rows : up_rows + features] = down_acc[:, lanes].astype(bf16)
                send[s, q, up_rows + features : used] = shared[
                    q * quarter : (q + 1) * quarter, s * 128 : (s + 1) * 128
                ]
                if used < send.shape[2]:
                    send[s, q, used:] = jnp.zeros((send.shape[2] - used, 128), bf16)


def back_kernel(
    count, group, steps, sums, spread, plan,
    qkv, probs, edge, lp, lself, gml, dots, fi, fil, qkvl, attl, gmleft, aw, send,
    tok, left, gh, ghl, gain, shift,
    out, attend_out, up_out, down_out, merge_out, rows_out,
    gpa, acc, gpl, awp, cols, xl, outl, *comm,
):
    step = pl.program_id(0)
    features = aw.shape[0]
    rows = xl.shape[0]
    pairs = HEADS // 2
    last = pairs * steps
    pair = lax.rem(step // steps, pairs)
    at_group = lax.rem(step, steps)
    used = len(sums.scratch())
    sums.bind(send, comm[:used])
    spread.bind(comm[used:])
    engines = {"sums": sums, "spread": spread}
    heads = head_rows(rows, 128)

    @pl.when(step == 0)
    def _():
        barrier = pltpu.get_barrier_semaphore()
        peers = sums.peers() + [spread.plane(3)[0]]
        for peer in peers:
            pl.semaphore_signal(barrier, inc=1, device_id=peer, device_id_type=pl.DeviceIdType.MESH)
        for part in range(pairs):
            for at in range(3):
                cut = slice(at * features + part * 128, at * features + (part + 1) * 128)
                awp[:, parts_of(at, part)] = aw[:, cut]
        cols[...] = as_column(row_of(gain))
        gpl[...] = jnp.zeros_like(gpl)
        pl.semaphore_wait(barrier, len(peers))
        for s in range(sums.streams):
            sums.start(1, s)

    for slot, name, phase, s in plan:
        if slot < last + steps:
            pl.when(step == slot)(functools.partial(engines[name].advance, phase, s))

    @pl.when(step < last)
    def _():
        at16 = lax.broadcasted_iota(jnp.int32, (16, MAIN), 0)
        minus = jnp.where(at16 < 2, -1.0, 0.0).astype(bf16)
        gp = gpa.at[at_group, pl.ds(pl.multiple_of(pair * 384, 128), 384)]
        held = {}
        units = [(g, r) for g in range(group) for r in range(2)]

        def lanes_of(g):
            return slice(g * MAIN, (g + 1) * MAIN)

        def part(at, r, g):
            return qkv[at * 128 + r * HEAD : at * 128 + (r + 1) * HEAD, lanes_of(g)]

        def both(at, g):
            return qkv[at * 128 : (at + 1) * 128, lanes_of(g)]

        def left_one(g):
            image = at_group * group + g
            row = qkvl[pl.ds(image, 1), :]
            ql, kl, vl = (row[:, at * 128 : (at + 1) * 128] for at in range(3))
            gm_row = gmleft[pl.ds(image, 1), :]
            row_dot = jnp.sum(heads * (gm_row * attl[pl.ds(image, 1), :]), axis=1, keepdims=True)
            self_prob = lself[g, 0][:, 0:1]
            self_grad = self_prob * (jnp.sum(heads * (gm_row * vl), axis=1, keepdims=True) - row_dot)
            self_grad = self_grad.astype(bf16).astype(f32)
            held["rows", g] = (ql, kl, vl, gm_row, row_dot, self_prob, self_grad)
            gmb = (heads * gm_row).astype(bf16)
            held["gmb", g] = gmb
            held["edge dp", g] = dot((heads * vl).astype(bf16), gml[:, lanes_of(g)])
            held["left dp", g] = dot(gmb, both(2, g))

        def left_two(g):
            ql, kl, vl, gm_row, row_dot, self_prob, self_grad = held["rows", g]
            edge_grad = (edge[g, 0] * (held.pop(("edge dp", g)) - dots[g, 0])).astype(bf16)
            left_grad = (lp[g, 0] * (held.pop(("left dp", g)) - row_dot)).astype(bf16)
            held["add", g] = (
                dot((heads * kl).astype(bf16), edge_grad, TN),
                dot((heads * ql).astype(bf16), left_grad, TN),
                dot(held.pop(("gmb", g)), lp[g, 0].astype(bf16), TN),
            )
            held["left", g] = (
                dot(left_grad, both(1, g), NT),
                dot(edge_grad, both(0, g), NT),
                dot(edge[g, 0].astype(bf16), gml[:, lanes_of(g)], NT),
            )

        def left_three(g):
            ql, kl, vl, gm_row, row_dot, self_prob, self_grad = held.pop(("rows", g))
            grad_ql, grad_kl, grad_vl = (
                jnp.sum(v * heads, axis=0, keepdims=True) for v in held.pop(("left", g))
            )
            self_row = jnp.sum(heads * self_grad, axis=0, keepdims=True)
            prob_row = jnp.sum(heads * self_prob.astype(bf16).astype(f32), axis=0, keepdims=True)
            image = at_group * group + g
            value = jnp.concatenate(
                [
                    (grad_ql + self_row * kl) * HEAD**-0.5,
                    grad_kl + self_row * ql,
                    grad_vl + prob_row * gm_row,
                ],
                axis=1,
            )
            gpl[pair, pl.ds(image, 1), :] = value.astype(bf16).astype(f32)

        def change(g, r):
            row_dot = dots[g, 0, r : r + 1, :]
            high = row_dot.astype(bf16).astype(f32)
            rest = jnp.where(at16 == 0, high, jnp.where(at16 == 1, row_dot - high, 0.0)).astype(bf16)
            held["z", g, r] = dot(
                jnp.concatenate([part(2, r, g), minus], axis=0),
                jnp.concatenate([gml[r * HEAD : (r + 1) * HEAD, lanes_of(g)], rest], axis=0),
                TN,
            )

        def scores(g, r):
            raised = probs[g, r]
            held["ds", g, r] = (raised.astype(f32) * held.pop(("z", g, r))).astype(bf16)
            held["v", g, r] = dot(gml[r * HEAD : (r + 1) * HEAD, lanes_of(g)], raised, NT)

        def grads(g, r):
            ds = held.pop(("ds", g, r))
            held["q", g, r] = dot(part(1, r, g), ds)
            held["k", g, r] = dot(part(0, r, g), ds, NT)

        def store(g, r):
            span = slice(r * HEAD, (r + 1) * HEAD)
            add_q, add_k, add_v = held["add", g]
            values = (
                (held.pop(("q", g, r)) + add_q[span]) * HEAD**-0.5,
                held.pop(("k", g, r)) + add_k[span],
                held.pop(("v", g, r)) + add_v[span],
            )
            for at, value in enumerate(values):
                gp[at * 128 + r * HEAD : at * 128 + (r + 1) * HEAD, lanes_of(g)] = value.astype(bf16)

        number = len(units)
        for t in range(-4, number + 4):
            for g in range(group):
                if t == 2 * g - 4:
                    left_one(g)
                if t == 2 * g - 2:
                    left_two(g)
                if t == 2 * g + 2:
                    left_three(g)
            if 0 <= t + 2 < number:
                change(*units[t + 2])
            if 0 <= t < number:
                scores(*units[t])
            if 0 <= t - 1 < number:
                grads(*units[t - 1])
            if 0 <= t - 3 < number:
                store(*units[t - 3])

        @pl.when(at_group == 0)
        def _():
            acc[...] = jnp.zeros_like(acc)

        acc[...] += dot(fi[...], gp[...], NT)

        @pl.when(at_group == steps - 1)
        def _():
            one = jnp.ones((rows, 16), f32)
            acc[...] += dot(
                jnp.concatenate([fil[...], one], axis=1).astype(bf16), gpl[pair].astype(bf16), TN
            )
            weight = awp[:, pl.ds(pl.multiple_of(pair * 384, 128), 384)].astype(f32)
            by_gain = weight * acc[:features, :]
            by_shift = weight * acc[features : features + 1, :]
            fold = lambda v: jnp.sum((v[:, :128] + v[:, 128:256] + v[:, 256:]).T, axis=0, keepdims=True)
            shift_row = fold(by_shift)
            gain_row = (fold(by_gain) - row_of(shift) * shift_row) / row_of(gain)
            block = features + 32
            for at in range(3):
                lanes = slice(at * 128, (at + 1) * 128)
                spread.send[pair, at * block : at * block + features + 16] = acc[:, lanes].astype(bf16)
                ends = rows_where(0, gain_row[:, lanes], 16, f32) + rows_where(1, shift_row[:, lanes], 16, f32)
                spread.send[pair, at * block + features + 16 : (at + 1) * block] = ends.astype(bf16)
            rest = spread.send.shape[1] - 3 * block
            if rest:
                spread.send[pair, 3 * block :] = jnp.zeros((rest, 128), bf16)
            spread.start(1, pair)

    @pl.when(step == last)
    def _():
        take_left(left, xl, count)
        normed, scale = norm_rows(xl[...])
        packed = jnp.concatenate([gpl[p] for p in range(pairs)], axis=1).astype(bf16)
        grad_first = dot(packed, awp[...], NT)
        outl[...] = ghl[...] + norm_back(grad_first * row_of(gain), normed, scale, 1)

    @pl.when(step >= last)
    def _():
        held = {}

        def product(g):
            held["grad", g] = dot(awp[...], gpa[at_group, :, g * MAIN : (g + 1) * MAIN])

        def norm(g):
            held["norm", g] = norm_columns(tok[g].T.astype(f32))

        def finish(g):
            normed, scale = held.pop(("norm", g))
            grad = norm_back(held.pop(("grad", g)) * wide(cols[...], MAIN), normed, scale, 0)
            result = gh[:, g * MAIN : (g + 1) * MAIN] + grad
            out[g, :MAIN, :] = result.astype(bf16).T
            image = at_group * group + g
            out[g, MAIN : MAIN + 1, :] = outl[pl.ds(image, 1), :].astype(bf16)

        product(0)
        norm(0)
        for g in range(group):
            if g + 1 < group:
                product(g + 1)
                norm(g + 1)
            finish(g)

    @pl.when(step == last + steps - 1)
    def _():
        for slot, name, phase, s in plan:
            if slot >= last + steps:
                engines[name].advance(phase, s)
        for s in range(sums.streams):
            lanes = slice(s * 128, (s + 1) * 128)
            up_out[:, lanes] = sums.quarter_rows(s, 0, features)
            rows_out[8:16, lanes] = sums.quarter_rows(s, features, 16)[:8]
            down_out[lanes, :] = sums.quarter_rows(s, features + 16, features).T
            shared = jnp.concatenate([sums.out[s, q].astype(f32) for q in range(4)], axis=0)
            merge_out[:, lanes] = shared[:features]
            rows_out[16:24, lanes] = shared[features : features + 8]
            rows_out[:8, lanes] = shared[features + 16 : features + 24]
        block = features + 32
        for at in range(3):
            total = jnp.zeros((16, 128), f32)
            for p in range(pairs):
                lanes = slice(at * features + p * 128, at * features + (p + 1) * 128)
                attend_out[:, lanes] = spread.out[p, at * block : at * block + features].astype(f32)
                total = total + spread.out[p, at * block + features + 16 : (at + 1) * block].astype(f32)
                if at != 1:
                    first = 32 + (at // 2) * 8
                    bias = spread.out[p, at * block + features : at * block + features + 16].astype(f32)
                    rows_out[first : first + 8, p * 128 : (p + 1) * 128] = bias[:8]
            rows_out[24:32, at * 128 : (at + 1) * 128] = total[:8]


def whole(*dims):
    return pl.BlockSpec(dims, lambda i: (0,) * len(dims))


def once(*dims):
    return pl.BlockSpec(dims, lambda i: (0,) * len(dims), pipeline_mode=pl.Buffered(1))


LIVE = pl.BlockSpec(memory_space=pltpu.SMEM)


def params(**more):
    return pltpu.CompilerParams(
        vmem_limit_bytes=60 * 2**20, dimension_semantics=("arbitrary",), **more
    )


def shape(dtype, *dims):
    return jax.ShapeDtypeStruct(dims, dtype)


def shards(
    mesh_sizes, tokens, image_mask, patch_mask, first_gain, first_shift, attend_weight, attend_bias,
    merge_weight, merge_bias, second_gain, second_shift, up_weight, up_bias, down_weight,
    down_bias, cotangent,
):
    n, seq, d = tokens.shape
    packed = attend_weight.shape[1]
    rows = -(-n // 16) * 16
    group = 2 if n % 2 == 0 else 1
    steps = n // group
    width = group * MAIN
    pairs = HEADS // 2
    total = n * MAIN
    left = pl.BlockSpec((n, 16, d), lambda i: (0, MAIN // 16, 0), pipeline_mode=pl.Buffered(1))
    up_all = lax.all_gather(up_weight, "tensor", axis=1, tiled=True)
    down_all = lax.all_gather(down_weight, "tensor", axis=0, tiled=True)
    up_bias_all = lax.all_gather(up_bias, "tensor", axis=0, tiled=True)[None, :]
    units = up_all.shape[1]

    here = lambda i: jnp.minimum(i, steps - 1)
    cols = lambda r: pl.BlockSpec((r, width), lambda i: (0, here(i)))
    images = lambda *dims: pl.BlockSpec((group, *dims), lambda i: (here(i),) + (0,) * len(dims))
    fi, qkv, probs, edges, invs, lp, lself, att, hid, fil, qkvl, attl, hidl = pl.pallas_call(
        functools.partial(attend_kernel, n, group, steps),
        grid=(steps + 1,),
        in_specs=[
            once(group, MAIN, d),
            pl.BlockSpec((group, MAIN, d), lambda i: (here(i + 1), 0, 0)),
            left, whole(n, MAIN), LIVE, whole(d), whole(d), whole(2, d), whole(d),
            once(d, packed), once(d, d),
        ],
        out_specs=[
            cols(d + 16), cols(packed), images(HEADS, MAIN, MAIN), images(pairs, 16, MAIN),
            images(16, MAIN), images(pairs, 16, MAIN), images(pairs, 16, 128), cols(d),
            pl.BlockSpec((d, width), lambda i: (0, jnp.maximum(i, 1) - 1)),
            whole(rows, d), whole(rows, packed), whole(rows, d), whole(rows, d),
        ],
        out_shape=[
            shape(bf16, d + 16, total), shape(bf16, packed, total), shape(bf16, n, HEADS, MAIN, MAIN),
            shape(f32, n, pairs, 16, MAIN), shape(f32, n, 16, MAIN), shape(f32, n, pairs, 16, MAIN),
            shape(f32, n, pairs, 16, 128), shape(bf16, d, total), shape(f32, d, total),
            shape(f32, rows, d), shape(f32, rows, packed), shape(f32, rows, d), shape(f32, rows, d),
        ],
        scratch_shapes=[
            pltpu.VMEM((packed, d + 128), bf16), pltpu.VMEM((d, d + 128), bf16),
            pltpu.VMEM((d + 128, width), bf16), pltpu.VMEM((d + 128, width), bf16),
            pltpu.VMEM((2, d, 128), f32), pltpu.VMEM((group, 16, MAIN), f32),
            pltpu.VMEM((group, 16, MAIN), f32), pltpu.VMEM((2, packed, width), bf16),
            pltpu.VMEM((3, d, width), bf16),
            pltpu.VMEM((rows, d), f32), pltpu.VMEM((rows, packed), f32), pltpu.VMEM((rows, d), f32),
        ],
        compiler_params=params(),
        name="attend",
    )(
        tokens, tokens, tokens, patch_mask, image_mask, first_gain, first_shift, attend_bias, merge_bias,
        attend_weight, merge_weight,
    )

    rows_quarter = d + 16 + d + (d + 64) // 4
    unit = 16 * mesh_sizes[0]
    rows_quarter = -(-rows_quarter // unit) * unit
    sums = Sums(mesh_sizes, d // 128, rows_quarter, (2 * d + 16, (d + 64) // 4))
    cols = lambda r: pl.BlockSpec((r, width), lambda i: (0, i))
    images = lambda *dims: pl.BlockSpec((group, *dims), lambda i: (i,) + (0,) * len(dims))
    output, gh, gml, dots, ghl, gmleft, send = pl.pallas_call(
        functools.partial(feed_kernel, n, group),
        grid=(steps,),
        in_specs=[
            cols(d), cols(d), images(16, MAIN), images(MAIN, d), left, LIVE, whole(d), whole(d), whole(d),
            whole(rows, d), whole(rows, d), once(d, units), whole(1, units), once(units, d), once(d, d),
        ],
        out_specs=[
            images(seq, d), cols(d), cols(d), images(pairs, 16, MAIN), whole(rows, d), whole(rows, d),
            once(sums.streams, 4, rows_quarter, 128),
        ],
        out_shape=[
            shape(bf16, n, seq, d), shape(f32, d, total), shape(bf16, d, total),
            shape(f32, n, pairs, 16, MAIN), shape(f32, rows, d), shape(f32, rows, d),
            shape(bf16, sums.streams, 4, rows_quarter, 128),
        ],
        scratch_shapes=[
            pltpu.VMEM((units, d + 128), bf16), pltpu.VMEM((d, units), bf16),
            pltpu.VMEM((d + 128, width), bf16), pltpu.VMEM((d + 128, width), bf16),
            pltpu.VMEM((units, width), bf16), pltpu.VMEM((units, width), bf16),
            pltpu.VMEM((d, width), bf16), pltpu.VMEM((3, d, 128), f32), pltpu.VMEM((2, d, 128), f32),
            pltpu.VMEM((rows, d), f32), pltpu.VMEM((rows, d), f32),
            pltpu.VMEM((d + 16, units), f32), pltpu.VMEM((d, units), f32), pltpu.VMEM((d + 16, d), f32),
            pltpu.VMEM((8, d), f32),
        ],
        compiler_params=params(),
        name="feed",
    )(
        hid, att, invs, cotangent, cotangent, image_mask, second_gain, second_shift, down_bias, hidl, attl,
        up_all, up_bias_all, down_all, merge_weight,
    )

    group = next(g for g in (7, 2, 1) if n % g == 0)
    steps = n // group
    width = group * MAIN
    last = pairs * steps
    chunk = -(-3 * (d + 32) // (8 * 16)) * 16
    spread = Spread(mesh_sizes, pairs, chunk)
    plan = [(min(phase, last + steps), "sums", phase, s) for phase in range(1, 8) for s in range(sums.streams)]
    for p in range(pairs):
        plan += [((p + 1) * steps + phase, "spread", phase, p) for phase in range(1, 6)]
    plan.sort(key=lambda item: item[0])
    early = lambda i: i - (i // last) * (i - (last - 1))
    late = lambda i: (i // last) * (i - last)
    by_pair = lambda r: pl.BlockSpec((r, width), lambda i: (early(i) // steps, early(i) % steps))
    of_pair = lambda *dims: pl.BlockSpec(
        (group, 1, *dims), lambda i: (early(i) % steps, early(i) // steps) + (0,) * len(dims)
    )
    pair_lanes = lambda w: pl.BlockSpec((rows, w), lambda i: (0, early(i) // steps))
    late_images = lambda *dims: pl.BlockSpec((group, *dims), lambda i: (late(i),) + (0,) * len(dims))
    input_grad, attend_grad, up_grad, down_grad, merge_grad, row_grads = pl.pallas_call(
        functools.partial(back_kernel, n, group, steps, sums, spread, plan),
        grid=(last + steps,),
        in_specs=[
            by_pair(3 * 128),
            pl.BlockSpec((group, 2, MAIN, MAIN), lambda i: (early(i) % steps, early(i) // steps, 0, 0)),
            of_pair(16, MAIN), of_pair(16, MAIN), of_pair(16, 128), by_pair(128), of_pair(16, MAIN),
            pl.BlockSpec((d + 16, width), lambda i: (0, early(i) % steps)),
            whole(rows, d), pair_lanes(384), pair_lanes(128), pair_lanes(128), once(d, packed),
            once(sums.streams, 4, rows_quarter, 128),
            late_images(MAIN, d), left, pl.BlockSpec((d, width), lambda i: (0, late(i))),
            whole(rows, d), whole(d), whole(d),
        ],
        out_specs=[
            late_images(seq, d), once(d, packed), once(d, d), once(d, d), once(d, d), whole(48, d),
        ],
        out_shape=[
            shape(bf16, n, seq, d), shape(f32, d, packed), shape(f32, d, d), shape(f32, d, d),
            shape(f32, d, d), shape(f32, 48, d),
        ],
        scratch_shapes=[
            pltpu.VMEM((steps, packed, width), bf16), pltpu.VMEM((d + 16, 384), f32),
            pltpu.VMEM((pairs, rows, 384), f32), pltpu.VMEM((d, packed), bf16), pltpu.VMEM((d, 128), f32),
            pltpu.VMEM((rows, d), f32), pltpu.VMEM((rows, d), f32), *sums.scratch(), *spread.scratch(),
        ],
        compiler_params=params(collective_id=0, has_side_effects=True),
        name="back",
    )(
        qkv, probs, edges, lp, lself, gml, dots, fi, fil, qkvl, attl, gmleft, attend_weight, send,
        tokens, tokens, gh, ghl, first_gain, first_shift,
    )
    return (
        output,
        input_grad,
        row_grads[24],
        row_grads[25],
        attend_grad,
        jnp.stack([row_grads[32], row_grads[40]]),
        merge_grad,
        row_grads[16],
        row_grads[0],
        row_grads[1],
        up_grad,
        row_grads[8],
        down_grad,
        row_grads[2],
    )


def solution(mesh):
    split = ("dp", "tensor")
    in_specs = (
        P(split, None, None), P(split), P(split, None), P(), P(), P(), P(), P(), P(), P(), P(),
        P(None, "tensor"), P("tensor"), P("tensor", None), P(), P(split, None, None),
    )
    out_specs = (
        P(split, None, None), P(split, None, None), P(), P(), P(), P(), P(), P(), P(), P(),
        P(None, "tensor"), P("tensor"), P("tensor", None), P(),
    )
    sizes = (mesh.shape["dp"], mesh.shape["tensor"])
    return jax.shard_map(functools.partial(shards, sizes), mesh=mesh, in_specs=in_specs, out_specs=out_specs, check_vma=False)
```

time: 306 us -> 190 us (0.62)
  waiting for transfers between devices: 79 us -> 6.58 us
  blocking collectives: 46.7 us -> 6.75 us
  local copies, waits for them, and re-layouts: 13.6 us -> 9.83 us
    psum x1 -> x0, waiting for transfers between devices: 77.6 us -> none  [shards(): lax.psum((attend_acc, first_sums), ('dp', 'tensor'))]
    psum x1 -> x0, blocking collectives: 40 us -> none  [shards(): lax.psum((attend_acc, first_sums), ('dp', 'tensor'))]
    unnamed x10 -> x14, local copies, waits for them, and re-layouts: 3.14 us -> 8.35 us
    all_gather x1, waiting for transfers between devices: 0.01 us -> 5.2 us  [shards(): down_all = lax.all_gather(down_weight, 'tensor', axis=0, tiled=True)]
    another operation x7 -> x0, local copies, waits for them, and re-layouts: 4.8 us -> none  [shards(): jnp.stack([v.astype(f32) for v in (first_gain, first_shift, attend_bias[0...]
    slice x3 -> x0, local copies, waits for them, and re-layouts: 4.18 us -> none  [the longest x1 2.86 us: shards(): attend_acc[:d]]
    pallas_call x3 -> x2, Pallas kernels: 106 us -> 105 us  [the longest x1 77.2 us: shards(): pl.pallas_call(functools.partial(back_kernel, n, group, steps, sums, spre...]
  transfers between devices with their start and end apart: 3 -> 2, of which waited for: 1 -> 1; matrix products, arithmetic and copies ran while one was open for 3% -> 0% of each run, Pallas kernels for 17% -> 15%
where the time goes in v3:
time: 190 us
  Pallas kernels  152 us (80%)
  between operations  14.1 us (7%)
  local copies, waits for them, and re-layouts  9.83 us (5%)
  blocking collectives  6.75 us (4%)
  waiting for transfers between devices  6.58 us (3%)
    pallas_call x1, Pallas kernels, shards(): pl.pallas_call(functools.partial(back_kernel, n, group, steps, sums, spre...  77.2 us
    pallas_call x1, Pallas kernels, shards(): pl.pallas_call(functools.partial(feed_kernel, n, group), grid=(steps,), i...  47.2 us
    pallas_call x1, Pallas kernels, shards(): pl.pallas_call(functools.partial(attend_kernel, n, group, steps), grid=(s...  27.5 us
    unnamed x14, local copies, waits for them, and re-layouts  8.35 us
    all_gather x1, blocking collectives, shards(): up_bias_all = lax.all_gather(up_bias, 'tensor', axis=0, tiled=True)[None, :]  6.75 us
    all_gather x1, waiting for transfers between devices, shards(): down_all = lax.all_gather(down_weight, 'tensor', axis=0, tiled=True)  5.2 us
  transfers between devices with their start and end apart: 2, of which 1 were waited for; matrix products, arithmetic and copies ran while one was open for 0% of the time, Pallas kernels for 15%

profile of v3, /device:TPU:0, one launch (start us, length us, event | category | flops | bytes accessed | tf_op | source)
XLA Modules:
  0.0 189.9 jit_solution(811555343439734748)
XLA Ops:
  7.2 0.0 all-gather.4.cloned.1.call-start
  7.2 0.7 all-gather.4.cloned.1.call-update
  7.9 0.0 all-gather.6.cloned.1.call-start
  8.0 0.7 all-gather.6.cloned.1.call-update
  8.7 0.7 reshape.28
  9.3 27.5 %attend.1 = (bf16[400,3584]{1,0:T(8,128)(2,1)}, bf16[1152,3584]{1,0:T(8,128)(2,1)}, bf16[14,6,256,256]{3,2,1,0:T(8,128)(2,1)}, f32[14,3,16,256]{3,2,1,0:T(8,128)...) custom-call(bf16[14,257,384]{2,1,0:T(8,128)(2,1)} %left.3, ...), custom_call_target="tpu_custom_call" | custom-call | tf_op jit(solution)/shard_map/attend/pallas_call | solution.py:970
  36.9 6.8 %all-gather = bf16[4,1,384]{2,1,0:T(2,128)(2,1)} all-gather(bf16[1,1,384]{2,1,0:T(2,128)(2,1)S(1)} %reshape.28), channel_id=1, replica_groups=mesh['dp'=8,'tensor'=4] {'tensor'}, dimensions={0}, use_global_device_ids=true | all-gather | bytes 3840 | tf_op jit(solution)/shard_map/all_gather | solution.py:964
  43.6 0.0 all-gather.4.cloned.1.call-done.upw
  43.6 5.2 %all-gather.6.cloned.1.call-done.dnw = bf16[1536,384]{1,0:T(8,128)(2,1)} async-done(((bf16[384,384]{1,0:T(8,128)(2,1)}), bf16[1536,384]{1,0:T(8,128)(2,1)}) %all-gather.6.cloned.1.call-update) | async-done | bytes 1179664 | tf_op jit(solution)/shard_map/all_gather | solution.py:963
  48.8 47.2 %feed.1 = (bf16[14,257,384]{2,1,0:T(8,128)(2,1)}, f32[384,3584]{1,0:T(8,128)}, bf16[384,3584]{1,0:T(8,128)(2,1)}, f32[14,3,16,256]{3,2,1,0:T(8,128)}, f32[16,384...) custom-call(f32[384,3584]{1,0:T(8,128)} %get-tuple-element.40.hid, ...), custom_call_target="tpu_custom_call" | custom-call | tf_op jit(solution)/shard_map/feed/pallas_call | solution.py:1012
  96.1 77.2 %back.1 = (bf16[14,257,384]{2,1,0:T(8,128)(2,1)}, f32[384,1152]{1,0:T(8,128)}, f32[384,384]{1,0:T(8,128)}, f32[384,384]{1,0:T(8,128)}, f32[384,384]{1,0:T(8,128)}, /*index=5*/f32[48,384]{1,0:T(8,128)}) custom-call(bf16[1152,3584]{1,0:T(8,128)(2,1)} %get-tuple-element.46.qkv, bf16[14,6,256,256]{3,2,1,0:T(8,128)(2,1)} %get-tuple-element.47.probs, ...), custom_call_target="tpu_custom_call" | custom-call | tf_op jit(solution)/shard_map/back/pallas_call | solution.py:1062
  173.3 1.5 slice_reduce_fusion
  174.8 0.6 pad_maximum_fusion
  175.4 0.0 copy-start
  175.4 3.8 %copy.35 = bf16[14,257,384]{2,1,0:T(8,128)(2,1)} copy(bf16[14,257,384]{2,1,0:T(8,128)(2,1)} %get-tuple-element.90) | data formatting | bytes 5526528
  179.1 0.0 copy-done
  179.1 0.0 copy-start.3
  179.1 0.0 copy-start.2
  179.1 0.0 copy-start.1
  179.2 1.2 copy.36
  180.4 0.2 copy-done.3
  180.6 0.8 copy.37
  181.4 0.0 copy-done.2
  181.4 0.8 copy.38
  182.2 0.0 copy-done.1
  182.2 0.8 copy.39
Async XLA Ops:
  7.2 36.5 %all-gather.4.cloned.1.call-start = ((), (), s32[]{:S(2)}) async-start(), calls=%async_computation | async-start | bytes 1474560 | tf_op jit(solution)/shard_map/all_gather | solution.py:962
  7.9 40.9 %all-gather.6.cloned.1.call-start = ((), (), s32[]{:S(2)}) async-start(), calls=%async_computation.1 | async-start | bytes 1474560 | tf_op jit(solution)/shard_map/all_gather | solution.py:963
  175.4 3.8 %copy-start = (f32[384,1152]{1,0:T(8,128)S(1)}, f32[384,1152]{1,0:T(8,128)}, u32[]{:S(2)}) copy-start(f32[384,1152]{1,0:T(8,128)} %get-tuple-element.93) | copy-start | bytes 5308420
  179.1 1.4 copy-start.3
  179.1 2.3 %copy-start.2 = (f32[384,384]{1,0:T(8,128)S(1)}, f32[384,384]{1,0:T(8,128)}, u32[]{:S(2)}) copy-start(f32[384,384]{1,0:T(8,128)} %get-tuple-element.99) | copy-start | bytes 1769476
  179.1 3.1 %copy-start.1 = (f32[384,384]{1,0:T(8,128)S(1)}, f32[384,384]{1,0:T(8,128)}, u32[]{:S(2)}) copy-start(f32[384,384]{1,0:T(8,128)} %get-tuple-element.101) | copy-start | bytes 1769476
Sparse Core Ops, SparseCore 0:
  9.6 20.1 all-gather.3
  31.3 17.4 all-gather.5

commit v4 on v3

v4 whole, which is shorter than its diff:
```python
import functools

import jax
import jax.numpy as jnp
from jax import lax
from jax.experimental import pallas as pl
from jax.experimental.pallas import tpu as pltpu
from jax.sharding import PartitionSpec as P

HEADS = 6
HEAD = 64
MAIN = 256
EPS = 1e-06
MASKED = -1e30
f32, bf16 = jnp.float32, jnp.bfloat16

NN = ((1,), (0,))
NT = ((1,), (1,))
TN = ((0,), (0,))


def dot(left, right, dims=NN):
    return lax.dot_general(left, right, (dims, ((), ())), preferred_element_type=f32)


def rows_where(index, value, rows, dtype):
    columns = value.shape[-1]
    at = lax.broadcasted_iota(jnp.int32, (rows, columns), 0)
    return jnp.where(at == index, value, 0.0).astype(dtype)


def wide(column, width):
    return jnp.concatenate([column] * (width // 128), axis=1)


def as_column(row):
    return jnp.broadcast_to(row, (128, row.shape[1])).T


def norm_columns(values):
    center = values - jnp.mean(values, axis=0, keepdims=True)
    scale = lax.rsqrt(jnp.mean(center * center, axis=0, keepdims=True) + EPS)
    return center * scale, scale


def norm_rows(values):
    center = values - jnp.mean(values, axis=1, keepdims=True)
    scale = lax.rsqrt(jnp.mean(center * center, axis=1, keepdims=True) + EPS)
    return center * scale, scale


def norm_back(grad, normed, scale, axis):
    mean_grad = jnp.mean(grad, axis=axis, keepdims=True)
    mean_both = jnp.mean(grad * normed, axis=axis, keepdims=True)
    return scale * (grad - mean_grad - normed * mean_both)


def gelu_both(pre):
    curve = 0.5 + 0.5 * lax.erf(pre * 0.7071067811865476)
    bell = 0.3989422804014327 * jnp.exp(-0.5 * pre * pre)
    return pre * curve, curve + pre * bell


def head_rows(rows, features):
    at = lax.broadcasted_iota(jnp.int32, (rows, features), 0)
    head = lax.broadcasted_iota(jnp.int32, (rows, features), 1) // HEAD
    return jnp.where(at == head, 1.0, 0.0)


def lane_live(live_ref, first, count):
    flags = [
        jnp.full((1, MAIN), live_ref[first + g].astype(f32)) for g in range(count)
    ]
    return jnp.concatenate(flags, axis=1)


def row_live(live_ref, count, rows):
    at = lax.broadcasted_iota(jnp.int32, (rows, 1), 0)
    flags = jnp.zeros((rows, 1), f32)
    for image in range(count):
        flags = jnp.where(at == image, live_ref[image].astype(f32), flags)
    return flags


def take_left(left_ref, to_ref, count):
    to_ref[...] = jnp.zeros_like(to_ref)
    for image in range(count):
        to_ref[image : image + 1, :] = left_ref[image].astype(f32)[0:1, :]


def flip(place, bits):
    if bits & 1:
        place = place + 1 - 2 * lax.rem(place, 2)
    if bits & 2:
        place = place + 2 - 4 * (place // 2)
    return place


def remote(src, dst, sends, recvs, index, peer):
    return pltpu.make_async_remote_copy(
        src_ref=src, dst_ref=dst, send_sem=sends.at[index], recv_sem=recvs.at[index],
        device_id=peer, device_id_type=pl.DeviceIdType.MESH,
    )


def greet(peers):
    barrier = pltpu.get_barrier_semaphore()
    for peer in peers:
        pl.semaphore_signal(barrier, inc=1, device_id=peer, device_id_type=pl.DeviceIdType.MESH)


def meet(peers):
    pl.semaphore_wait(pltpu.get_barrier_semaphore(), len(peers))


class Quarter:
    def __init__(self, dp, streams, rows):
        self.far = dp // 2
        self.streams, self.half = streams, rows // 2
        self.chunk = -(-self.half // (16 * self.far)) * 16
        self.padded = self.chunk * self.far
        self.copies = 3 + 2 * (self.far - 1)

    def scratch(self):
        s = self.streams
        vm = lambda *dims: pltpu.VMEM((s, *dims, 128), bf16)
        return [
            vm(2 * self.half), vm(2 * self.half), vm(self.half), vm(self.padded),
            vm(max(self.far - 1, 1), self.chunk), vm(2, self.padded),
            pltpu.SemaphoreType.DMA((s, self.copies)), pltpu.SemaphoreType.DMA((s, self.copies)),
        ]

    def bind(self, mine, beside, refs):
        self.mine, self.beside = mine, beside
        self.r1, self.work, self.r2, self.cur, self.r3, self.fin, self.sends, self.recvs = refs
        self.me_dp, self.me_t = lax.axis_index("dp"), lax.axis_index("tensor")
        self.x, self.z = lax.rem(self.me_dp, 2), self.me_dp // 2

    def line(self, j):
        return (lax.rem(self.z + j, self.far) * 2 + self.x, self.me_t)

    def copies_of(self, phase, s):
        across = (self.z * 2 + 1 - self.x, self.me_t)
        cp = lambda index, src, dst, peer: remote(src, dst, self.sends, self.recvs, (s, index), peer)
        if phase == 1:
            return [cp(0, self.beside.at[s], self.r1.at[s], (self.me_dp, flip(self.me_t, 1)))]
        if phase == 2:
            other = pl.ds(pl.multiple_of((1 - self.x) * self.half, 16), self.half)
            return [cp(1, self.work.at[s, other], self.r2.at[s], across)]
        found = []
        if phase == 3:
            for j in range(1, self.far):
                place = lax.rem(self.z + j, self.far)
                src = self.cur.at[s, pl.ds(pl.multiple_of(place * self.chunk, 16), self.chunk)]
                found.append(cp(1 + j, src, self.r3.at[s, j - 1], self.line(j)))
        if phase == 4:
            ref = self.fin.at[s, self.x, pl.ds(pl.multiple_of(self.z * self.chunk, 16), self.chunk)]
            for j in range(1, self.far):
                found.append(cp(self.far + j, ref, ref, self.line(j)))
        if phase == 5:
            ref = self.fin.at[s, self.x, pl.ds(0, self.half)]
            found.append(cp(2 * self.far, ref, ref, across))
        return found

    def start(self, phase, s):
        for copy in self.copies_of(phase, s):
            copy.start()

    def advance(self, phase, s):
        for copy in self.copies_of(phase, s):
            copy.wait()
        if phase == 1:
            self.work[s] = (self.mine[s].astype(f32) + self.r1[s].astype(f32)).astype(bf16)
        if phase == 2:
            kept = self.work[s, pl.ds(pl.multiple_of(self.x * self.half, 16), self.half)]
            self.cur[s, : self.half] = (kept.astype(f32) + self.r2[s].astype(f32)).astype(bf16)
            if self.padded > self.half:
                self.cur[s, self.half :] = jnp.zeros((self.padded - self.half, 128), bf16)
        if phase == 3:
            mine = pl.ds(pl.multiple_of(self.z * self.chunk, 16), self.chunk)
            total = self.cur[s, mine].astype(f32)
            for j in range(self.far - 1):
                total = total + self.r3[s, j].astype(f32)
            self.fin[s, self.x, mine] = total.astype(bf16)
        if phase < 5:
            self.start(phase + 1, s)


class Spread:
    def __init__(self, mesh_sizes, streams, chunk):
        self.dp, self.tensor = mesh_sizes
        self.far = self.dp // 2
        self.streams, self.chunk = streams, chunk
        self.copies = 1 + 3 + (self.far - 1) + 3 + 1

    def scratch(self):
        s, c = self.streams, self.chunk
        vm = lambda *dims: pltpu.VMEM((s, *dims, 128), bf16)
        return [
            vm(8 * c), vm(4 * c), vm(4 * c), vm(3, c), vm(self.far, c), vm(8 * c),
            pltpu.SemaphoreType.DMA((s, self.copies)), pltpu.SemaphoreType.DMA((s, self.copies)),
        ]

    def bind(self, refs):
        self.send, self.r1, self.work, self.r2, self.r3, self.out, self.ss, self.rs = refs
        self.me_dp, self.me_t = lax.axis_index("dp"), lax.axis_index("tensor")
        self.x, self.z = lax.rem(self.me_dp, 2), self.me_dp // 2
        self.c, self.y = lax.rem(self.me_t, 2), self.me_t // 2
        self.place = 2 * self.y + self.x

    def plane(self, j):
        x = 1 - self.x if j & 1 else self.x
        y = 1 - self.y if j & 2 else self.y
        return (self.z * 2 + x, 2 * y + self.c), 2 * y + x

    def core(self):
        return (self.me_dp, 2 * self.y + 1 - self.c)

    def line(self, j):
        return (lax.rem(self.z + j, self.far) * 2 + self.x, self.me_t)

    def rows(self, first, count):
        return pl.ds(pl.multiple_of(first * self.chunk, 16), count * self.chunk)

    def copies_of(self, phase, s):
        def cp(index, src, dst, peer):
            return pltpu.make_async_remote_copy(
                src_ref=src, dst_ref=dst, send_sem=self.ss.at[s, index], recv_sem=self.rs.at[s, index],
                device_id=peer, device_id_type=pl.DeviceIdType.MESH,
            )

        if phase == 1:
            return [cp(0, self.send.at[s, self.rows(4 * (1 - self.c), 4)], self.r1.at[s], self.core())]
        found = []
        if phase == 2:
            for j in (1, 2, 3):
                peer, place = self.plane(j)
                found.append(cp(j, self.work.at[s, self.rows(place, 1)], self.r2.at[s, j - 1], peer))
        if phase == 3:
            for j in range(1, self.far):
                ref = self.r3.at[s, self.z]
                found.append(cp(3 + j, ref, ref, self.line(j)))
        mine = self.out.at[s, self.rows(4 * self.c + self.place, 1)]
        if phase == 4:
            for j in (1, 2, 3):
                found.append(cp(2 + self.far + j, mine, mine, self.plane(j)[0]))
        if phase == 5:
            ref = self.out.at[s, self.rows(4 * self.c, 4)]
            found.append(cp(6 + self.far, ref, ref, self.core()))
        return found

    def start(self, phase, s):
        for copy in self.copies_of(phase, s):
            copy.start()

    def advance(self, phase, s):
        for copy in self.copies_of(phase, s):
            copy.wait()
        if phase == 1:
            half = self.send[s, self.rows(4 * self.c, 4)].astype(f32)
            self.work[s] = (half + self.r1[s].astype(f32)).astype(bf16)
        if phase == 2:
            total = self.work[s, self.rows(self.place, 1)].astype(f32)
            for j in range(3):
                total = total + self.r2[s, j].astype(f32)
            self.r3[s, self.z] = total.astype(bf16)
        if phase == 3:
            total = self.r3[s, 0].astype(f32)
            for j in range(1, self.far):
                total = total + self.r3[s, j].astype(f32)
            self.out[s, self.rows(4 * self.c + self.place, 1)] = total.astype(bf16)
        if phase < 5:
            self.start(phase + 1, s)


def row_of(ref):
    return ref[...].astype(f32).reshape(1, ref.shape[0])


def parts_of(at, pair):
    return slice(pair * 384 + at * 128, pair * 384 + (at + 1) * 128)


def attend_kernel(
    count, group, steps,
    tok0, tok, left, pmask, live, gain, shift, abias, mbias, aw, mw, up, ubias, down,
    fi_out, qkv_out, probs_out, edge_out, inv_out, lp_out, lself_out, att_out, hid_out,
    fil_out, qkvl_out, attl_out, hidl_out, wall, ball,
    awt, mwt, fia, atta, cols, edges, qkv2, toks, xl, qkvl, attl, brow, sends, recvs, own,
):
    step = pl.program_id(0)
    me_dp, me_t = lax.axis_index("dp"), lax.axis_index("tensor")
    beside, across = (me_dp, flip(me_t, 1)), (me_dp, flip(me_t, 2))

    def places(owner):
        return (wall.at[owner, 0], wall.at[owner, 1], ball.at[owner])

    def first_copies(peer, first):
        return [
            remote(src, dst, sends, recvs, first + k, peer)
            for k, (src, dst) in enumerate(zip((up, down, brow), places(me_t)))
        ]

    def second_copies():
        return [
            remote(ref, ref, sends, recvs, 6 + k, beside) for k, ref in enumerate(places(flip(me_t, 2)))
        ]

    def own_copies():
        return [
            pltpu.make_async_copy(src, dst, own.at[k])
            for k, (src, dst) in enumerate(zip((up, down, brow), places(me_t)))
        ]

    @pl.when(step == 0)
    def _():
        greet((beside, across))
        brow[...] = rows_where(0, row_of(ubias), 16, bf16)
        meet((beside, across))
        for copy in first_copies(across, 3) + first_copies(beside, 0) + own_copies():
            copy.start()

    @pl.when(step == steps - 2)
    def _():
        for copy in first_copies(across, 3):
            copy.wait()
        for copy in second_copies():
            copy.start()

    features = aw.shape[0]
    packed = aw.shape[1]
    rows = xl.shape[0]
    width = group * MAIN
    pairs = HEADS // 2
    heads = head_rows(rows, features)

    def first_norm(block):
        tokens = jnp.concatenate([block[g].T for g in range(group)], axis=1)
        normed, _ = norm_columns(tokens.astype(f32))
        return tokens, (normed * wide(cols[0], width) + wide(cols[1], width)).astype(bf16)

    def project(slot, part):
        span = slice(part * features, (part + 1) * features)
        qkv2[slot, span, :] = dot(awt[span, :], fia[...]).astype(bf16)

    @pl.when(step == 0)
    def _():
        ab = abias[...].astype(f32)
        for pair in range(pairs):
            for at in range(3):
                cut = slice(at * features + pair * 128, at * features + (pair + 1) * 128)
                to = parts_of(at, pair)
                scale = HEAD**-0.5 if at == 0 else 1.0
                awt[to, :features] = (aw[:, cut].astype(f32).T * scale).astype(bf16)
                if at == 1:
                    bias = jnp.zeros((1, 128), f32)
                else:
                    bias = ab[at // 2 : at // 2 + 1, pair * 128 : (pair + 1) * 128] * scale
                awt[to, features:] = rows_where(0, bias, 128, f32).T.astype(bf16)
        mwt[:, :features] = mw[...].astype(f32).T.astype(bf16)
        mwt[:, features:] = rows_where(0, row_of(mbias), 128, f32).T.astype(bf16)
        ones = rows_where(0, jnp.ones((1, fia.shape[1]), f32), 128, bf16)
        fia[features:, :] = ones
        atta[features:, :] = ones
        cols[0] = as_column(row_of(gain))
        cols[1] = as_column(row_of(shift))
        edges[...] = jnp.zeros_like(edges)
        take_left(left, xl, count)
        normed, _ = norm_rows(xl[...])
        fil = (normed * row_of(gain) + row_of(shift)).astype(bf16)
        fil_out[...] = fil.astype(f32)
        plain = dot(fil, aw[...])
        for pair in range(pairs):
            for at in range(3):
                cut = slice(at * features + pair * 128, at * features + (pair + 1) * 128)
                value = plain[:, cut]
                if at != 1:
                    value = value + ab[at // 2 : at // 2 + 1, pair * 128 : (pair + 1) * 128]
                value = value.astype(bf16).astype(f32)
                qkvl[:, parts_of(at, pair)] = value * (HEAD**-0.5) if at == 0 else value
        qkvl_out[...] = qkvl[...]
        attl[...] = jnp.zeros_like(attl)
        tokens, fi = first_norm(tok0)
        toks[0] = tokens
        fia[:features, :] = fi
        for part in range(3):
            project(0, part)

    def merge_branch():
        return dot(mwt[...], atta[...])

    def hidden_of(branch, index):
        tokens = toks[lax.rem(index, 3)].astype(f32)
        return tokens + lane_live(live, index * group, group) * branch

    @pl.when(step < steps)
    def _():
        now, later = lax.rem(step, 2), lax.rem(step + 1, 2)
        one_row = rows_where(0, jnp.ones((1, MAIN), f32), 16, bf16)
        held = {}
        units = [(g, h) for g in range(group) for h in range(HEADS)]

        def lanes_of(g):
            return slice(g * MAIN, (g + 1) * MAIN)

        def part(at, g, h):
            low = (h // 2) * 384 + at * 128 + (h % 2) * HEAD
            return qkv2[now, low : low + HEAD, lanes_of(g)]

        def all_heads(at, g):
            return jnp.concatenate(
                [qkv2[now, parts_of(at, pair), lanes_of(g)] for pair in range(pairs)], axis=0
            )

        def begin(g):
            image = step * group + g
            row = qkvl[pl.ds(image, 1), :]
            ql, kl, vl = (
                jnp.concatenate([row[:, parts_of(at, pair)] for pair in range(pairs)], axis=1)
                for at in range(3)
            )
            key_bias = jnp.where(pmask[pl.ds(image, 1), :] == 1, 0.0, MASKED)
            moved = pltpu.roll(key_bias, 1, axis=1)
            at = lax.broadcasted_iota(jnp.int32, moved.shape, 1)
            main_bias = jnp.where(at == 0, 0.0, moved)
            left_bias = moved[:, 0:1]
            held["bias", g] = rows_where(0, main_bias, 16, bf16)
            held["vl", g] = vl
            held["slk", g] = dot((heads * kl).astype(bf16), all_heads(0, g)) + left_bias
            held["sl", g] = dot((heads * ql).astype(bf16), all_heads(1, g)) + main_bias
            held["self", g] = jnp.sum(heads * (ql * kl), axis=1, keepdims=True) + left_bias

        def left_query(g):
            sl, self_score = held.pop(("sl", g)), held.pop(("self", g))
            peak = jnp.maximum(jnp.max(sl, axis=1, keepdims=True), self_score)
            raised = jnp.exp(sl - peak)
            raised_self = jnp.exp(self_score - peak)
            inv = 1.0 / (jnp.sum(raised, axis=1, keepdims=True) + raised_self)
            lp = raised * inv
            lself = raised_self * inv
            lp_out[g] = lp
            lself_out[g] = jnp.broadcast_to(lself, (rows, 128))
            mixed = dot(lp.astype(bf16), all_heads(2, g), NT) + lself * held["vl", g]
            image = step * group + g
            attl[pl.ds(image, 1), :] = (
                jnp.sum(mixed * heads, axis=0, keepdims=True).astype(bf16).astype(f32)
            )

        def scores(g, h):
            held["s", g, h] = dot(
                jnp.concatenate([part(1, g, h), held["bias", g]], axis=0),
                jnp.concatenate([part(0, g, h), one_row], axis=0),
                TN,
            )

        def soften(g, h):
            value = held.pop(("s", g, h))
            slk = held["slk", g][h : h + 1, :]
            peak = jnp.maximum(jnp.max(value, axis=0, keepdims=True), slk)
            raised = jnp.exp(value - peak).astype(bf16)
            probs_out[g, h] = raised
            held["e", g, h] = raised
            edge = jnp.exp(slk - peak)
            held["edge", g, h] = edge
            edges[g, h : h + 1, :] = edge

        def mix(g, h):
            held["o", g, h] = dot(
                jnp.concatenate([part(2, g, h), one_row], axis=0), held.pop(("e", g, h))
            )

        def add_left(g):
            edge_out[g] = edges[g]
            held["add", g] = dot((heads * held["vl", g]).astype(bf16), edges[g].astype(bf16), TN)

        def finish(g, h):
            out = held.pop(("o", g, h))
            span = slice(h * HEAD, (h + 1) * HEAD)
            inv = 1.0 / (out[HEAD : HEAD + 1, :] + held["edge", g, h])
            inv_out[g, h : h + 1, :] = inv
            mixed = ((out[:HEAD, :] + held["add", g][span]) * inv).astype(bf16)
            atta[span, lanes_of(g)] = mixed
            att_out[span, lanes_of(g)] = mixed

        count_units = len(units)
        for t in range(-2, count_units + 4):
            if t + 2 == 0:
                for g in range(group):
                    begin(g)
                held["branch"] = merge_branch()
            if 0 <= t + 2 < count_units:
                scores(*units[t + 2])
            if t == -1:
                hid_out[...] = hidden_of(held.pop("branch"), step - 1 + 3 * (1 - jnp.minimum(step, 1)))
                qkv_out[...] = qkv2[now]
                fi_out[:features, :] = fia[:features, :]
                fi_out[features:, :] = fia[features : features + 16, :]
                held["next"] = first_norm(tok)
            if t == 1:
                tokens, fi = held.pop("next")
                toks[lax.rem(step + 1, 3)] = tokens
                fia[:features, :] = fi
            if t in (2, 4, 6):
                project(later, (t - 2) // 2)
            if 0 <= t < count_units:
                soften(*units[t])
            if 0 <= t - 2 < count_units:
                mix(*units[t - 2])
            for g in range(group):
                if t == HEADS * g + 3:
                    left_query(g)
                if t == HEADS * (g + 1):
                    add_left(g)
                if t == HEADS * (g + 1) + 3:
                    for h in range(HEADS):
                        finish(g, h)

    @pl.when(step == steps)
    def _():
        hid_out[...] = hidden_of(merge_branch(), step - 1)
        attl_out[...] = attl[...]
        branch = dot(attl[...].astype(bf16), mw[...]) + row_of(mbias)
        hidl_out[...] = xl[...] + row_live(live, count, rows) * branch
        for copy in first_copies(beside, 0) + second_copies() + own_copies():
            copy.wait()


def feed_kernel(
    count, group, steps,
    hid, att, inv, cot, cleft, live, gain, shift, dbias, hidl, attl, wall, ball, mw,
    out, gh_out, gml_out, dots_out, ghl_out, gmleft_out, mine, beside, shared,
    upt, dnt, sia, atta, act, gpre, gb, cols, gsum, xl, outl, sil, gbl, actl, gprel,
    outp, gradp, up_acc, down_acc, merge_acc, sums, biases, kept, away, r1, across, r2, sends, recvs,
):
    step = pl.program_id(0)
    at_step = lax.rem(step, steps)
    second = step // steps
    features = mw.shape[0]
    rows = xl.shape[0]
    width = group * MAIN
    quarters = wall.shape[0]
    me_dp, me_t = lax.axis_index("dp"), lax.axis_index("tensor")
    core, chip = (me_dp, flip(me_t, 1)), (me_dp, flip(me_t, 2))
    first_of = (1 - second) * flip(me_t, 2) + second * me_t
    now = (first_of, flip(first_of, 1))

    def to_core():
        return remote(away, r1, sends, recvs, 0, core)

    def to_chip():
        return remote(across, r2, sends, recvs, 1, chip)

    @pl.when(step == 0)
    def _():
        greet((core, chip))
        gain_row, shift_row, dbias_row = row_of(gain), row_of(shift), row_of(dbias)
        for q in range(quarters):
            upt[q, :, :features] = wall[q, 0].astype(f32).T.astype(bf16)
            upt[q, :, features:] = rows_where(0, ball[q, 0:1, :].astype(f32), 128, f32).T.astype(bf16)
            dnt[q] = wall[q, 1].astype(f32).T.astype(bf16)
        ones = rows_where(0, jnp.ones((1, width), f32), 128, bf16)
        for k in range(steps):
            sia[k, features:, :] = ones
        atta[features:, :] = ones
        cols[0] = as_column(gain_row)
        cols[1] = as_column(shift_row)
        cols[2] = as_column(dbias_row)
        gsum[...] = jnp.zeros_like(gsum)
        biases[...] = jnp.zeros_like(biases)
        take_left(cleft, xl, count)
        alive = row_live(live, count, rows)
        normed, scale = norm_rows(hidl[...])
        si = (normed * gain_row + shift_row).astype(bf16)
        grad_branch = (alive * xl[...]).astype(bf16)
        total = hidl[...] + alive * dbias_row
        grad_second = jnp.zeros_like(total)
        for q in range(quarters):
            pre = dot(si, wall[q, 0]) + ball[q, 0:1, :].astype(f32)
            value, slope = gelu_both(pre)
            value = value.astype(bf16)
            actl[q] = value
            total = total + alive * dot(value, wall[q, 1])
            grad_pre = (dot(grad_branch, wall[q, 1], NT) * slope).astype(bf16)
            gprel[q] = grad_pre
            grad_second = grad_second + dot(grad_pre, wall[q, 0], NT)
        outl[...] = total
        grad_hidden = xl[...] + norm_back(grad_second * gain_row, normed, scale, 1)
        ghl_out[...] = grad_hidden
        grad_attn = (alive * grad_hidden).astype(bf16)
        gmleft_out[...] = dot(grad_attn, mw[...], NT).astype(bf16).astype(f32)
        one = jnp.ones((rows, 16), f32)
        sil[...] = jnp.concatenate([si.astype(f32), one], axis=1).astype(bf16)
        gbl[...] = grad_branch
        merge_acc[...] = dot(jnp.concatenate([attl[...], one], axis=1).astype(bf16), grad_attn, TN)
        sums[...] = jnp.zeros_like(sums)
        sums[0:1, :] = jnp.sum(grad_second * normed, axis=0, keepdims=True)
        sums[1:2, :] = jnp.sum(grad_second, axis=0, keepdims=True)
        sums[2:3, :] = jnp.sum(grad_branch.astype(f32), axis=0, keepdims=True)
        meet((core, chip))

    @pl.when(at_step == 0)
    def _():
        for c, q in enumerate(now):
            lanes = slice(c * features, (c + 1) * features)
            up_acc[:, lanes] = dot(sil[...], gprel[q], TN)
            down_acc[:, lanes] = dot(gbl[...], actl[q], TN)

    def rounded(ref, lanes, at):
        lanes = slice(lanes + at * 128, lanes + (at + 1) * 128)
        return jnp.concatenate([up_acc[:features, lanes], down_acc[:, lanes]], axis=0)

    @pl.when(step == steps + 1)
    def _():
        to_core().wait()
        for at in range(kept.shape[0]):
            across[at] = (kept[at] + r1[at].astype(f32)).astype(bf16)
        to_chip().start()

    pres, grads = {}, {}

    def into(c):
        pres[c] = dot(upt[now[c]], sia[at_step])
        grads[c] = dot(wall[now[c], 1], gb[at_step])

    def through(c):
        span = slice(c * features, (c + 1) * features)
        value, slope = gelu_both(pres.pop(c))
        act[span, :] = value.astype(bf16)
        gpre[span, :] = (grads.pop(c) * slope).astype(bf16)

    def both_of(ref, *more):
        return jnp.concatenate([ref[(q, *more)] for q in now], axis=1)

    def up_product():
        up_acc[...] += dot(sia[at_step, : up_acc.shape[0], :], gpre[...], NT)

    def down_product():
        down_acc[...] += dot(gb[at_step], act[...], NT)

    @pl.when(second == 0)
    def _():
        hidden = hid[...]
        normed, _ = norm_columns(hidden)
        sia[at_step, :features, :] = (normed * wide(cols[0], width) + wide(cols[1], width)).astype(bf16)
        alive = lane_live(live, at_step * group, group)
        cotangent = jnp.concatenate([cot[g].T for g in range(group)], axis=1).astype(f32)
        gb[at_step] = (cotangent * alive).astype(bf16)
        for c in range(2):
            into(c)
        for c in range(2):
            through(c)
        gradp[at_step] = dot(both_of(wall, 0), gpre[...])
        outp[at_step] = dot(both_of(dnt), act[...])
        up_product()
        down_product()

    @pl.when(second == 1)
    def _():
        alive = lane_live(live, at_step * group, group)
        for c in range(2):
            into(c)
        hidden = hid[...]
        normed, scale = norm_columns(hidden)
        cotangent = jnp.concatenate([cot[g].T for g in range(group)], axis=1).astype(f32)
        for c in range(2):
            through(c)
        grad_second = gradp[at_step] + dot(both_of(wall, 0), gpre[...])
        reduced = outp[at_step] + dot(both_of(dnt), act[...])
        up_product()
        grad_hidden = cotangent + norm_back(grad_second * wide(cols[0], width), normed, scale, 0)
        gh_out[...] = grad_hidden
        grad_attn = (alive * grad_hidden).astype(bf16)
        grad_mixed = dot(mw[...], grad_attn)
        down_product()
        result = hidden + alive * (reduced + wide(cols[2], width))
        for g in range(group):
            image = at_step * group + g
            out[g, :MAIN, :] = result[:, g * MAIN : (g + 1) * MAIN].astype(bf16).T
            out[g, MAIN : MAIN + 1, :] = outl[pl.ds(image, 1), :].astype(bf16)
        both = grad_second * normed
        for at in range(0, width, 128):
            gsum[0] += both[:, at : at + 128]
            gsum[1] += grad_second[:, at : at + 128]
        sums[2:3, :] += dot(jnp.ones((16, width), bf16), gb[at_step], NT)[0:1, :]
        atta[:features, :] = att[...]
        merge_acc[...] += dot(atta[: merge_acc.shape[0], :], grad_attn, NT)
        grad_mixed = grad_mixed.astype(bf16).astype(f32)
        both = grad_mixed * att[...].astype(f32)
        dots_out[...] = jnp.zeros_like(dots_out)
        for g in range(group):
            lanes = slice(g * MAIN, (g + 1) * MAIN)
            for h in range(HEADS):
                span = slice(h * HEAD, (h + 1) * HEAD)
                row_inv = inv[g, h : h + 1, :]
                gml_out[span, lanes] = (grad_mixed[span, lanes] * row_inv).astype(bf16)
                row_dot = jnp.sum(both[span, lanes], axis=0, keepdims=True) * row_inv
                dots_out[g, h : h + 1, :] = row_dot

    @pl.when(at_step == steps - 1)
    def _():
        for c, q in enumerate(now):
            biases[pl.ds(q, 1), :] = up_acc[features : features + 1, c * features : (c + 1) * features]

    @pl.when(step == steps - 1)
    def _():
        for at in range(kept.shape[0]):
            kept[at] = rounded(up_acc, 0, at)
            away[at] = rounded(up_acc, features, at).astype(bf16)
        to_core().start()

    @pl.when(step == 2 * steps - 1)
    def _():
        sums[0:1, :] += jnp.sum(gsum[0].T, axis=0, keepdims=True)
        sums[1:2, :] += jnp.sum(gsum[1].T, axis=0, keepdims=True)
        ends = jnp.concatenate([sums[...], biases[...]], axis=0)
        merged = jnp.concatenate([merge_acc[:features, :], merge_acc[features : features + 16, :], ends], axis=0)
        for at in range(features // 128):
            block = merged.shape[0]
            shared[at * block : (at + 1) * block] = merged[:, at * 128 : (at + 1) * 128].astype(bf16)
        rest = shared.shape[0] - (features // 128) * merged.shape[0]
        if rest:
            shared[shared.shape[0] - rest :] = jnp.zeros((rest, 128), bf16)
        for at in range(kept.shape[0]):
            beside[at] = rounded(up_acc, features, at).astype(bf16)
        to_chip().wait()
        for at in range(kept.shape[0]):
            mine[at] = (rounded(up_acc, 0, at) + r2[at].astype(f32)).astype(bf16)


def back_kernel(
    count, group, steps, late_group, late_steps, quarter, spread, plan,
    qkv, probs, edge, lp, lself, gml, dots, fi, fil, qkvl, attl, gmleft, aw, mine, beside, shared,
    tok, left, gh, ghl, gain, shift,
    out, quarter_out, spread_out, bias_out,
    gpa, acc, gpl, gplt, awp, cols, xl, outl, fis, own, *comm,
):
    step = pl.program_id(0)
    features = aw.shape[0]
    rows = xl.shape[0]
    pairs = HEADS // 2
    last = pairs * steps
    pair = lax.rem(step // steps, pairs)
    at_group = lax.rem(step, steps)
    used = len(quarter.scratch())
    quarter.bind(mine, beside, comm[:used])
    spread.bind(comm[used:])
    engines = {"quarter": quarter, "spread": spread}
    at = lax.broadcasted_iota(jnp.int32, (rows, 128), 0)
    heads = jnp.where(at == lax.broadcasted_iota(jnp.int32, (rows, 128), 1) // HEAD, 1.0, 0.0)

    def fi_copy(k):
        width = group * MAIN
        return pltpu.make_async_copy(fi.at[:, pl.ds(k * width, width)], fis.at[k], own.at[k])

    @pl.when(step == 0)
    def _():
        peers = [
            (quarter.me_dp, flip(quarter.me_t, 1)), *(spread.plane(j)[0] for j in (1, 2, 3)),
            *(spread.line(j) for j in range(1, spread.far)),
        ]
        greet(peers)
        for k in range(steps):
            fi_copy(k).start()
        spread.send[0] = shared[...]
        for part in range(pairs):
            for k in range(3):
                cut = slice(k * features + part * 128, k * features + (part + 1) * 128)
                awp[:, parts_of(k, part)] = aw[:, cut]
        cols[...] = as_column(row_of(gain))
        gpl[...] = jnp.zeros_like(gpl)
        meet(peers)
        for s in range(quarter.streams):
            quarter.start(1, s)
        spread.start(1, 0)

    for slot, name, phase, s in plan:
        if slot < last + late_steps:
            pl.when(step == slot)(functools.partial(engines[name].advance, phase, s))

    @pl.when(step < last)
    def _():
        at16 = lax.broadcasted_iota(jnp.int32, (16, MAIN), 0)
        minus = jnp.where(at16 < 2, -1.0, 0.0).astype(bf16)
        ends_row = jnp.where(lax.broadcasted_iota(jnp.int32, (1, 16), 1) < 2, -1.0, 0.0)
        gp = gpa.at[at_group, pl.ds(pl.multiple_of(pair * 384, 128), 384)]
        held = {}
        units = [(g, r) for g in range(group) for r in range(2)]

        @pl.when(at_group == 0)
        def _():
            acc[...] = jnp.zeros_like(acc)
            gplt[...] = jnp.zeros_like(gplt)

        def lanes_of(g):
            return slice(g * MAIN, (g + 1) * MAIN)

        def part(at, r, g):
            return qkv[at * 128 + r * HEAD : at * 128 + (r + 1) * HEAD, lanes_of(g)]

        def lower(value):
            return value.astype(bf16).astype(f32)

        def prepare(g):
            image = at_group * group + g
            row = qkvl[pl.ds(image, 1), :]
            ql, kl, vl = (row[:, at * 128 : (at + 1) * 128] for at in range(3))
            gm_row = gmleft[pl.ds(image, 1), :]
            row_dot = jnp.sum(heads * (gm_row * attl[pl.ds(image, 1), :]), axis=1, keepdims=True)
            prob = jnp.sum(heads * (gm_row * vl), axis=1, keepdims=True)
            held["cols", g] = tuple(as_column(v) for v in (ql, kl, gm_row))
            held["left", g] = (vl, row_dot, prob - row_dot)

        def change(g, r):
            row_dot = dots[g, pl.ds(2 * pair + r, 1), :]
            high = row_dot.astype(bf16).astype(f32)
            rest = jnp.where(at16 == 0, high, jnp.where(at16 == 1, row_dot - high, 0.0)).astype(bf16)
            values = jnp.concatenate([part(2, r, g), minus], axis=0).T
            vl = held["left", g][0][:, r * HEAD : (r + 1) * HEAD]
            last_row = rows_where(0, jnp.concatenate([vl, ends_row], axis=1), 16, bf16)
            held["z", g, r] = dot(
                jnp.concatenate([values, last_row], axis=0),
                jnp.concatenate([gml[r * HEAD : (r + 1) * HEAD, lanes_of(g)], rest], axis=0),
            )

        def left_unit(g, r, edge_change):
            image = at_group * group + g
            span = slice(r * HEAD, (r + 1) * HEAD)
            head = pl.ds(2 * pair + r, 1)
            colq, colk, colg = (wide(v[span], MAIN) for v in held["cols", g])
            _, row_dot, self_change = held["left", g]
            row_dot, self_change = row_dot[r : r + 1, :], self_change[r : r + 1, :]
            edge_row, lp_row, self_prob = edge[g, head, :], lp[g, head, :], lself[g, head, 0:1]
            edge_grad = lower(edge_row * edge_change)
            left_change = jnp.sum(colg * part(2, r, g).astype(f32), axis=0, keepdims=True) - row_dot
            left_grad = lower(lp_row * left_change)
            self_grad = lower(self_prob * self_change)
            held["add", g, r] = (colk * edge_grad, colq * left_grad, colg * lower(lp_row))
            grad_q = jnp.sum(part(1, r, g).astype(f32) * left_grad, axis=1, keepdims=True)
            grad_k = jnp.sum(part(0, r, g).astype(f32) * edge_grad, axis=1, keepdims=True)
            grad_v = jnp.sum(
                gml[span, lanes_of(g)].astype(f32) * lower(edge_row), axis=1, keepdims=True
            )
            values = (
                (grad_q + self_grad * colk[:, 0:1]) * HEAD**-0.5,
                grad_k + self_grad * colq[:, 0:1],
                grad_v + lower(self_prob) * colg[:, 0:1],
            )
            at = lax.broadcasted_iota(jnp.int32, (HEAD, 128), 1)
            for k, value in enumerate(values):
                to = slice(k * 128 + r * HEAD, k * 128 + (r + 1) * HEAD)
                gplt[to, :] = jnp.where(at == image, lower(value), gplt[to, :])

        def scores(g, r):
            raised = probs[g, r]
            value = held.pop(("z", g, r))
            held["ds", g, r] = (raised.astype(f32) * value[:MAIN]).astype(bf16)
            left_unit(g, r, value[MAIN : MAIN + 1])
            held["v", g, r] = dot(gml[r * HEAD : (r + 1) * HEAD, lanes_of(g)], raised, NT)

        def grads(g, r):
            ds = held.pop(("ds", g, r))
            held["q", g, r] = dot(part(1, r, g), ds)
            held["k", g, r] = dot(part(0, r, g), ds, NT)

        def store(g, r):
            span = slice(r * HEAD, (r + 1) * HEAD)
            add_q, add_k, add_v = held.pop(("add", g, r))
            values = (
                (held.pop(("q", g, r)) + add_q) * HEAD**-0.5,
                held.pop(("k", g, r)) + add_k,
                held.pop(("v", g, r)) + add_v,
            )
            for at, value in enumerate(values):
                gp[at * 128 + r * HEAD : at * 128 + (r + 1) * HEAD, lanes_of(g)] = value.astype(bf16)

        number = len(units)
        for t in range(-4, number + 4):
            for g in range(group):
                if t == 2 * g - 4:
                    prepare(g)
            if 0 <= t + 2 < number:
                change(*units[t + 2])
            if 0 <= t < number:
                scores(*units[t])
            if 0 <= t - 1 < number:
                grads(*units[t - 1])
            if 0 <= t - 3 < number:
                store(*units[t - 3])

        for k in range(steps):
            pl.when(step == k)(lambda k=k: fi_copy(k).wait())
        acc[...] += dot(fis[at_group], gp[...], NT)

        @pl.when(at_group == steps - 1)
        def _():
            one = jnp.ones((rows, 16), f32)
            gpl[pair] = gplt[...].T[:rows, :]
            acc[...] += dot(
                jnp.concatenate([fil[...], one], axis=1).astype(bf16), gpl[pair].astype(bf16), TN
            )
            weight = awp[:, pl.ds(pl.multiple_of(pair * 384, 128), 384)].astype(f32)
            by_gain = weight * acc[:features, :]
            by_shift = weight * acc[features : features + 1, :]
            fold = lambda v: jnp.sum((v[:, :128] + v[:, 128:256] + v[:, 256:]).T, axis=0, keepdims=True)
            shift_row = fold(by_shift)
            gain_row = (fold(by_gain) - row_of(shift) * shift_row) / row_of(gain)
            block = features + 32
            stream = pair + 1
            for k in range(3):
                lanes = slice(k * 128, (k + 1) * 128)
                spread.send[stream, k * block : k * block + features + 16] = acc[:, lanes].astype(bf16)
                ends = rows_where(0, gain_row[:, lanes], 16, f32) + rows_where(1, shift_row[:, lanes], 16, f32)
                spread.send[stream, k * block + features + 16 : (k + 1) * block] = ends.astype(bf16)
            rest = spread.send.shape[1] - 3 * block
            if rest:
                spread.send[stream, 3 * block :] = jnp.zeros((rest, 128), bf16)
            spread.start(1, stream)

    @pl.when(step == last)
    def _():
        take_left(left, xl, count)
        normed, scale = norm_rows(xl[...])
        packed = jnp.concatenate([gpl[p] for p in range(pairs)], axis=1).astype(bf16)
        grad_first = dot(packed, awp[...], NT)
        outl[...] = ghl[...] + norm_back(grad_first * row_of(gain), normed, scale, 1)

    @pl.when(step >= last)
    def _():
        held = {}
        first = (step - last) * late_group

        def product(g):
            image = first + g
            lanes = pl.ds(pl.multiple_of(lax.rem(image, group) * MAIN, MAIN), MAIN)
            held["grad", g] = dot(awp[...], gpa[image // group, :, lanes])

        def norm(g):
            held["norm", g] = norm_columns(tok[g].T.astype(f32))

        def finish(g):
            normed, scale = held.pop(("norm", g))
            grad = norm_back(held.pop(("grad", g)) * wide(cols[...], MAIN), normed, scale, 0)
            result = gh[:, g * MAIN : (g + 1) * MAIN] + grad
            out[g, :MAIN, :] = result.astype(bf16).T
            out[g, MAIN : MAIN + 1, :] = outl[pl.ds(first + g, 1), :].astype(bf16)

        product(0)
        norm(0)
        for g in range(late_group):
            if g + 1 < late_group:
                product(g + 1)
                norm(g + 1)
            finish(g)

    @pl.when(step == last + late_steps - 1)
    def _():
        for slot, name, phase, s in plan:
            if slot >= last + late_steps:
                engines[name].advance(phase, s)
        for s in range(quarter.streams):
            for side in range(2):
                quarter_out[s, side] = quarter.fin[s, side, : quarter.half]
        spread_out[...] = spread.out[...]
        block = features + 32
        for k in range(3):
            low = k * block + features + 16
            ends = spread.out[0, low : low + 16].astype(f32)
            at = lax.broadcasted_iota(jnp.int32, ends.shape, 0)
            row = jnp.sum(jnp.where(at == 8 + quarter.me_t, ends, 0.0), axis=0, keepdims=True)
            bias_out[:, k * 128 : (k + 1) * 128] = jnp.broadcast_to(row, (8, 128))


def place_kernel(
    pairs, parts, quarter, spread, bias, output, input_grad,
    output_to, input_to, first_gain, first_shift, attend, attend_bias, merge, merge_bias,
    second_gain, second_shift, up, up_bias, down, down_bias, held, sems,
):
    features = merge.shape[0]
    count = output.shape[0]
    ins, outs = [], []
    for k, (src, to) in enumerate(((output, output_to), (input_grad, input_to))):
        for image in range(count):
            ins.append(pltpu.make_async_copy(src.at[image], held.at[k, image], sems.at[0, k, image]))
            outs.append(pltpu.make_async_copy(held.at[k, image], to.at[image], sems.at[1, k, image]))
    for copy in ins:
        copy.start()
    for s in range(quarter.shape[0]):
        lanes = slice(s * 128, (s + 1) * 128)
        up[:, lanes] = quarter[s, 0].astype(f32)
        down[lanes, :] = quarter[s, 1].astype(f32).T
    up_bias[...] = bias[0:1, :].reshape(features)
    block = features + 32
    ends, firsts, seconds, merge_ends = [], [], [], []
    for k in range(3):
        merge[:, k * 128 : (k + 1) * 128] = spread[0, k * block : k * block + features].astype(f32)
        low = k * block + features
        merge_ends.append(spread[0, low : low + 16].astype(f32))
        seconds.append(spread[0, low + 16 : low + 32].astype(f32))
        total = jnp.zeros((16, 128), f32)
        for pair in range(pairs):
            lanes = slice(k * features + pair * 128, k * features + (pair + 1) * 128)
            attend[:, lanes] = spread[pair + 1, k * block : k * block + features].astype(f32)
            total = total + spread[pair + 1, low + 16 : low + 32].astype(f32)
        firsts.append(total)
    merge_ends, firsts, seconds = (jnp.concatenate(v, axis=1) for v in (merge_ends, firsts, seconds))
    merge_bias[...] = merge_ends[0:1, :].reshape(features)
    first_gain[...] = firsts[0:1, :].reshape(features)
    first_shift[...] = firsts[1:2, :].reshape(features)
    second_gain[...] = seconds[0:1, :].reshape(features)
    second_shift[...] = seconds[1:2, :].reshape(features)
    down_bias[...] = seconds[2:3, :].reshape(features)
    for to, k in ((0, 0), (1, 2)):
        rows = [
            spread[pair + 1, k * block + features : k * block + features + 16].astype(f32)[0:1, :]
            for pair in range(pairs)
        ]
        attend_bias[to : to + 1, :] = jnp.concatenate(rows, axis=1)
    for copy, on in zip(ins, outs):
        copy.wait()
        on.start()
    for copy in outs:
        copy.wait()


def transfers(streams, steps, last, late_steps):
    end = last + late_steps
    plan = [(1, "quarter", 1, s) for s in range(streams)] + [(1, "spread", 1, 0)]
    plan += [(min(3 + s // 2, last), "quarter", 2, s) for s in range(streams)]
    plan += [(min(5 + s // 2, last), "quarter", 3, s) for s in range(streams)]
    plan += [(3, "spread", 2, 0), (5, "spread", 3, 0), (last, "spread", 4, 0), (last + 2, "spread", 5, 0)]
    plan += [
        (steps + 1, "spread", 1, 1), (steps + 2, "spread", 2, 1), (last, "spread", 3, 1),
        (last + 2, "spread", 4, 1), (last + 4, "spread", 5, 1),
        (2 * steps + 1, "spread", 1, 2), (last, "spread", 2, 2), (last + 5, "spread", 3, 2),
        (3 * steps + 2, "spread", 1, 3),
    ]
    plan.sort(key=lambda item: item[0])
    plan += [
        (end, "spread", 2, 3), (end, "quarter", 4, 0), (end, "quarter", 4, 1), (end, "quarter", 4, 2),
        (end, "spread", 4, 2), (end, "spread", 3, 3), (end, "quarter", 5, 0), (end, "quarter", 5, 1),
        (end, "spread", 5, 2), (end, "spread", 4, 3), (end, "quarter", 5, 2), (end, "spread", 5, 3),
    ]
    return plan


def whole(*dims):
    return pl.BlockSpec(dims, lambda i: (0,) * len(dims))


def once(*dims):
    return pl.BlockSpec(dims, lambda i: (0,) * len(dims), pipeline_mode=pl.Buffered(1))


LIVE = pl.BlockSpec(memory_space=pltpu.SMEM)
ANY = pl.BlockSpec(memory_space=pl.ANY)


def params(**more):
    return pltpu.CompilerParams(
        vmem_limit_bytes=60 * 2**20, dimension_semantics=("arbitrary",), **more
    )


def shape(dtype, *dims):
    return jax.ShapeDtypeStruct(dims, dtype)


def shards(
    mesh_sizes, tokens, image_mask, patch_mask, first_gain, first_shift, attend_weight, attend_bias,
    merge_weight, merge_bias, second_gain, second_shift, up_weight, up_bias, down_weight,
    down_bias, cotangent,
):
    n, seq, d = tokens.shape
    packed = attend_weight.shape[1]
    rows = -(-n // 16) * 16
    group = 2 if n % 2 == 0 else 1
    steps = n // group
    width = group * MAIN
    pairs = HEADS // 2
    total = n * MAIN
    left = pl.BlockSpec((n, 16, d), lambda i: (0, MAIN // 16, 0), pipeline_mode=pl.Buffered(1))
    quarters, share = mesh_sizes[1], up_weight.shape[1]

    here = lambda i: jnp.minimum(i, steps - 1)
    cols = lambda r: pl.BlockSpec((r, width), lambda i: (0, here(i)))
    images = lambda *dims: pl.BlockSpec((group, *dims), lambda i: (here(i),) + (0,) * len(dims))
    fi, qkv, probs, edges, invs, lp, lself, att, hid, fil, qkvl, attl, hidl, wall, ball = pl.pallas_call(
        functools.partial(attend_kernel, n, group, steps),
        grid=(steps + 1,),
        in_specs=[
            once(group, MAIN, d),
            pl.BlockSpec((group, MAIN, d), lambda i: (here(i + 1), 0, 0)),
            left, whole(n, MAIN), LIVE, whole(d), whole(d), whole(2, d), whole(d),
            once(d, packed), once(d, d), ANY, whole(share), ANY,
        ],
        out_specs=[
            cols(d + 16), cols(packed), images(HEADS, MAIN, MAIN), images(16, MAIN),
            images(16, MAIN), images(16, MAIN), images(16, 128), cols(d),
            pl.BlockSpec((d, width), lambda i: (0, jnp.maximum(i, 1) - 1)),
            whole(rows, d), whole(rows, packed), whole(rows, d), whole(rows, d), ANY, ANY,
        ],
        out_shape=[
            shape(bf16, d + 16, total), shape(bf16, packed, total), shape(bf16, n, HEADS, MAIN, MAIN),
            shape(f32, n, 16, MAIN), shape(f32, n, 16, MAIN), shape(f32, n, 16, MAIN),
            shape(f32, n, 16, 128), shape(bf16, d, total), shape(f32, d, total),
            shape(f32, rows, d), shape(f32, rows, packed), shape(f32, rows, d), shape(f32, rows, d),
            shape(bf16, quarters, 2, d, share), shape(bf16, quarters, 16, share),
        ],
        scratch_shapes=[
            pltpu.VMEM((packed, d + 128), bf16), pltpu.VMEM((d, d + 128), bf16),
            pltpu.VMEM((d + 128, width), bf16), pltpu.VMEM((d + 128, width), bf16),
            pltpu.VMEM((2, d, 128), f32), pltpu.VMEM((group, 16, MAIN), f32),
            pltpu.VMEM((2, packed, width), bf16),
            pltpu.VMEM((3, d, width), bf16),
            pltpu.VMEM((rows, d), f32), pltpu.VMEM((rows, packed), f32), pltpu.VMEM((rows, d), f32),
            pltpu.VMEM((16, share), bf16), pltpu.SemaphoreType.DMA((9,)), pltpu.SemaphoreType.DMA((9,)),
            pltpu.SemaphoreType.DMA((3,)),
        ],
        compiler_params=params(collective_id=0, has_side_effects=True),
        name="attend",
    )(
        tokens, tokens, tokens, patch_mask, image_mask, first_gain, first_shift, attend_bias, merge_bias,
        attend_weight, merge_weight, up_weight, up_bias, down_weight,
    )

    streams = d // 128
    block = d + 32
    chunk = -(-3 * block // (8 * 16)) * 16
    half_images = lambda *dims: pl.BlockSpec((group, *dims), lambda i: (i % steps,) + (0,) * len(dims))
    late_images = lambda *dims: pl.BlockSpec(
        (group, *dims), lambda i: ((i // steps) * (i - steps),) + (0,) * len(dims)
    )
    late_cols = lambda r: pl.BlockSpec((r, width), lambda i: (0, (i // steps) * (i - steps)))
    quarter_vm = lambda dtype: pltpu.VMEM((streams, 2 * d, 128), dtype)
    output, gh, gml, dots, ghl, gmleft, mine, beside, shared = pl.pallas_call(
        functools.partial(feed_kernel, n, group, steps),
        grid=(2 * steps,),
        in_specs=[
            pl.BlockSpec((d, width), lambda i: (0, i % steps)), late_cols(d), late_images(16, MAIN),
            half_images(MAIN, d), left, LIVE, whole(d), whole(d), whole(d),
            whole(rows, d), whole(rows, d), once(quarters, 2, d, share), once(quarters, 16, share), once(d, d),
        ],
        out_specs=[
            late_images(seq, d), late_cols(d), late_cols(d), late_images(16, MAIN),
            whole(rows, d), whole(rows, d),
            once(streams, 2 * d, 128), once(streams, 2 * d, 128), once(8 * chunk, 128),
        ],
        out_shape=[
            shape(bf16, n, seq, d), shape(f32, d, total), shape(bf16, d, total),
            shape(f32, n, 16, MAIN), shape(f32, rows, d), shape(f32, rows, d),
            shape(bf16, streams, 2 * d, 128), shape(bf16, streams, 2 * d, 128), shape(bf16, 8 * chunk, 128),
        ],
        scratch_shapes=[
            pltpu.VMEM((quarters, share, d + 128), bf16), pltpu.VMEM((quarters, d, share), bf16),
            pltpu.VMEM((steps, d + 128, width), bf16), pltpu.VMEM((d + 128, width), bf16),
            pltpu.VMEM((2 * share, width), bf16), pltpu.VMEM((2 * share, width), bf16),
            pltpu.VMEM((steps, d, width), bf16), pltpu.VMEM((3, d, 128), f32), pltpu.VMEM((2, d, 128), f32),
            pltpu.VMEM((rows, d), f32), pltpu.VMEM((rows, d), f32),
            pltpu.VMEM((rows, d + 16), bf16), pltpu.VMEM((rows, d), bf16),
            pltpu.VMEM((quarters, rows, share), bf16), pltpu.VMEM((quarters, rows, share), bf16),
            pltpu.VMEM((steps, d, width), f32), pltpu.VMEM((steps, d, width), f32),
            pltpu.VMEM((d + 16, 2 * share), f32), pltpu.VMEM((d, 2 * share), f32),
            pltpu.VMEM((d + 16, d), f32), pltpu.VMEM((8, d), f32), pltpu.VMEM((8, d), f32),
            quarter_vm(f32), quarter_vm(bf16), quarter_vm(bf16), quarter_vm(bf16), quarter_vm(bf16),
            pltpu.SemaphoreType.DMA((2,)), pltpu.SemaphoreType.DMA((2,)),
        ],
        compiler_params=params(collective_id=1, has_side_effects=True),
        name="feed",
    )(
        hid, att, invs, cotangent, cotangent, image_mask, second_gain, second_shift, down_bias, hidl, attl,
        wall, ball, merge_weight,
    )

    late_group, late_steps = group, steps
    group = next(g for g in (7, 2, 1) if n % g == 0)
    steps = n // group
    width = group * MAIN
    last = pairs * steps
    quarter = Quarter(mesh_sizes[0], streams, 2 * d)
    spread = Spread(mesh_sizes, pairs + 1, chunk)
    plan = transfers(streams, steps, last, late_steps)
    side = lambda i: (i + late_steps) // (last + late_steps)
    early = lambda i: i - side(i) * (i - (last - 1))
    late = lambda i: side(i) * (i - last)
    by_pair = lambda r: pl.BlockSpec((r, width), lambda i: (early(i) // steps, early(i) % steps))
    early_images = lambda *dims: pl.BlockSpec((group, *dims), lambda i: (early(i) % steps,) + (0,) * len(dims))
    pair_lanes = lambda w: pl.BlockSpec((rows, w), lambda i: (0, early(i) // steps))
    late_images = lambda *dims: pl.BlockSpec((late_group, *dims), lambda i: (late(i),) + (0,) * len(dims))
    input_grad, quarter_sum, spread_sum, bias_sum = pl.pallas_call(
        functools.partial(back_kernel, n, group, steps, late_group, late_steps, quarter, spread, plan),
        grid=(last + late_steps,),
        in_specs=[
            by_pair(3 * 128),
            pl.BlockSpec((group, 2, MAIN, MAIN), lambda i: (early(i) % steps, early(i) // steps, 0, 0)),
            early_images(16, MAIN), early_images(16, MAIN), early_images(16, 128), by_pair(128),
            early_images(16, MAIN), ANY,
            whole(rows, d), pair_lanes(384), pair_lanes(128), pair_lanes(128), once(d, packed),
            once(streams, 2 * d, 128), once(streams, 2 * d, 128), once(8 * chunk, 128),
            late_images(MAIN, d), left, pl.BlockSpec((d, late_group * MAIN), lambda i: (0, late(i))),
            whole(rows, d), whole(d), whole(d),
        ],
        out_specs=[
            late_images(seq, d), once(streams, 2, d, 128), once(pairs + 1, 8 * chunk, 128), whole(8, d),
        ],
        out_shape=[
            shape(bf16, n, seq, d), shape(bf16, streams, 2, d, 128), shape(bf16, pairs + 1, 8 * chunk, 128),
            shape(f32, 8, d),
        ],
        scratch_shapes=[
            pltpu.VMEM((steps, packed, width), bf16), pltpu.VMEM((d + 16, 384), f32),
            pltpu.VMEM((pairs, rows, 384), f32), pltpu.VMEM((384, 128), f32),
            pltpu.VMEM((d, packed), bf16), pltpu.VMEM((d, 128), f32),
            pltpu.VMEM((rows, d), f32), pltpu.VMEM((rows, d), f32),
            pltpu.VMEM((steps, d + 16, width), bf16), pltpu.SemaphoreType.DMA((steps,)),
            *quarter.scratch(), *spread.scratch(),
        ],
        compiler_params=params(collective_id=2, has_side_effects=True),
        name="back",
    )(
        qkv, probs, edges, lp, lself, gml, dots, fi, fil, qkvl, attl, gmleft, attend_weight,
        mine, beside, shared, tokens, tokens, gh, ghl, first_gain, first_shift,
    )
    row = lambda: pl.BlockSpec(memory_space=pltpu.VMEM)
    return pl.pallas_call(
        functools.partial(place_kernel, pairs, quarters),
        in_specs=[row(), row(), row(), ANY, ANY],
        out_specs=[ANY, ANY] + [row()] * 12,
        out_shape=[
            shape(bf16, n, seq, d), shape(bf16, n, seq, d), shape(f32, d), shape(f32, d),
            shape(f32, d, packed), shape(f32, 2, d), shape(f32, d, d), shape(f32, d), shape(f32, d),
            shape(f32, d), shape(f32, d, share), shape(f32, share), shape(f32, share, d), shape(f32, d),
        ],
        scratch_shapes=[pltpu.VMEM((2, n, seq, d), bf16), pltpu.SemaphoreType.DMA((2, 2, n))],
        compiler_params=pltpu.CompilerParams(vmem_limit_bytes=60 * 2**20),
        name="place",
    )(quarter_sum, spread_sum, bias_sum, output, input_grad)


def solution(mesh):
    split = ("dp", "tensor")
    in_specs = (
        P(split, None, None), P(split), P(split, None), P(), P(), P(), P(), P(), P(), P(), P(),
        P(None, "tensor"), P("tensor"), P("tensor", None), P(), P(split, None, None),
    )
    out_specs = (
        P(split, None, None), P(split, None, None), P(), P(), P(), P(), P(), P(), P(), P(),
        P(None, "tensor"), P("tensor"), P("tensor", None), P(),
    )
    sizes = (mesh.shape["dp"], mesh.shape["tensor"])
    return jax.shard_map(functools.partial(shards, sizes), mesh=mesh, in_specs=in_specs, out_specs=out_specs, check_vma=False)
```

time: 190 us -> 157 us (0.83)
  between operations: 14.1 us -> 0.85 us
  local copies, waits for them, and re-layouts: 9.83 us -> 0 us
  blocking collectives: 6.75 us -> 0 us
  waiting for transfers between devices: 6.58 us -> 0 us
  Pallas kernels: 152 us -> 156 us
    unnamed x14 -> x0, local copies, waits for them, and re-layouts: 8.35 us -> none
    all_gather x1 -> x0, blocking collectives: 6.75 us -> none  [shards(): up_bias_all = lax.all_gather(up_bias, 'tensor', axis=0, tiled=True)[None, :]]
    all_gather x2 -> x0, waiting for transfers between devices: 5.2 us -> none  [the longest x1 5.2 us: shards(): down_all = lax.all_gather(down_weight, 'tensor', axis=0, tiled=True)]
    pallas_call x1, Pallas kernels: 27.5 us -> 31.2 us  [shards(): pl.pallas_call(functools.partial(attend_kernel, n, group, steps), grid=(s...]
    pallas_call x2 -> x3, Pallas kernels: 124 us -> 125 us  [the longest x1 61.8 us: shards(): pl.pallas_call(functools.partial(back_kernel, n, group, steps, late_group...]
  transfers between devices with their start and end apart: 2 -> 0, of which waited for: 1 -> 0; matrix products, arithmetic and copies ran while one was open for 0% -> 0% of each run, Pallas kernels for 15% -> 0%
where the time goes in v4:
time: 157 us
  Pallas kernels  156 us (99%)
    pallas_call x1, Pallas kernels, shards(): pl.pallas_call(functools.partial(back_kernel, n, group, steps, late_group...  61.8 us
    pallas_call x1, Pallas kernels, shards(): pl.pallas_call(functools.partial(feed_kernel, n, group, steps), grid=(2 *...  54.7 us
    pallas_call x1, Pallas kernels, shards(): pl.pallas_call(functools.partial(attend_kernel, n, group, steps), grid=(s...  31.2 us
    pallas_call x1, Pallas kernels, shards(): pl.pallas_call(functools.partial(place_kernel, pairs, quarters), in_specs...  8.59 us

profile of v4, /device:TPU:0, one launch (start us, length us, event | category | flops | bytes accessed | tf_op | source)
XLA Modules:
  0.0 157.1 jit_solution(5702944773970277202)
XLA Ops:
  0.6 31.2 %attend.1 = (bf16[400,3584]{1,0:T(8,128)(2,1)}, bf16[1152,3584]{1,0:T(8,128)(2,1)}, bf16[14,6,256,256]{3,2,1,0:T(8,128)(2,1)}, f32[14,16,256]{2,1,0:T(8,128)}, f...) custom-call(bf16[14,257,384]{2,1,0:T(8,128)(2,1)} %left.3, ...), custom_call_target="tpu_custom_call" | custom-call | tf_op jit(solution)/shard_map/attend/pallas_call | solution.py:1087
  31.9 54.7 %feed.1 = (bf16[14,257,384]{2,1,0:T(8,128)(2,1)}, f32[384,3584]{1,0:T(8,128)}, bf16[384,3584]{1,0:T(8,128)(2,1)}, f32[14,16,256]{2,1,0:T(8,128)}, f32[16,384]{1,...) custom-call(f32[384,3584]{1,0:T(8,128)} %get-tuple-element.47.hid, ...), custom_call_target="tpu_custom_call" | custom-call | tf_op jit(solution)/shard_map/feed/pallas_call | solution.py:1135
  86.6 61.8 %back.1 = (bf16[14,257,384]{2,1,0:T(8,128)(2,1)}, bf16[3,2,384,128]{3,2,1,0:T(8,128)(2,1)}, bf16[4,1280,128]{2,1,0:T(8,128)(2,1)}, f32[8,384]{1,0:T(8,128)}) custom-call(bf16[1152,3584]{1,0:T(8,128)(2,1)} %get-tuple-element.42.qkv, bf16[14,6,256,256]{3,2,1,0:T(8,128)(2,1)} %get-tuple-element.43.probs, f32[14,16,256]{2,1,0:T(8,128)} %get-tuple-element.44.edge, ...), custom_call_target="tpu_custom_call" | custom-call | tf_op jit(solution)/shard_map/back/pallas_call | solution.py:1189
  148.4 8.6 %place.1 = (bf16[14,257,384]{2,1,0:T(8,128)(2,1)}, bf16[14,257,384]{2,1,0:T(8,128)(2,1)}, f32[384]{0:T(512)}, f32[384]{0:T(512)}, f32[384,1152]{1,0:T(8,128)}, /...) custom-call(bf16[3,2,384,128]{3,2,1,0:T(8,128)(2,1)} %get-tuple-elem, ...), custom_call_target="tpu_custom_call" | custom-call | tf_op jit(solution)/shard_map/place/pallas_call | solution.py:1224

commit v5 on v4

--- a/solution.py
+++ b/solution.py
@@ -190,19 +190,24 @@
     def __init__(self, mesh_sizes, streams, chunk):
         self.dp, self.tensor = mesh_sizes
         self.far = self.dp // 2
+        self.hops = self.far.bit_length() - 1
         self.streams, self.chunk = streams, chunk
         self.copies = 1 + 3 + (self.far - 1) + 3 + 1
+
+    def phases(self, s):
+        hops = ["line"] if s == self.streams - 1 else [("hop", k) for k in range(self.hops)]
+        return ["core", "plane", *hops, "plane back", "core back"]
 
     def scratch(self):
         s, c = self.streams, self.chunk
         vm = lambda *dims: pltpu.VMEM((s, *dims, 128), bf16)
         return [
-            vm(8 * c), vm(4 * c), vm(4 * c), vm(3, c), vm(self.far, c), vm(8 * c),
+            vm(8 * c), vm(4 * c), vm(4 * c), vm(3, c), vm(self.far, c), vm(c), vm(8 * c),
             pltpu.SemaphoreType.DMA((s, self.copies)), pltpu.SemaphoreType.DMA((s, self.copies)),
         ]
 
     def bind(self, refs):
-        self.send, self.r1, self.work, self.r2, self.r3, self.out, self.ss, self.rs = refs
+        self.send, self.r1, self.work, self.r2, self.r3, self.cur, self.out, self.ss, self.rs = refs
         self.me_dp, self.me_t = lax.axis_index("dp"), lax.axis_index("tensor")
         self.x, self.z = lax.rem(self.me_dp, 2), self.me_dp // 2
         self.c, self.y = lax.rem(self.me_t, 2), self.me_t // 2
@@ -219,58 +224,71 @@
     def line(self, j):
         return (lax.rem(self.z + j, self.far) * 2 + self.x, self.me_t)
 
+    def hop(self, k):
+        step = 1 << k
+        there = self.z + step - 2 * step * lax.rem(self.z // step, 2)
+        return (there * 2 + self.x, self.me_t)
+
     def rows(self, first, count):
         return pl.ds(pl.multiple_of(first * self.chunk, 16), count * self.chunk)
 
-    def copies_of(self, phase, s):
-        def cp(index, src, dst, peer):
-            return pltpu.make_async_remote_copy(
-                src_ref=src, dst_ref=dst, send_sem=self.ss.at[s, index], recv_sem=self.rs.at[s, index],
-                device_id=peer, device_id_type=pl.DeviceIdType.MESH,
-            )
-
-        if phase == 1:
+    def copies_of(self, kind, s):
+        cp = lambda index, src, dst, peer: remote(src, dst, self.ss, self.rs, (s, index), peer)
+        if kind == "core":
             return [cp(0, self.send.at[s, self.rows(4 * (1 - self.c), 4)], self.r1.at[s], self.core())]
         found = []
-        if phase == 2:
+        if kind == "plane":
             for j in (1, 2, 3):
                 peer, place = self.plane(j)
                 found.append(cp(j, self.work.at[s, self.rows(place, 1)], self.r2.at[s, j - 1], peer))
-        if phase == 3:
+        if kind == "line":
             for j in range(1, self.far):
                 ref = self.r3.at[s, self.z]
                 found.append(cp(3 + j, ref, ref, self.line(j)))
-        mine = self.out.at[s, self.rows(4 * self.c + self.place, 1)]
-        if phase == 4:
+        if kind[0] == "hop":
+            found.append(cp(4 + kind[1], self.cur.at[s], self.r3.at[s, kind[1]], self.hop(kind[1])))
+        if kind == "plane back":
+            mine = self.out.at[s, self.rows(4 * self.c + self.place, 1)]
             for j in (1, 2, 3):
                 found.append(cp(2 + self.far + j, mine, mine, self.plane(j)[0]))
-        if phase == 5:
+        if kind == "core back":
             ref = self.out.at[s, self.rows(4 * self.c, 4)]
             found.append(cp(6 + self.far, ref, ref, self.core()))
         return found
 
-    def start(self, phase, s):
-        for copy in self.copies_of(phase, s):
+    def start(self, kind, s):
+        for copy in self.copies_of(kind, s):
             copy.start()
 
     def advance(self, phase, s):
-        for copy in self.copies_of(phase, s):
+        phases = self.phases(s)
+        kind = phases[phase - 1]
+        for copy in self.copies_of(kind, s):
             copy.wait()
-        if phase == 1:
+        mine = self.rows(4 * self.c + self.place, 1)
+        if kind == "core":
             half = self.send[s, self.rows(4 * self.c, 4)].astype(f32)
             self.work[s] = (half + self.r1[s].astype(f32)).astype(bf16)
-        if phase == 2:
+        if kind == "plane":
             total = self.work[s, self.rows(self.place, 1)].astype(f32)
             for j in range(3):
                 total = total + self.r2[s, j].astype(f32)
-            self.r3[s, self.z] = total.astype(bf16)
-        if phase == 3:
+            if phases[2] == "line":
+                self.r3[s, self.z] = total.astype(bf16)
+            else:
+                self.cur[s] = total.astype(bf16)
+        if kind == "line":
             total = self.r3[s, 0].astype(f32)
             for j in range(1, self.far):
                 total = total + self.r3[s, j].astype(f32)
-            self.out[s, self.rows(4 * self.c + self.place, 1)] = total.astype(bf16)
-        if phase < 5:
-            self.start(phase + 1, s)
+            self.out[s, mine] = total.astype(bf16)
+        if kind[0] == "hop":
+            total = (self.cur[s].astype(f32) + self.r3[s, kind[1]].astype(f32)).astype(bf16)
+            self.cur[s] = total
+            if kind[1] == self.hops - 1:
+                self.out[s, mine] = total
+        if phase < len(phases):
+            self.start(phases[phase], s)
 
 
 def row_of(ref):
@@ -527,9 +545,9 @@
 
 def feed_kernel(
     count, group, steps,
-    hid, att, inv, cot, cleft, live, gain, shift, dbias, hidl, attl, wall, ball, mw,
+    hid0, hid, att, inv, cot0, cot, cleft, live, gain, shift, dbias, hidl, attl, wall, ball, mw,
     out, gh_out, gml_out, dots_out, ghl_out, gmleft_out, mine, beside, shared,
-    upt, dnt, sia, atta, act, gpre, gb, cols, gsum, xl, outl, sil, gbl, actl, gprel,
+    upt, dnt, sia, atta, act, gpre, gb, gattn, cols, gsum, xl, outl, sil, gbl, actl, gprel,
     outp, gradp, up_acc, down_acc, merge_acc, sums, biases, kept, away, r1, across, r2, sends, recvs,
 ):
     step = pl.program_id(0)
@@ -574,15 +592,15 @@
         grad_branch = (alive * xl[...]).astype(bf16)
         total = hidl[...] + alive * dbias_row
         grad_second = jnp.zeros_like(total)
+        pre_of = [dot(si, wall[q, 0]) + ball[q, 0:1, :].astype(f32) for q in range(quarters)]
+        grad_of = [dot(grad_branch, wall[q, 1], NT) for q in range(quarters)]
         for q in range(quarters):
-            pre = dot(si, wall[q, 0]) + ball[q, 0:1, :].astype(f32)
-            value, slope = gelu_both(pre)
-            value = value.astype(bf16)
-            actl[q] = value
-            total = total + alive * dot(value, wall[q, 1])
-            grad_pre = (dot(grad_branch, wall[q, 1], NT) * slope).astype(bf16)
-            gprel[q] = grad_pre
-            grad_second = grad_second + dot(grad_pre, wall[q, 0], NT)
+            value, slope = gelu_both(pre_of[q])
+            actl[q] = value.astype(bf16)
+            gprel[q] = (grad_of[q] * slope).astype(bf16)
+        for q in range(quarters):
+            total = total + alive * dot(actl[q], wall[q, 1])
+            grad_second = grad_second + dot(gprel[q], wall[q, 0], NT)
         outl[...] = total
         grad_hidden = xl[...] + norm_back(grad_second * gain_row, normed, scale, 1)
         ghl_out[...] = grad_hidden
@@ -617,84 +635,116 @@
         to_chip().start()
 
     pres, grads = {}, {}
-
-    def into(c):
-        pres[c] = dot(upt[now[c]], sia[at_step])
-        grads[c] = dot(wall[now[c], 1], gb[at_step])
-
-    def through(c):
-        span = slice(c * features, (c + 1) * features)
-        value, slope = gelu_both(pres.pop(c))
-        act[span, :] = value.astype(bf16)
-        gpre[span, :] = (grads.pop(c) * slope).astype(bf16)
+    lanes_of = [slice(g * MAIN, (g + 1) * MAIN) for g in range(group)]
+
+    def enter(hidden, cotangent, to):
+        normed, _ = norm_columns(hidden[...])
+        sia[to, :features, :] = (normed * wide(cols[0], width) + wide(cols[1], width)).astype(bf16)
+        alive = lane_live(live, to * group, group)
+        turned = jnp.concatenate([cotangent[g].T for g in range(group)], axis=1).astype(f32)
+        gb[to] = (turned * alive).astype(bf16)
+
+    def into(g):
+        for c in range(2):
+            pres[g, c] = dot(upt[now[c]], sia[at_step, :, lanes_of[g]])
+            grads[g, c] = dot(wall[now[c], 1], gb[at_step, :, lanes_of[g]])
+
+    def through(g):
+        for c in range(2):
+            span = slice(c * features, (c + 1) * features)
+            value, slope = gelu_both(pres.pop((g, c)))
+            act[span, lanes_of[g]] = value.astype(bf16)
+            gpre[span, lanes_of[g]] = (grads.pop((g, c)) * slope).astype(bf16)
 
     def both_of(ref, *more):
         return jnp.concatenate([ref[(q, *more)] for q in now], axis=1)
 
+    def second_sum(g):
+        return dot(both_of(wall, 0), gpre[:, lanes_of[g]])
+
+    def output_sum(g):
+        return dot(both_of(dnt), act[:, lanes_of[g]])
+
     def up_product():
         up_acc[...] += dot(sia[at_step, : up_acc.shape[0], :], gpre[...], NT)
 
     def down_product():
         down_acc[...] += dot(gb[at_step], act[...], NT)
 
+    @pl.when(step == 0)
+    def _():
+        enter(hid0, cot0, 0)
+
     @pl.when(second == 0)
     def _():
-        hidden = hid[...]
-        normed, _ = norm_columns(hidden)
-        sia[at_step, :features, :] = (normed * wide(cols[0], width) + wide(cols[1], width)).astype(bf16)
-        alive = lane_live(live, at_step * group, group)
-        cotangent = jnp.concatenate([cot[g].T for g in range(group)], axis=1).astype(f32)
-        gb[at_step] = (cotangent * alive).astype(bf16)
-        for c in range(2):
-            into(c)
-        for c in range(2):
-            through(c)
-        gradp[at_step] = dot(both_of(wall, 0), gpre[...])
-        outp[at_step] = dot(both_of(dnt), act[...])
+        for g in range(group):
+            into(g)
+        for g in range(group):
+            through(g)
+            gradp[at_step, :, lanes_of[g]] = second_sum(g)
+            outp[at_step, :, lanes_of[g]] = output_sum(g)
         up_product()
+        enter(hid, cot, at_step + 1 - (at_step + 1) // steps)
         down_product()
 
     @pl.when(second == 1)
     def _():
-        alive = lane_live(live, at_step * group, group)
-        for c in range(2):
-            into(c)
-        hidden = hid[...]
-        normed, scale = norm_columns(hidden)
-        cotangent = jnp.concatenate([cot[g].T for g in range(group)], axis=1).astype(f32)
-        for c in range(2):
-            through(c)
-        grad_second = gradp[at_step] + dot(both_of(wall, 0), gpre[...])
-        reduced = outp[at_step] + dot(both_of(dnt), act[...])
-        up_product()
-        grad_hidden = cotangent + norm_back(grad_second * wide(cols[0], width), normed, scale, 0)
-        gh_out[...] = grad_hidden
-        grad_attn = (alive * grad_hidden).astype(bf16)
-        grad_mixed = dot(mw[...], grad_attn)
-        down_product()
-        result = hidden + alive * (reduced + wide(cols[2], width))
+        held = {}
         for g in range(group):
+            into(g)
+        for g in range(group):
+            hidden = hid[:, lanes_of[g]]
+            held["norm", g] = norm_columns(hidden)
+            held["cot", g] = cot[g].T.astype(f32)
+        for g in range(group):
+            through(g)
+            held["second", g] = gradp[at_step, :, lanes_of[g]] + second_sum(g)
+            held["out", g] = outp[at_step, :, lanes_of[g]] + output_sum(g)
+
+        def back(g):
+            grad_second = held["second", g]
+            normed, scale = held["norm", g]
+            grad = held["cot", g] + norm_back(grad_second * wide(cols[0], MAIN), normed, scale, 0)
+            gh_out[:, lanes_of[g]] = grad
+            alive = live[at_step * group + g].astype(f32)
+            gattn[:, lanes_of[g]] = (alive * grad).astype(bf16)
+            both = grad_second * normed
+            for at in range(0, MAIN, 128):
+                gsum[0] += both[:, at : at + 128]
+                gsum[1] += grad_second[:, at : at + 128]
+
+        def write(g):
             image = at_step * group + g
-            out[g, :MAIN, :] = result[:, g * MAIN : (g + 1) * MAIN].astype(bf16).T
+            alive = live[image].astype(f32)
+            result = hid[:, lanes_of[g]] + alive * (held["out", g] + wide(cols[2], MAIN))
+            out[g, :MAIN, :] = result.astype(bf16).T
             out[g, MAIN : MAIN + 1, :] = outl[pl.ds(image, 1), :].astype(bf16)
-        both = grad_second * normed
-        for at in range(0, width, 128):
-            gsum[0] += both[:, at : at + 128]
-            gsum[1] += grad_second[:, at : at + 128]
-        sums[2:3, :] += dot(jnp.ones((16, width), bf16), gb[at_step], NT)[0:1, :]
-        atta[:features, :] = att[...]
-        merge_acc[...] += dot(atta[: merge_acc.shape[0], :], grad_attn, NT)
-        grad_mixed = grad_mixed.astype(bf16).astype(f32)
-        both = grad_mixed * att[...].astype(f32)
-        dots_out[...] = jnp.zeros_like(dots_out)
-        for g in range(group):
-            lanes = slice(g * MAIN, (g + 1) * MAIN)
+
+        def scale_rows(g):
+            mixed = held["mixed", g].astype(bf16).astype(f32)
+            both = mixed * att[:, lanes_of[g]].astype(f32)
             for h in range(HEADS):
                 span = slice(h * HEAD, (h + 1) * HEAD)
                 row_inv = inv[g, h : h + 1, :]
-                gml_out[span, lanes] = (grad_mixed[span, lanes] * row_inv).astype(bf16)
-                row_dot = jnp.sum(both[span, lanes], axis=0, keepdims=True) * row_inv
+                gml_out[span, lanes_of[g]] = (mixed[span] * row_inv).astype(bf16)
+                row_dot = jnp.sum(both[span], axis=0, keepdims=True) * row_inv
                 dots_out[g, h : h + 1, :] = row_dot
+
+        dots_out[...] = jnp.zeros_like(dots_out)
+        atta[:features, :] = att[...]
+        back(0)
+        up_product()
+        for g in range(1, group):
+            back(g)
+        for g in range(group):
+            held["mixed", g] = dot(mw[...], gattn[:, lanes_of[g]])
+        down_product()
+        for g in range(group):
+            scale_rows(g)
+        merge_acc[...] += dot(atta[: merge_acc.shape[0], :], gattn[...], NT)
+        sums[2:3, :] += dot(jnp.ones((16, width), bf16), gb[at_step], NT)[0:1, :]
+        for g in range(group):
+            write(g)
 
     @pl.when(at_step == steps - 1)
     def _():
@@ -732,7 +782,7 @@
     qkv, probs, edge, lp, lself, gml, dots, fi, fil, qkvl, attl, gmleft, aw, mine, beside, shared,
     tok, left, gh, ghl, gain, shift,
     out, quarter_out, spread_out, bias_out,
-    gpa, acc, gpl, gplt, awp, cols, xl, outl, fis, own, *comm,
+    gpa, acc, gpl, gplt, awp, cols, xl, outl, fis, minev, own, *comm,
 ):
     step = pl.program_id(0)
     features = aw.shape[0]
@@ -742,7 +792,7 @@
     pair = lax.rem(step // steps, pairs)
     at_group = lax.rem(step, steps)
     used = len(quarter.scratch())
-    quarter.bind(mine, beside, comm[:used])
+    quarter.bind(minev, beside, comm[:used])
     spread.bind(comm[used:])
     engines = {"quarter": quarter, "spread": spread}
     at = lax.broadcasted_iota(jnp.int32, (rows, 128), 0)
@@ -751,6 +801,19 @@
     def fi_copy(k):
         width = group * MAIN
         return pltpu.make_async_copy(fi.at[:, pl.ds(k * width, width)], fis.at[k], own.at[k])
+
+    def shared_copy():
+        return pltpu.make_async_copy(shared, spread.send.at[0], own.at[steps])
+
+    def early_copies():
+        found = [pltpu.make_async_copy(mine, minev, own.at[steps + 1])]
+        for part in range(pairs):
+            for k in range(3):
+                cut = pl.ds(k * features + part * 128, 128)
+                to = pl.ds(part * 384 + k * 128, 128)
+                sem = own.at[steps + 2 + part * 3 + k]
+                found.append(pltpu.make_async_copy(aw.at[:, cut], awp.at[:, to], sem))
+        return found
 
     @pl.when(step == 0)
     def _():
@@ -759,23 +822,36 @@
             *(spread.line(j) for j in range(1, spread.far)),
         ]
         greet(peers)
+        shared_copy().start()
+        for copy in early_copies():
+            copy.start()
         for k in range(steps):
             fi_copy(k).start()
-        spread.send[0] = shared[...]
-        for part in range(pairs):
-            for k in range(3):
-                cut = slice(k * features + part * 128, k * features + (part + 1) * 128)
-                awp[:, parts_of(k, part)] = aw[:, cut]
         cols[...] = as_column(row_of(gain))
         gpl[...] = jnp.zeros_like(gpl)
+        gplt[...] = jnp.zeros_like(gplt)
+        acc[...] = jnp.zeros_like(acc)
         meet(peers)
         for s in range(quarter.streams):
             quarter.start(1, s)
-        spread.start(1, 0)
-
-    for slot, name, phase, s in plan:
-        if slot < last + late_steps:
-            pl.when(step == slot)(functools.partial(engines[name].advance, phase, s))
+        shared_copy().wait()
+        spread.start("core", 0)
+
+    for k in range(steps):
+        pl.when(step == k)(lambda k=k: fi_copy(k).wait())
+
+    @pl.when(step == 1)
+    def _():
+        for copy in early_copies():
+            copy.wait()
+
+    def advance(slot):
+        for at, name, phase, s in plan:
+            if at == slot:
+                engines[name].advance(phase, s)
+
+    for slot in sorted({item[0] for item in plan if item[0] < last + late_steps}):
+        pl.when(step == slot)(functools.partial(advance, slot))
 
     @pl.when(step < last)
     def _():
@@ -785,11 +861,6 @@
         gp = gpa.at[at_group, pl.ds(pl.multiple_of(pair * 384, 128), 384)]
         held = {}
         units = [(g, r) for g in range(group) for r in range(2)]
-
-        @pl.when(at_group == 0)
-        def _():
-            acc[...] = jnp.zeros_like(acc)
-            gplt[...] = jnp.zeros_like(gplt)
 
         def lanes_of(g):
             return slice(g * MAIN, (g + 1) * MAIN)
@@ -887,9 +958,7 @@
             if 0 <= t - 3 < number:
                 store(*units[t - 3])
 
-        for k in range(steps):
-            pl.when(step == k)(lambda k=k: fi_copy(k).wait())
-        acc[...] += dot(fis[at_group], gp[...], NT)
+        acc[...] = jnp.where(at_group == 0, 0.0, acc[...]) + dot(fis[at_group], gp[...], NT)
 
         @pl.when(at_group == steps - 1)
         def _():
@@ -914,7 +983,7 @@
             rest = spread.send.shape[1] - 3 * block
             if rest:
                 spread.send[stream, 3 * block :] = jnp.zeros((rest, 128), bf16)
-            spread.start(1, stream)
+            spread.start("core", stream)
 
     @pl.when(step == last)
     def _():
@@ -971,26 +1040,32 @@
 
 
 def place_kernel(
-    pairs, parts, quarter, spread, bias, output, input_grad,
-    output_to, input_to, first_gain, first_shift, attend, attend_bias, merge, merge_bias,
-    second_gain, second_shift, up, up_bias, down, down_bias, held, sems,
+    pairs, quarter_in, spread_in, bias, output, input_grad,
+    output_to, input_to, first_gain, first_shift, attend_to, attend_bias, merge_to, merge_bias,
+    second_gain, second_shift, up_to, up_bias, down_to, down_bias,
+    held, quarter, spread, attend, merge, up, down, sems, small,
 ):
     features = merge.shape[0]
     count = output.shape[0]
+    got = [
+        pltpu.make_async_copy(quarter_in, quarter, small.at[0]),
+        pltpu.make_async_copy(spread_in, spread, small.at[1]),
+    ]
     ins, outs = [], []
     for k, (src, to) in enumerate(((output, output_to), (input_grad, input_to))):
         for image in range(count):
             ins.append(pltpu.make_async_copy(src.at[image], held.at[k, image], sems.at[0, k, image]))
             outs.append(pltpu.make_async_copy(held.at[k, image], to.at[image], sems.at[1, k, image]))
-    for copy in ins:
+    for copy in got + ins:
         copy.start()
+    for copy in got:
+        copy.wait()
     for s in range(quarter.shape[0]):
         lanes = slice(s * 128, (s + 1) * 128)
         up[:, lanes] = quarter[s, 0].astype(f32)
         down[lanes, :] = quarter[s, 1].astype(f32).T
-    up_bias[...] = bias[0:1, :].reshape(features)
     block = features + 32
-    ends, firsts, seconds, merge_ends = [], [], [], []
+    firsts, seconds, merge_ends = [], [], []
     for k in range(3):
         merge[:, k * 128 : (k + 1) * 128] = spread[0, k * block : k * block + features].astype(f32)
         low = k * block + features
@@ -1002,7 +1077,14 @@
             attend[:, lanes] = spread[pair + 1, k * block : k * block + features].astype(f32)
             total = total + spread[pair + 1, low + 16 : low + 32].astype(f32)
         firsts.append(total)
+    puts = [
+        pltpu.make_async_copy(src, to, small.at[2 + k])
+        for k, (src, to) in enumerate(((attend, attend_to), (merge, merge_to), (up, up_to), (down, down_to)))
+    ]
+    for copy in puts:
+        copy.start()
     merge_ends, firsts, seconds = (jnp.concatenate(v, axis=1) for v in (merge_ends, firsts, seconds))
+    up_bias[...] = bias[0:1, :].reshape(features)
     merge_bias[...] = merge_ends[0:1, :].reshape(features)
     first_gain[...] = firsts[0:1, :].reshape(features)
     first_shift[...] = firsts[1:2, :].reshape(features)
@@ -1018,29 +1100,28 @@
     for copy, on in zip(ins, outs):
         copy.wait()
         on.start()
-    for copy in outs:
+    for copy in outs + puts:
         copy.wait()
 
 
-def transfers(streams, steps, last, late_steps):
+def transfers(quarter, spread, steps, last, late_steps):
     end = last + late_steps
-    plan = [(1, "quarter", 1, s) for s in range(streams)] + [(1, "spread", 1, 0)]
-    plan += [(min(3 + s // 2, last), "quarter", 2, s) for s in range(streams)]
-    plan += [(min(5 + s // 2, last), "quarter", 3, s) for s in range(streams)]
-    plan += [(3, "spread", 2, 0), (5, "spread", 3, 0), (last, "spread", 4, 0), (last + 2, "spread", 5, 0)]
-    plan += [
-        (steps + 1, "spread", 1, 1), (steps + 2, "spread", 2, 1), (last, "spread", 3, 1),
-        (last + 2, "spread", 4, 1), (last + 4, "spread", 5, 1),
-        (2 * steps + 1, "spread", 1, 2), (last, "spread", 2, 2), (last + 5, "spread", 3, 2),
-        (3 * steps + 2, "spread", 1, 3),
-    ]
+    when = {
+        ("quarter", 0): [1, 3, 5, last + 6, end + 0.4],
+        ("quarter", 1): [1, 3, 5, last + 6, end + 0.4],
+        ("quarter", 2): [1, 4, last, end + 0.1, end + 0.45],
+        ("spread", 0): [1, 3, 4, 5, last, last + 2],
+        ("spread", 1): [steps + 1, steps + 2, steps + 3, last + 1, last + 4, last + 6],
+        ("spread", 2): [2 * steps + 1, last + 1, last + 4, end + 0.2, end + 0.35, end + 0.6],
+        ("spread", 3): [last + 1, last + 5, end + 0.3, end + 0.5, end + 0.7],
+    }
+    plan = []
+    for (name, s), times in when.items():
+        phases = 5 if name == "quarter" else len(spread.phases(s))
+        times = times[:2] + [times[2]] * (phases - len(times)) + times[2:]
+        plan += [(time, name, phase + 1, s) for phase, time in enumerate(times)]
     plan.sort(key=lambda item: item[0])
-    plan += [
-        (end, "spread", 2, 3), (end, "quarter", 4, 0), (end, "quarter", 4, 1), (end, "quarter", 4, 2),
-        (end, "spread", 4, 2), (end, "spread", 3, 3), (end, "quarter", 5, 0), (end, "quarter", 5, 1),
-        (end, "spread", 5, 2), (end, "spread", 4, 3), (end, "quarter", 5, 2), (end, "spread", 5, 3),
-    ]
-    return plan
+    return [(int(time), *rest) for time, *rest in plan]
 
 
 def whole(*dims):
@@ -1126,7 +1207,7 @@
     streams = d // 128
     block = d + 32
     chunk = -(-3 * block // (8 * 16)) * 16
-    half_images = lambda *dims: pl.BlockSpec((group, *dims), lambda i: (i % steps,) + (0,) * len(dims))
+    ahead = lambda i: (i // steps) * (i - steps) + (1 - i // steps) * (i + 1 - (i + 1) // steps)
     late_images = lambda *dims: pl.BlockSpec(
         (group, *dims), lambda i: ((i // steps) * (i - steps),) + (0,) * len(dims)
     )
@@ -1136,8 +1217,8 @@
         functools.partial(feed_kernel, n, group, steps),
         grid=(2 * steps,),
         in_specs=[
-            pl.BlockSpec((d, width), lambda i: (0, i % steps)), late_cols(d), late_images(16, MAIN),
-            half_images(MAIN, d), left, LIVE, whole(d), whole(d), whole(d),
+            once(d, width), pl.BlockSpec((d, width), lambda i: (0, ahead(i))), late_cols(d), late_images(16, MAIN),
+            once(group, MAIN, d), pl.BlockSpec((group, MAIN, d), lambda i: (ahead(i), 0, 0)), left, LIVE, whole(d), whole(d), whole(d),
             whole(rows, d), whole(rows, d), once(quarters, 2, d, share), once(quarters, 16, share), once(d, d),
         ],
         out_specs=[
@@ -1154,7 +1235,8 @@
             pltpu.VMEM((quarters, share, d + 128), bf16), pltpu.VMEM((quarters, d, share), bf16),
             pltpu.VMEM((steps, d + 128, width), bf16), pltpu.VMEM((d + 128, width), bf16),
             pltpu.VMEM((2 * share, width), bf16), pltpu.VMEM((2 * share, width), bf16),
-            pltpu.VMEM((steps, d, width), bf16), pltpu.VMEM((3, d, 128), f32), pltpu.VMEM((2, d, 128), f32),
+            pltpu.VMEM((steps, d, width), bf16), pltpu.VMEM((d, width), bf16),
+            pltpu.VMEM((3, d, 128), f32), pltpu.VMEM((2, d, 128), f32),
             pltpu.VMEM((rows, d), f32), pltpu.VMEM((rows, d), f32),
             pltpu.VMEM((rows, d + 16), bf16), pltpu.VMEM((rows, d), bf16),
             pltpu.VMEM((quarters, rows, share), bf16), pltpu.VMEM((quarters, rows, share), bf16),
@@ -1167,7 +1249,7 @@
         compiler_params=params(collective_id=1, has_side_effects=True),
         name="feed",
     )(
-        hid, att, invs, cotangent, cotangent, image_mask, second_gain, second_shift, down_bias, hidl, attl,
+        hid, hid, att, invs, cotangent, cotangent, cotangent, image_mask, second_gain, second_shift, down_bias, hidl, attl,
         wall, ball, merge_weight,
     )
 
@@ -1178,7 +1260,7 @@
     last = pairs * steps
     quarter = Quarter(mesh_sizes[0], streams, 2 * d)
     spread = Spread(mesh_sizes, pairs + 1, chunk)
-    plan = transfers(streams, steps, last, late_steps)
+    plan = transfers(quarter, spread, steps, last, late_steps)
     side = lambda i: (i + late_steps) // (last + late_steps)
     early = lambda i: i - side(i) * (i - (last - 1))
     late = lambda i: side(i) * (i - last)
@@ -1194,8 +1276,7 @@
             pl.BlockSpec((group, 2, MAIN, MAIN), lambda i: (early(i) % steps, early(i) // steps, 0, 0)),
             early_images(16, MAIN), early_images(16, MAIN), early_images(16, 128), by_pair(128),
             early_images(16, MAIN), ANY,
-            whole(rows, d), pair_lanes(384), pair_lanes(128), pair_lanes(128), once(d, packed),
-            once(streams, 2 * d, 128), once(streams, 2 * d, 128), once(8 * chunk, 128),
+            whole(rows, d), pair_lanes(384), pair_lanes(128), pair_lanes(128), ANY, ANY, ANY, ANY,
             late_images(MAIN, d), left, pl.BlockSpec((d, late_group * MAIN), lambda i: (0, late(i))),
             whole(rows, d), whole(d), whole(d),
         ],
@@ -1211,7 +1292,8 @@
             pltpu.VMEM((pairs, rows, 384), f32), pltpu.VMEM((384, 128), f32),
             pltpu.VMEM((d, packed), bf16), pltpu.VMEM((d, 128), f32),
             pltpu.VMEM((rows, d), f32), pltpu.VMEM((rows, d), f32),
-            pltpu.VMEM((steps, d + 16, width), bf16), pltpu.SemaphoreType.DMA((steps,)),
+            pltpu.VMEM((steps, d + 16, width), bf16), pltpu.VMEM((streams, 2 * d, 128), bf16),
+            pltpu.SemaphoreType.DMA((steps + 2 + 3 * pairs,)),
             *quarter.scratch(), *spread.scratch(),
         ],
         compiler_params=params(collective_id=2, has_side_effects=True),
@@ -1222,15 +1304,22 @@
     )
     row = lambda: pl.BlockSpec(memory_space=pltpu.VMEM)
     return pl.pallas_call(
-        functools.partial(place_kernel, pairs, quarters),
-        in_specs=[row(), row(), row(), ANY, ANY],
-        out_specs=[ANY, ANY] + [row()] * 12,
+        functools.partial(place_kernel, pairs),
+        in_specs=[ANY, ANY, row(), ANY, ANY],
+        out_specs=[
+            ANY, ANY, row(), row(), ANY, row(), ANY, row(), row(), row(), ANY, row(), ANY, row(),
+        ],
         out_shape=[
             shape(bf16, n, seq, d), shape(bf16, n, seq, d), shape(f32, d), shape(f32, d),
             shape(f32, d, packed), shape(f32, 2, d), shape(f32, d, d), shape(f32, d), shape(f32, d),
             shape(f32, d), shape(f32, d, share), shape(f32, share), shape(f32, share, d), shape(f32, d),
         ],
-        scratch_shapes=[pltpu.VMEM((2, n, seq, d), bf16), pltpu.SemaphoreType.DMA((2, 2, n))],
+        scratch_shapes=[
+            pltpu.VMEM((2, n, seq, d), bf16), pltpu.VMEM((streams, 2, d, 128), bf16),
+            pltpu.VMEM((pairs + 1, 8 * chunk, 128), bf16), pltpu.VMEM((d, packed), f32), pltpu.VMEM((d, d), f32),
+            pltpu.VMEM((d, share), f32), pltpu.VMEM((share, d), f32),
+            pltpu.SemaphoreType.DMA((2, 2, n)), pltpu.SemaphoreType.DMA((6,)),
+        ],
         compiler_params=pltpu.CompilerParams(vmem_limit_bytes=60 * 2**20),
         name="place",
     )(quarter_sum, spread_sum, bias_sum, output, input_grad)

time: 157 us -> 152 us (0.968)
  Pallas kernels: 156 us -> 151 us
    pallas_call x1, Pallas kernels: 61.8 us -> 58.7 us  [shards(): pl.pallas_call(functools.partial(back_kernel, n, group, steps, late_group...]
    pallas_call x1, Pallas kernels: 54.7 us -> 51.9 us  [shards(): pl.pallas_call(functools.partial(feed_kernel, n, group, steps), grid=(2 *...]
where the time goes in v5:
time: 152 us
  Pallas kernels  151 us (99%)
    pallas_call x1, Pallas kernels, shards(): pl.pallas_call(functools.partial(back_kernel, n, group, steps, late_group...  58.7 us
    pallas_call x1, Pallas kernels, shards(): pl.pallas_call(functools.partial(feed_kernel, n, group, steps), grid=(2 *...  51.9 us
    pallas_call x1, Pallas kernels, shards(): pl.pallas_call(functools.partial(attend_kernel, n, group, steps), grid=(s...  31.2 us
    pallas_call x1, Pallas kernels, shards(): pl.pallas_call(functools.partial(place_kernel, pairs), in_specs=[ANY, ANY...  8.93 us

profile of v5, /device:TPU:0, one launch (start us, length us, event | category | flops | bytes accessed | tf_op | source)
XLA Modules:
  0.0 151.6 jit_solution(3949425319470297232)
XLA Ops:
  0.6 31.2 %attend.1 = (bf16[400,3584]{1,0:T(8,128)(2,1)}, bf16[1152,3584]{1,0:T(8,128)(2,1)}, bf16[14,6,256,256]{3,2,1,0:T(8,128)(2,1)}, f32[14,16,256]{2,1,0:T(8,128)}, f...) custom-call(bf16[14,257,384]{2,1,0:T(8,128)(2,1)} %left.3, ...), custom_call_target="tpu_custom_call" | custom-call | tf_op jit(solution)/shard_map/attend/pallas_call | solution.py:1168
  31.9 51.9 %feed.1 = (bf16[14,257,384]{2,1,0:T(8,128)(2,1)}, f32[384,3584]{1,0:T(8,128)}, bf16[384,3584]{1,0:T(8,128)(2,1)}, f32[14,16,256]{2,1,0:T(8,128)}, f32[16,384]{1,...) custom-call(f32[384,3584]{1,0:T(8,128)} %get-tuple-element.47.hid0.h, ...), custom_call_target="tpu_custom_call" | custom-call | tf_op jit(solution)/shard_map/feed/pallas_call | solution.py:1216
  83.8 58.7 %back.1 = (bf16[14,257,384]{2,1,0:T(8,128)(2,1)}, bf16[3,2,384,128]{3,2,1,0:T(8,128)(2,1)}, bf16[4,1280,128]{2,1,0:T(8,128)(2,1)}, f32[8,384]{1,0:T(8,128)}) custom-call(bf16[1152,3584]{1,0:T(8,128)(2,1)} %get-tuple-element.42.qkv, bf16[14,6,256,256]{3,2,1,0:T(8,128)(2,1)} %get-tuple-element.43.probs, f32[14,16,256]{2,1,0:T(8,128)} %get-tuple-element.44.edge, ...), custom_call_target="tpu_custom_call" | custom-call | tf_op jit(solution)/shard_map/back/pallas_call | solution.py:1271
  142.5 8.9 %place.1 = (bf16[14,257,384]{2,1,0:T(8,128)(2,1)}, bf16[14,257,384]{2,1,0:T(8,128)(2,1)}, f32[384]{0:T(512)}, f32[384]{0:T(512)}, f32[384,1152]{1,0:T(8,128)}, /...) custom-call(bf16[3,2,384,128]{3,2,1,0:T(8,128)(2,1)} %get-tuple-elem, ...), custom_call_target="tpu_custom_call" | custom-call | tf_op jit(solution)/shard_map/place/pallas_call | solution.py:1306

commit v6 on v5

--- a/solution.py
+++ b/solution.py
@@ -518,8 +518,8 @@
                 tokens, fi = held.pop("next")
                 toks[lax.rem(step + 1, 3)] = tokens
                 fia[:features, :] = fi
-            if t in (2, 4, 6):
-                project(later, (t - 2) // 2)
+            if t in (5, 7, 9):
+                project(later, (t - 5) // 2)
             if 0 <= t < count_units:
                 soften(*units[t])
             if 0 <= t - 2 < count_units:
@@ -945,6 +945,14 @@
                 gp[at * 128 + r * HEAD : at * 128 + (r + 1) * HEAD, lanes_of(g)] = value.astype(bf16)
 
         number = len(units)
+        thirds = sorted({0, -(-group // 3), -(-2 * group // 3), group})
+        cuts = list(zip(thirds[:-1], thirds[1:]))
+
+        def add_product(low, high):
+            lanes = slice(low * MAIN, high * MAIN)
+            before = jnp.where(at_group == 0, 0.0, acc[...]) if low == 0 else acc[...]
+            acc[...] = before + dot(fis[at_group, :, lanes], gp[:, lanes], NT)
+
         for t in range(-4, number + 4):
             for g in range(group):
                 if t == 2 * g - 4:
@@ -957,8 +965,11 @@
                 grads(*units[t - 1])
             if 0 <= t - 3 < number:
                 store(*units[t - 3])
-
-        acc[...] = jnp.where(at_group == 0, 0.0, acc[...]) + dot(fis[at_group], gp[...], NT)
+            for low, high in cuts[:-1]:
+                if t - 3 == 2 * high - 1:
+                    add_product(low, high)
+
+        add_product(*cuts[-1])
 
         @pl.when(at_group == steps - 1)
         def _():
@@ -1110,9 +1121,9 @@
         ("quarter", 0): [1, 3, 5, last + 6, end + 0.4],
         ("quarter", 1): [1, 3, 5, last + 6, end + 0.4],
         ("quarter", 2): [1, 4, last, end + 0.1, end + 0.45],
-        ("spread", 0): [1, 3, 4, 5, last, last + 2],
-        ("spread", 1): [steps + 1, steps + 2, steps + 3, last + 1, last + 4, last + 6],
-        ("spread", 2): [2 * steps + 1, last + 1, last + 4, end + 0.2, end + 0.35, end + 0.6],
+        ("spread", 0): [2, 4, last, last + 2, last + 4, end + 0.01],
+        ("spread", 1): [4, last, last + 2, last + 5, end + 0.02, end + 0.15],
+        ("spread", 2): [last, last + 3, end + 0.05, end + 0.31, end + 0.51, end + 0.6],
         ("spread", 3): [last + 1, last + 5, end + 0.3, end + 0.5, end + 0.7],
     }
     plan = []

time: 152 us -> 149 us (0.980)
  Pallas kernels: 151 us -> 148 us
    pallas_call x1, Pallas kernels: 31.2 us -> 29.6 us  [shards(): pl.pallas_call(functools.partial(attend_kernel, n, group, steps), grid=(s...]
    pallas_call x1, Pallas kernels: 58.7 us -> 57.1 us  [shards(): pl.pallas_call(functools.partial(back_kernel, n, group, steps, late_group...]
where the time goes in v6:
time: 149 us; the launch traced here: 148 us
  Pallas kernels  148 us (99%)
    pallas_call x1, Pallas kernels, shards(): pl.pallas_call(functools.partial(back_kernel, n, group, steps, late_group...  57.1 us
    pallas_call x1, Pallas kernels, shards(): pl.pallas_call(functools.partial(feed_kernel, n, group, steps), grid=(2 *...  51.9 us
    pallas_call x1, Pallas kernels, shards(): pl.pallas_call(functools.partial(attend_kernel, n, group, steps), grid=(s...  29.6 us
    pallas_call x1, Pallas kernels, shards(): pl.pallas_call(functools.partial(place_kernel, pairs), in_specs=[ANY, ANY...  8.93 us

profile of v6, /device:TPU:0, one launch (start us, length us, event | category | flops | bytes accessed | tf_op | source)
XLA Modules:
  0.0 148.5 jit_solution(17969393709539831063)
XLA Ops:
  0.6 29.6 %attend.1 = (bf16[400,3584]{1,0:T(8,128)(2,1)}, bf16[1152,3584]{1,0:T(8,128)(2,1)}, bf16[14,6,256,256]{3,2,1,0:T(8,128)(2,1)}, f32[14,16,256]{2,1,0:T(8,128)}, f...) custom-call(bf16[14,257,384]{2,1,0:T(8,128)(2,1)} %left.3, ...), custom_call_target="tpu_custom_call" | custom-call | tf_op jit(solution)/shard_map/attend/pallas_call | solution.py:1179
  30.2 51.9 %feed.1 = (bf16[14,257,384]{2,1,0:T(8,128)(2,1)}, f32[384,3584]{1,0:T(8,128)}, bf16[384,3584]{1,0:T(8,128)(2,1)}, f32[14,16,256]{2,1,0:T(8,128)}, f32[16,384]{1,...) custom-call(f32[384,3584]{1,0:T(8,128)} %get-tuple-element.47.hid0.h, ...), custom_call_target="tpu_custom_call" | custom-call | tf_op jit(solution)/shard_map/feed/pallas_call | solution.py:1227
  82.2 57.1 %back.1 = (bf16[14,257,384]{2,1,0:T(8,128)(2,1)}, bf16[3,2,384,128]{3,2,1,0:T(8,128)(2,1)}, bf16[4,1280,128]{2,1,0:T(8,128)(2,1)}, f32[8,384]{1,0:T(8,128)}) custom-call(bf16[1152,3584]{1,0:T(8,128)(2,1)} %get-tuple-element.42.qkv, bf16[14,6,256,256]{3,2,1,0:T(8,128)(2,1)} %get-tuple-element.43.probs, f32[14,16,256]{2,1,0:T(8,128)} %get-tuple-element.44.edge, ...), custom_call_target="tpu_custom_call" | custom-call | tf_op jit(solution)/shard_map/back/pallas_call | solution.py:1282
  139.3 8.9 %place.1 = (bf16[14,257,384]{2,1,0:T(8,128)(2,1)}, bf16[14,257,384]{2,1,0:T(8,128)(2,1)}, f32[384]{0:T(512)}, f32[384]{0:T(512)}, f32[384,1152]{1,0:T(8,128)}, /...) custom-call(bf16[3,2,384,128]{3,2,1,0:T(8,128)(2,1)} %get-tuple-elem, ...), custom_call_target="tpu_custom_call" | custom-call | tf_op jit(solution)/shard_map/place/pallas_call | solution.py:1317

commit v7 on v6

--- a/solution.py
+++ b/solution.py
@@ -304,7 +304,7 @@
     tok0, tok, left, pmask, live, gain, shift, abias, mbias, aw, mw, up, ubias, down,
     fi_out, qkv_out, probs_out, edge_out, inv_out, lp_out, lself_out, att_out, hid_out,
     fil_out, qkvl_out, attl_out, hidl_out, wall, ball,
-    awt, mwt, fia, atta, cols, edges, qkv2, toks, xl, qkvl, attl, brow, sends, recvs, own,
+    awt, mwt, fia, atta, cols, edges, qkv2, toks, xl, qkvl, attl, brow, sends, recvs, own, leave,
 ):
     step = pl.program_id(0)
     me_dp, me_t = lax.axis_index("dp"), lax.axis_index("tensor")
@@ -404,6 +404,15 @@
         for part in range(3):
             project(0, part)
 
+    def qkv_copy(index):
+        slot = lax.rem(index, 2)
+        lanes = pl.ds(pl.multiple_of(index * width, 128), width)
+        return pltpu.make_async_copy(qkv2.at[slot], qkv_out.at[:, lanes], leave.at[slot])
+
+    @pl.when(step > 0)
+    def _():
+        qkv_copy(step - 1).wait()
+
     def merge_branch():
         return dot(mwt[...], atta[...])
 
@@ -414,6 +423,7 @@
     @pl.when(step < steps)
     def _():
         now, later = lax.rem(step, 2), lax.rem(step + 1, 2)
+        qkv_copy(step).start()
         one_row = rows_where(0, jnp.ones((1, MAIN), f32), 16, bf16)
         held = {}
         units = [(g, h) for g in range(group) for h in range(HEADS)]
@@ -505,12 +515,12 @@
             if t + 2 == 0:
                 for g in range(group):
                     begin(g)
-                held["branch"] = merge_branch()
+                    held["branch"] = merge_branch()
+                att_out[features:, :] = atta[features : features + 16, :]
             if 0 <= t + 2 < count_units:
                 scores(*units[t + 2])
             if t == -1:
                 hid_out[...] = hidden_of(held.pop("branch"), step - 1 + 3 * (1 - jnp.minimum(step, 1)))
-                qkv_out[...] = qkv2[now]
                 fi_out[:features, :] = fia[:features, :]
                 fi_out[features:, :] = fia[features : features + 16, :]
                 held["next"] = first_norm(tok)
@@ -547,7 +557,7 @@
     count, group, steps,
     hid0, hid, att, inv, cot0, cot, cleft, live, gain, shift, dbias, hidl, attl, wall, ball, mw,
     out, gh_out, gml_out, dots_out, ghl_out, gmleft_out, mine, beside, shared,
-    upt, dnt, sia, atta, act, gpre, gb, gattn, cols, gsum, xl, outl, sil, gbl, actl, gprel,
+    upt, dnt, sia, act, gpre, gb, gattn, cols, gsum, xl, outl, sil, gbl, actl, gprel,
     outp, gradp, up_acc, down_acc, merge_acc, sums, biases, kept, away, r1, across, r2, sends, recvs,
 ):
     step = pl.program_id(0)
@@ -579,7 +589,6 @@
         ones = rows_where(0, jnp.ones((1, width), f32), 128, bf16)
         for k in range(steps):
             sia[k, features:, :] = ones
-        atta[features:, :] = ones
         cols[0] = as_column(gain_row)
         cols[1] = as_column(shift_row)
         cols[2] = as_column(dbias_row)
@@ -722,7 +731,7 @@
 
         def scale_rows(g):
             mixed = held["mixed", g].astype(bf16).astype(f32)
-            both = mixed * att[:, lanes_of[g]].astype(f32)
+            both = mixed * att[:features, lanes_of[g]].astype(f32)
             for h in range(HEADS):
                 span = slice(h * HEAD, (h + 1) * HEAD)
                 row_inv = inv[g, h : h + 1, :]
@@ -731,7 +740,6 @@
                 dots_out[g, h : h + 1, :] = row_dot
 
         dots_out[...] = jnp.zeros_like(dots_out)
-        atta[:features, :] = att[...]
         back(0)
         up_product()
         for g in range(1, group):
@@ -741,7 +749,7 @@
         down_product()
         for g in range(group):
             scale_rows(g)
-        merge_acc[...] += dot(atta[: merge_acc.shape[0], :], gattn[...], NT)
+        merge_acc[...] += dot(att[...], gattn[...], NT)
         sums[2:3, :] += dot(jnp.ones((16, width), bf16), gb[at_step], NT)[0:1, :]
         for g in range(group):
             write(g)
@@ -1186,15 +1194,15 @@
             once(d, packed), once(d, d), ANY, whole(share), ANY,
         ],
         out_specs=[
-            cols(d + 16), cols(packed), images(HEADS, MAIN, MAIN), images(16, MAIN),
-            images(16, MAIN), images(16, MAIN), images(16, 128), cols(d),
+            cols(d + 16), ANY, images(HEADS, MAIN, MAIN), images(16, MAIN),
+            images(16, MAIN), images(16, MAIN), images(16, 128), cols(d + 16),
             pl.BlockSpec((d, width), lambda i: (0, jnp.maximum(i, 1) - 1)),
             whole(rows, d), whole(rows, packed), whole(rows, d), whole(rows, d), ANY, ANY,
         ],
         out_shape=[
             shape(bf16, d + 16, total), shape(bf16, packed, total), shape(bf16, n, HEADS, MAIN, MAIN),
             shape(f32, n, 16, MAIN), shape(f32, n, 16, MAIN), shape(f32, n, 16, MAIN),
-            shape(f32, n, 16, 128), shape(bf16, d, total), shape(f32, d, total),
+            shape(f32, n, 16, 128), shape(bf16, d + 16, total), shape(f32, d, total),
             shape(f32, rows, d), shape(f32, rows, packed), shape(f32, rows, d), shape(f32, rows, d),
             shape(bf16, quarters, 2, d, share), shape(bf16, quarters, 16, share),
         ],
@@ -1206,7 +1214,7 @@
             pltpu.VMEM((3, d, width), bf16),
             pltpu.VMEM((rows, d), f32), pltpu.VMEM((rows, packed), f32), pltpu.VMEM((rows, d), f32),
             pltpu.VMEM((16, share), bf16), pltpu.SemaphoreType.DMA((9,)), pltpu.SemaphoreType.DMA((9,)),
-            pltpu.SemaphoreType.DMA((3,)),
+            pltpu.SemaphoreType.DMA((3,)), pltpu.SemaphoreType.DMA((2,)),
         ],
         compiler_params=params(collective_id=0, has_side_effects=True),
         name="attend",
@@ -1228,7 +1236,7 @@
         functools.partial(feed_kernel, n, group, steps),
         grid=(2 * steps,),
         in_specs=[
-            once(d, width), pl.BlockSpec((d, width), lambda i: (0, ahead(i))), late_cols(d), late_images(16, MAIN),
+            once(d, width), pl.BlockSpec((d, width), lambda i: (0, ahead(i))), late_cols(d + 16), late_images(16, MAIN),
             once(group, MAIN, d), pl.BlockSpec((group, MAIN, d), lambda i: (ahead(i), 0, 0)), left, LIVE, whole(d), whole(d), whole(d),
             whole(rows, d), whole(rows, d), once(quarters, 2, d, share), once(quarters, 16, share), once(d, d),
         ],
@@ -1244,7 +1252,7 @@
         ],
         scratch_shapes=[
             pltpu.VMEM((quarters, share, d + 128), bf16), pltpu.VMEM((quarters, d, share), bf16),
-            pltpu.VMEM((steps, d + 128, width), bf16), pltpu.VMEM((d + 128, width), bf16),
+            pltpu.VMEM((steps, d + 128, width), bf16),
             pltpu.VMEM((2 * share, width), bf16), pltpu.VMEM((2 * share, width), bf16),
             pltpu.VMEM((steps, d, width), bf16), pltpu.VMEM((d, width), bf16),
             pltpu.VMEM((3, d, 128), f32), pltpu.VMEM((2, d, 128), f32),

time: 149 us -> 148 us (level)
  no operation moved by 1% of the time
where the time goes in v7:
time: 148 us
  Pallas kernels  147 us (99%)
    pallas_call x1, Pallas kernels, shards(): pl.pallas_call(functools.partial(back_kernel, n, group, steps, late_group...  57.3 us
    pallas_call x1, Pallas kernels, shards(): pl.pallas_call(functools.partial(feed_kernel, n, group, steps), grid=(2 *...  52 us
    pallas_call x1, Pallas kernels, shards(): pl.pallas_call(functools.partial(attend_kernel, n, group, steps), grid=(s...  28.5 us
    pallas_call x1, Pallas kernels, shards(): pl.pallas_call(functools.partial(place_kernel, pairs), in_specs=[ANY, ANY...  8.93 us

profile of v7, /device:TPU:0, one launch (start us, length us, event | category | flops | bytes accessed | tf_op | source)
XLA Modules:
  0.0 147.6 jit_solution(4338137265174827926)
XLA Ops:
  0.6 28.5 %attend.1 = (bf16[400,3584]{1,0:T(8,128)(2,1)}, bf16[1152,3584]{1,0:T(8,128)(2,1)}, bf16[14,6,256,256]{3,2,1,0:T(8,128)(2,1)}, f32[14,16,256]{2,1,0:T(8,128)}, f...) custom-call(bf16[14,257,384]{2,1,0:T(8,128)(2,1)} %left.3, ...), custom_call_target="tpu_custom_call" | custom-call | tf_op jit(solution)/shard_map/attend/pallas_call | solution.py:1187
  29.2 52.0 %feed.1 = (bf16[14,257,384]{2,1,0:T(8,128)(2,1)}, f32[384,3584]{1,0:T(8,128)}, bf16[384,3584]{1,0:T(8,128)(2,1)}, f32[14,16,256]{2,1,0:T(8,128)}, f32[16,384]{1,...) custom-call(f32[384,3584]{1,0:T(8,128)} %get-tuple-element.47.hid0.h, ...), custom_call_target="tpu_custom_call" | custom-call | tf_op jit(solution)/shard_map/feed/pallas_call | solution.py:1235
  81.2 57.3 %back.1 = (bf16[14,257,384]{2,1,0:T(8,128)(2,1)}, bf16[3,2,384,128]{3,2,1,0:T(8,128)(2,1)}, bf16[4,1280,128]{2,1,0:T(8,128)(2,1)}, f32[8,384]{1,0:T(8,128)}) custom-call(bf16[1152,3584]{1,0:T(8,128)(2,1)} %get-tuple-element.42.qkv, bf16[14,6,256,256]{3,2,1,0:T(8,128)(2,1)} %get-tuple-element.43.probs, f32[14,16,256]{2,1,0:T(8,128)} %get-tuple-element.44.edge, ...), custom_call_target="tpu_custom_call" | custom-call | tf_op jit(solution)/shard_map/back/pallas_call | solution.py:1290
  138.5 8.9 %place.1 = (bf16[14,257,384]{2,1,0:T(8,128)(2,1)}, bf16[14,257,384]{2,1,0:T(8,128)(2,1)}, f32[384]{0:T(512)}, f32[384]{0:T(512)}, f32[384,1152]{1,0:T(8,128)}, /...) custom-call(bf16[3,2,384,128]{3,2,1,0:T(8,128)(2,1)} %get-tuple-elem, ...), custom_call_target="tpu_custom_call" | custom-call | tf_op jit(solution)/shard_map/place/pallas_call | solution.py:1325

commit v8 on v7

--- a/solution.py
+++ b/solution.py
@@ -359,7 +359,7 @@
 
     def project(slot, part):
         span = slice(part * features, (part + 1) * features)
-        qkv2[slot, span, :] = dot(awt[span, :], fia[...]).astype(bf16)
+        qkv2[slot, span, :] = dot(awt[span, :], fia[slot]).astype(bf16)
 
     @pl.when(step == 0)
     def _():
@@ -377,8 +377,9 @@
                 awt[to, features:] = rows_where(0, bias, 128, f32).T.astype(bf16)
         mwt[:, :features] = mw[...].astype(f32).T.astype(bf16)
         mwt[:, features:] = rows_where(0, row_of(mbias), 128, f32).T.astype(bf16)
-        ones = rows_where(0, jnp.ones((1, fia.shape[1]), f32), 128, bf16)
-        fia[features:, :] = ones
+        ones = rows_where(0, jnp.ones((1, width), f32), 128, bf16)
+        fia[0, features:, :] = ones
+        fia[1, features:, :] = ones
         atta[features:, :] = ones
         cols[0] = as_column(row_of(gain))
         cols[1] = as_column(row_of(shift))
@@ -400,7 +401,7 @@
         attl[...] = jnp.zeros_like(attl)
         tokens, fi = first_norm(tok0)
         toks[0] = tokens
-        fia[:features, :] = fi
+        fia[0, :features, :] = fi
         for part in range(3):
             project(0, part)
 
@@ -409,9 +410,16 @@
         lanes = pl.ds(pl.multiple_of(index * width, 128), width)
         return pltpu.make_async_copy(qkv2.at[slot], qkv_out.at[:, lanes], leave.at[slot])
 
+    def fi_copy(index):
+        slot = lax.rem(index, 2)
+        lanes = pl.ds(pl.multiple_of(index * width, 128), width)
+        src = fia.at[slot, pl.ds(0, features + 16)]
+        return pltpu.make_async_copy(src, fi_out.at[:, lanes], leave.at[2 + slot])
+
     @pl.when(step > 0)
     def _():
         qkv_copy(step - 1).wait()
+        fi_copy(step - 1).wait()
 
     def merge_branch():
         return dot(mwt[...], atta[...])
@@ -424,6 +432,7 @@
     def _():
         now, later = lax.rem(step, 2), lax.rem(step + 1, 2)
         qkv_copy(step).start()
+        fi_copy(step).start()
         one_row = rows_where(0, jnp.ones((1, MAIN), f32), 16, bf16)
         held = {}
         units = [(g, h) for g in range(group) for h in range(HEADS)]
@@ -521,13 +530,11 @@
                 scores(*units[t + 2])
             if t == -1:
                 hid_out[...] = hidden_of(held.pop("branch"), step - 1 + 3 * (1 - jnp.minimum(step, 1)))
-                fi_out[:features, :] = fia[:features, :]
-                fi_out[features:, :] = fia[features : features + 16, :]
                 held["next"] = first_norm(tok)
             if t == 1:
                 tokens, fi = held.pop("next")
                 toks[lax.rem(step + 1, 3)] = tokens
-                fia[:features, :] = fi
+                fia[later, :features, :] = fi
             if t in (5, 7, 9):
                 project(later, (t - 5) // 2)
             if 0 <= t < count_units:
@@ -1194,7 +1201,7 @@
             once(d, packed), once(d, d), ANY, whole(share), ANY,
         ],
         out_specs=[
-            cols(d + 16), ANY, images(HEADS, MAIN, MAIN), images(16, MAIN),
+            ANY, ANY, images(HEADS, MAIN, MAIN), images(16, MAIN),
             images(16, MAIN), images(16, MAIN), images(16, 128), cols(d + 16),
             pl.BlockSpec((d, width), lambda i: (0, jnp.maximum(i, 1) - 1)),
             whole(rows, d), whole(rows, packed), whole(rows, d), whole(rows, d), ANY, ANY,
@@ -1208,13 +1215,13 @@
         ],
         scratch_shapes=[
             pltpu.VMEM((packed, d + 128), bf16), pltpu.VMEM((d, d + 128), bf16),
-            pltpu.VMEM((d + 128, width), bf16), pltpu.VMEM((d + 128, width), bf16),
+            pltpu.VMEM((2, d + 128, width), bf16), pltpu.VMEM((d + 128, width), bf16),
             pltpu.VMEM((2, d, 128), f32), pltpu.VMEM((group, 16, MAIN), f32),
             pltpu.VMEM((2, packed, width), bf16),
             pltpu.VMEM((3, d, width), bf16),
             pltpu.VMEM((rows, d), f32), pltpu.VMEM((rows, packed), f32), pltpu.VMEM((rows, d), f32),
             pltpu.VMEM((16, share), bf16), pltpu.SemaphoreType.DMA((9,)), pltpu.SemaphoreType.DMA((9,)),
-            pltpu.SemaphoreType.DMA((3,)), pltpu.SemaphoreType.DMA((2,)),
+            pltpu.SemaphoreType.DMA((3,)), pltpu.SemaphoreType.DMA((4,)),
         ],
         compiler_params=params(collective_id=0, has_side_effects=True),
         name="attend",

time: 148 us -> 147 us (level)
  no operation moved by 1% of the time
where the time goes in v8:
time: 147 us
  Pallas kernels  146 us (99%)
    pallas_call x1, Pallas kernels, shards(): pl.pallas_call(functools.partial(back_kernel, n, group, steps, late_group...  57.2 us
    pallas_call x1, Pallas kernels, shards(): pl.pallas_call(functools.partial(feed_kernel, n, group, steps), grid=(2 *...  52 us
    pallas_call x1, Pallas kernels, shards(): pl.pallas_call(functools.partial(attend_kernel, n, group, steps), grid=(s...  28.1 us
    pallas_call x1, Pallas kernels, shards(): pl.pallas_call(functools.partial(place_kernel, pairs), in_specs=[ANY, ANY...  8.93 us

profile of v8, /device:TPU:0, one launch (start us, length us, event | category | flops | bytes accessed | tf_op | source)
XLA Modules:
  0.0 147.2 jit_solution(5650048948926464181)
XLA Ops:
  0.6 28.1 %attend.1 = (bf16[400,3584]{1,0:T(8,128)(2,1)}, bf16[1152,3584]{1,0:T(8,128)(2,1)}, bf16[14,6,256,256]{3,2,1,0:T(8,128)(2,1)}, f32[14,16,256]{2,1,0:T(8,128)}, f...) custom-call(bf16[14,257,384]{2,1,0:T(8,128)(2,1)} %left.3, ...), custom_call_target="tpu_custom_call" | custom-call | tf_op jit(solution)/shard_map/attend/pallas_call | solution.py:1194
  28.8 52.0 %feed.1 = (bf16[14,257,384]{2,1,0:T(8,128)(2,1)}, f32[384,3584]{1,0:T(8,128)}, bf16[384,3584]{1,0:T(8,128)(2,1)}, f32[14,16,256]{2,1,0:T(8,128)}, f32[16,384]{1,...) custom-call(f32[384,3584]{1,0:T(8,128)} %get-tuple-element.47.hid0.h, ...), custom_call_target="tpu_custom_call" | custom-call | tf_op jit(solution)/shard_map/feed/pallas_call | solution.py:1242
  80.8 57.2 %back.1 = (bf16[14,257,384]{2,1,0:T(8,128)(2,1)}, bf16[3,2,384,128]{3,2,1,0:T(8,128)(2,1)}, bf16[4,1280,128]{2,1,0:T(8,128)(2,1)}, f32[8,384]{1,0:T(8,128)}) custom-call(bf16[1152,3584]{1,0:T(8,128)(2,1)} %get-tuple-element.42.qkv, bf16[14,6,256,256]{3,2,1,0:T(8,128)(2,1)} %get-tuple-element.43.probs, f32[14,16,256]{2,1,0:T(8,128)} %get-tuple-element.44.edge, ...), custom_call_target="tpu_custom_call" | custom-call | tf_op jit(solution)/shard_map/back/pallas_call | solution.py:1297
  138.1 8.9 %place.1 = (bf16[14,257,384]{2,1,0:T(8,128)(2,1)}, bf16[14,257,384]{2,1,0:T(8,128)(2,1)}, f32[384]{0:T(512)}, f32[384]{0:T(512)}, f32[384,1152]{1,0:T(8,128)}, /...) custom-call(bf16[3,2,384,128]{3,2,1,0:T(8,128)(2,1)} %get-tuple-elem, ...), custom_call_target="tpu_custom_call" | custom-call | tf_op jit(solution)/shard_map/place/pallas_call | solution.py:1332
